TPU v7x, 32 devices: a whole 2x2x4 slice. The times are simulated.
32 devices in a mesh: layers: 2 (over y), blk: 4 (over z), tok: 4 (over x, core).
Axes of the slice: x: 2, y: 2, z: 4, core: 2. Of those that a mesh axis runs over, the one named last changes fastest.
Arguments:
- inputs: bfloat16 [8192, 1024], P(('layers', 'blk', 'tok')), parts along dimension 0, may hold values from -6 to 6
- targets: bfloat16 [8192, 1024], P(('layers', 'blk', 'tok')), parts along dimension 0, may hold values from -6 to 6
- mask: int32 [8192, 128], P(('layers', 'blk', 'tok')), parts along dimension 0, may hold values from 0 to 1, as said below
- enc_weight: bfloat16 [256, 1024], P(('layers', 'blk')), parts along dimension 0, may hold values from -0.1875 to 0.1875
- enc_bias: bfloat16 [256], P(('layers', 'blk')), parts along dimension 0, may hold values from -3 to 3
- dec_weight: bfloat16 [256, 1024], P(('layers', 'blk')), parts along dimension 0, may hold values from -0.5 to 0.5
- dec_bias: float32 [2048], P('layers'), parts along dimension 0, may hold values from -3 to 3
Outputs:
- recon: bfloat16 [8192, 1024], P(('layers', 'blk', 'tok')), parts along dimension 0
- grad_enc: float32 [256, 1024], P(('layers', 'blk'), 'tok'), parts along dimension 0
- grad_dec: float32 [256, 1024], P(('layers', 'blk'), 'tok'), parts along dimension 0
There are 2 independent parts, one for each index of `layers`. A program takes and returns all parts, laid end to end along the dimension named above; each array names one. Nothing has to cross between parts.
Inputs may be any that keep to these rules, and one draw needn't show every extreme that they name: `mask`: each block of 256 tokens (one device's) by 32 latents is either all zero or holds independent 0 and 1 entries; how many blocks are live differs between devices.
All inputs are finite; a program needn't handle non-finite values.
Results may differ from a plain program's by a relative error of at most 0.0095.
Values may be sent and summed in bfloat16 or wider, within the bound.
No kernel may reach another device: no remote copies, remote signals or barrier semaphores. Data moves between devices by JAX's collectives and lax.ppermute only.
A program may use at most 64 MiB of HBM per device.

v0:
```python
import math

import jax
import jax.numpy as jnp
from jax import lax
from jax.sharding import PartitionSpec as P


def passed_along(array, axis, by):
    peers = lax.axis_size(axis)
    return lax.ppermute(array, axis, [(i, (i + by) % peers) for i in range(peers)])


def body(inputs, targets, mask, enc_weight, enc_bias, dec_weight, dec_bias):
    count = lax.axis_size("blk")
    rank = lax.axis_index("blk")
    block = enc_weight.shape[0]
    width = enc_weight.shape[1]
    latents = block * count
    tok_rows = inputs.shape[0]
    gate = mask.astype(jnp.float32)
    store = (
        jnp.zeros((tok_rows, latents), jnp.float32),
        jnp.zeros((latents, width), jnp.bfloat16),
        jnp.zeros((latents,), jnp.bfloat16),
        jnp.zeros((latents, width), jnp.bfloat16),
    )

    def place(store, moving, start):
        act_all, enc_all, bias_all, dec_all = store
        enc_part, bias_part, dec_part = moving
        pre = lax.dot_general(
            inputs, enc_part, (((1,), (1,)), ((), ())), preferred_element_type=jnp.float32
        )
        pre = pre + bias_part.astype(jnp.float32)[None, :]
        cols = lax.dynamic_slice_in_dim(gate, start, enc_part.shape[0], 1)
        act_all = lax.dynamic_update_slice_in_dim(act_all, pre * cols, start, 1)
        dec_all = lax.dynamic_update_slice_in_dim(dec_all, dec_part, start, 0)
        return (act_all, enc_all, bias_all, dec_all)

    def forward_step(step, carry):
        held, moving = carry
        held = place(held, moving, (rank - step) % count * block)
        moving = passed_along((moving[0], moving[1], moving[2]), "blk", 1)
        return (held, moving)

    store, moving = lax.fori_loop(
        0, count - 1, forward_step, (store, (enc_weight, enc_bias, dec_weight))
    )
    store = place(store, moving, (rank - (count - 1)) % count * block)
    act_all, enc_all, bias_all, dec_all = store
    act_half = act_all.astype(jnp.bfloat16)
    recon_full = jnp.dot(act_half, dec_all, preferred_element_type=jnp.float32) + dec_bias[None, :]
    recon = recon_full.astype(jnp.bfloat16)
    error = (recon_full - targets.astype(jnp.float32)).astype(jnp.bfloat16)
    back = lax.dot_general(
        error, dec_all, (((1,), (1,)), ((), ())), preferred_element_type=jnp.float32
    )
    dpre = (back * gate).astype(jnp.bfloat16)
    enc_terms = lax.dot_general(
        dpre, inputs, (((0,), (0,)), ((), ())), preferred_element_type=jnp.float32
    )
    dec_terms = lax.dot_general(
        act_half, error, (((0,), (0,)), ((), ())), preferred_element_type=jnp.float32
    )

    def add_terms(accum, start, rows):
        return (
            accum[0] + lax.dynamic_slice_in_dim(enc_terms, start, rows, 0),
            accum[1] + lax.dynamic_slice_in_dim(dec_terms, start, rows, 0),
        )

    def backward_step(step, accum):
        accum = add_terms(accum, (rank - 1 - step) % count * block, block)
        return (
            passed_along(accum[0].astype(jnp.bfloat16), "blk", 1).astype(jnp.float32),
            passed_along(accum[1].astype(jnp.bfloat16), "blk", 1).astype(jnp.float32),
        )

    zeros_full = jnp.zeros((block, width), jnp.float32)
    accum = lax.fori_loop(0, count - 1, backward_step, (zeros_full, zeros_full))
    accum = add_terms(accum, (rank - count) % count * block, block)
    enc_accum, dec_accum = accum
    total = tok_rows * count * lax.axis_size("tok")
    factor = 1.0 / math.sqrt(total)
    grad_enc, grad_dec = (
        lax.psum_scatter(
            enc_accum.astype(jnp.bfloat16), "tok", scatter_dimension=1, tiled=True
        ).astype(jnp.float32),
        lax.psum_scatter(
            dec_accum.astype(jnp.bfloat16), "tok", scatter_dimension=1, tiled=True
        ).astype(jnp.float32),
    )
    return (recon, grad_enc * factor, grad_dec * factor)


def solution(mesh):
    placed = (
        P(("layers", "blk", "tok"), None),
        P(("layers", "blk", "tok"), None),
        P(("layers", "blk", "tok"), None),
        P(("layers", "blk"), None),
        P(("layers", "blk")),
        P(("layers", "blk"), None),
        P("layers"),
    )
    return jax.shard_map(
        body,
        mesh=mesh,
        in_specs=placed,
        out_specs=(
            P(("layers", "blk", "tok"), None),
            P(("layers", "blk"), "tok"),
            P(("layers", "blk"), "tok"),
        ),
        check_vma=False,
    )
```

profile of v0, /device:TPU:0, one launch (start us, length us, event | category | flops | bytes accessed | tf_op | source)
XLA Modules:
  0.0 109.8 jit_solution(3161171403756978696)
XLA Ops:
  7.2 0.0 reduce-scatter.5.cloned.1.call-start
  7.2 0.0 copy-start.4
  7.2 0.0 copy-start
  7.3 0.8 copy-done.4
  8.1 0.1 copy.10
  8.3 0.0 copy-start.1
  8.3 0.0 copy-start.2
  8.3 0.0 copy-start.6
  8.3 0.0 copy-done
  8.3 0.8 copy-done.1
  9.1 0.0 copy-done.2
  9.1 0.0 copy-done.6
  9.1 26.0 %while.41 = (s32[]{:T(128)}, bf16[256,128]{0,1:T(8,128)(2,1)S(1)}, bf16[128,1024]{1,0:T(8,128)(2,1)S(1)}, bf16[32,1024]{1,0:T(8,128)(2,1)S(1)}, bf16[32]{0:T(256...) while((s32[]{:T(128)}, bf16[256,128]{0,1:T(8,128)(2,1)S(1)}, ...), condition=%wide.region_1.2_spmd, body=%wide.region_0.1_spmd.sunk | while | flops 16793648 | bytes 1574388 | solution.py:47
  9.1 3.1 %collective-permute-start.1 = (bf16[32]{0:T(256)(128)(2,1)S(1)}, bf16[32]{0:T(256)(128)(2,1)S(1)}, u32[]{:S(2)}, u32[]{:S(2)}) collective-permute-start(bf16[32]{0:T(256)(128)(2,1)S(1)} %copy.23), channel_id=1, source_target_pairs={{0,4},{4,8},{8,12},{12,0},{1,5},{5,9},{9,13},{13,1},{2,6},{6,10},{... | collective-permute-start | bytes 200 | tf_op jit(solution)/shard_map/while/body/eval_jaxpr/ppermute | solution.py:11
  12.2 1.6 %collective-permute-start = (bf16[32,1024]{1,0:T(8,128)(2,1)S(1)}, bf16[32,1024]{1,0:T(8,128)(2,1)S(1)}, u32[]{:S(2)}, u32[]{:S(2)}) collective-permute-start(bf16[32,1024]{1,0:T(8,128)(2,1)S(1)} %copy.22), channel_id=1, source_target_pairs={{0,4},{4,8},{8,12},{12,0},{1,5},{5,9},{9,13},{13,1},{2,6},{6,10},{... | collective-permute-start | bytes 196616 | tf_op jit(solution)/shard_map/while/body/eval_jaxpr/ppermute | solution.py:11
  13.8 1.6 %collective-permute-start.2 = (bf16[32,1024]{1,0:T(8,128)(2,1)S(1)}, bf16[32,1024]{1,0:T(8,128)(2,1)S(1)}, u32[]{:S(2)}, u32[]{:S(2)}) collective-permute-start(bf16[32,1024]{1,0:T(8,128)(2,1)S(1)} %copy.24), channel_id=1, source_target_pairs={{0,4},{4,8},{8,12},{12,0},{1,5},{5,9},{9,13},{13,1},{2,6},{6,10},{... | collective-permute-start | bytes 196616 | tf_op jit(solution)/shard_map/while/body/eval_jaxpr/ppermute | solution.py:11
  15.4 0.3 fusion.30
  15.7 0.1 collective-permute-done.1
  15.7 3.1 %collective-permute-done = bf16[32,1024]{1,0:T(8,128)(2,1)S(1)} collective-permute-done((bf16[32,1024]{1,0:T(8,128)(2,1)S(1)}, bf16[32,1024]{1,0:T(8,128)(2,1)S(1)}, u32[]{:S(2)}, u32[]{:S(2)}) %collective-permute-start) | collective-permute-done | bytes 65568 | tf_op jit(solution)/shard_map/while/body/eval_jaxpr/ppermute | solution.py:11
  18.9 1.0 collective-permute-done.2
  19.9 0.0 collective-permute-start.1
  19.9 0.5 collective-permute-start
  20.3 1.1 %collective-permute-start.2 = (bf16[32,1024]{1,0:T(8,128)(2,1)S(1)}, bf16[32,1024]{1,0:T(8,128)(2,1)S(1)}, u32[]{:S(2)}, u32[]{:S(2)}) collective-permute-start(bf16[32,1024]{1,0:T(8,128)(2,1)S(1)} %copy.24), channel_id=1, source_target_pairs={{0,4},{4,8},{8,12},{12,0},{1,5},{5,9},{9,13},{13,1},{2,6},{6,10},{... | collective-permute-start | bytes 196616 | tf_op jit(solution)/shard_map/while/body/eval_jaxpr/ppermute | solution.py:11
  21.4 0.3 fusion.30
  21.7 3.5 %collective-permute-done.1 = bf16[32]{0:T(256)(128)(2,1)S(1)} collective-permute-done((bf16[32]{0:T(256)(128)(2,1)S(1)}, bf16[32]{0:T(256)(128)(2,1)S(1)}, u32[]{:S(2)}, u32[]{:S(2)}) %collective-permute-start.1) | collective-permute-done | bytes 96 | tf_op jit(solution)/shard_map/while/body/eval_jaxpr/ppermute | solution.py:11
  25.2 0.8 collective-permute-done
  26.0 0.7 collective-permute-done.2
  26.7 0.0 collective-permute-start.1
  26.7 2.4 %collective-permute-start = (bf16[32,1024]{1,0:T(8,128)(2,1)S(1)}, bf16[32,1024]{1,0:T(8,128)(2,1)S(1)}, u32[]{:S(2)}, u32[]{:S(2)}) collective-permute-start(bf16[32,1024]{1,0:T(8,128)(2,1)S(1)} %copy.22), channel_id=1, source_target_pairs={{0,4},{4,8},{8,12},{12,0},{1,5},{5,9},{9,13},{13,1},{2,6},{6,10},{... | collective-permute-start | bytes 196616 | tf_op jit(solution)/shard_map/while/body/eval_jaxpr/ppermute | solution.py:11
  29.1 0.7 collective-permute-start.2
  29.8 0.3 fusion.30
  30.1 1.9 %collective-permute-done.1 = bf16[32]{0:T(256)(128)(2,1)S(1)} collective-permute-done((bf16[32]{0:T(256)(128)(2,1)S(1)}, bf16[32]{0:T(256)(128)(2,1)S(1)}, u32[]{:S(2)}, u32[]{:S(2)}) %collective-permute-start.1) | collective-permute-done | bytes 96 | tf_op jit(solution)/shard_map/while/body/eval_jaxpr/ppermute | solution.py:11
  32.0 0.8 collective-permute-done
  32.8 2.4 %collective-permute-done.2 = bf16[32,1024]{1,0:T(8,128)(2,1)S(1)} collective-permute-done((bf16[32,1024]{1,0:T(8,128)(2,1)S(1)}, bf16[32,1024]{1,0:T(8,128)(2,1)S(1)}, u32[]{:S(2)}, u32[]{:S(2)}) %collective-permute-start.2) | collective-permute-done | bytes 65568 | tf_op jit(solution)/shard_map/while/body/eval_jaxpr/ppermute | solution.py:11
  35.2 0.0 copy-start.5
  35.2 0.3 fusion.8
  35.5 0.4 copy-done.5
  35.9 0.0 copy-start.3
  35.9 1.1 %fusion.13 = (bf16[256,1024]{1,0:T(8,128)(2,1)}, f32[256,1024]{1,0:T(8,128)S(1)}) fusion(f32[1024]{0:T(1024)S(1)} %copy-done.5, bf16[256,128]{0,1:T(8,128)(2,1)S(1)} %fusion.8, bf16[128,1024]{1,0:T(8,128)(2,1)S(1)} %constant_dynamic-update-slice_fusion.1), kind=kOutput, calls=%fused_computation.26 | convolution fusion | flops 67633152 | bytes 1904640 | tf_op jit(solution)/shard_map/dot_general | solution.py:53
  37.0 0.0 copy-done.3
  37.0 0.6 fusion.5
  37.6 0.3 fusion.9
  37.9 22.4 %while.42 = (s32[]{:T(128)}, f32[32,1024]{1,0:T(8,128)S(1)}, f32[32,1024]{1,0:T(8,128)S(1)}, s32[]{:T(128)}, f32[128,1024]{1,0:T(8,128)S(1)}, /*index=5*/f32[128...) while((s32[]{:T(128)}, f32[32,1024]{1,0:T(8,128)S(1)}, ...), condition=%wide.region_3.4_spmd.clone, body=%wide.region_2.3_spmd.clone.sunk | while | flops 262163 | bytes 1573247 | solution.py:81
  37.9 0.1 collective-permute-start.3
  38.0 0.8 collective-permute-start.4
  38.8 5.7 %collective-permute-done.3 = bf16[32,1024]{1,0:T(8,128)(2,1)S(1)} collective-permute-done((bf16[32,1024]{1,0:T(8,128)(2,1)S(1)}, bf16[32,1024]{1,0:T(8,128)(2,1)S(1)}, u32[]{:S(2)}, u32[]{:S(2)}) %collective-permute-start.3) | collective-permute-done | bytes 65568 | tf_op jit(solution)/shard_map/while/body/eval_jaxpr/ppermute | solution.py:11
  44.5 1.4 %collective-permute-done.4 = bf16[32,1024]{1,0:T(8,128)(2,1)S(1)} collective-permute-done((bf16[32,1024]{1,0:T(8,128)(2,1)S(1)}, bf16[32,1024]{1,0:T(8,128)(2,1)S(1)}, u32[]{:S(2)}, u32[]{:S(2)}) %collective-permute-start.4) | collective-permute-done | bytes 65568 | tf_op jit(solution)/shard_map/while/body/eval_jaxpr/ppermute | solution.py:11
  46.0 0.1 collective-permute-start.3
  46.1 0.1 collective-permute-start.4
  46.1 6.5 %collective-permute-done.3 = bf16[32,1024]{1,0:T(8,128)(2,1)S(1)} collective-permute-done((bf16[32,1024]{1,0:T(8,128)(2,1)S(1)}, bf16[32,1024]{1,0:T(8,128)(2,1)S(1)}, u32[]{:S(2)}, u32[]{:S(2)}) %collective-permute-start.3) | collective-permute-done | bytes 65568 | tf_op jit(solution)/shard_map/while/body/eval_jaxpr/ppermute | solution.py:11
  52.6 0.7 collective-permute-done.4
  53.4 0.1 collective-permute-start.3
  53.5 0.1 collective-permute-start.4
  53.6 6.0 %collective-permute-done.3 = bf16[32,1024]{1,0:T(8,128)(2,1)S(1)} collective-permute-done((bf16[32,1024]{1,0:T(8,128)(2,1)S(1)}, bf16[32,1024]{1,0:T(8,128)(2,1)S(1)}, u32[]{:S(2)}, u32[]{:S(2)}) %collective-permute-start.3) | collective-permute-done | bytes 65568 | tf_op jit(solution)/shard_map/while/body/eval_jaxpr/ppermute | solution.py:11
  59.5 0.7 collective-permute-done.4
  60.3 0.6 add_convert_fusion
  60.9 0.0 reduce-scatter.5.cloned.1.call-update
  60.9 0.0 reduce-scatter.3.cloned.1.call-start
  61.0 0.6 add_convert_fusion.1
  61.6 0.1 reduce-scatter.3.cloned.1.call-update
  61.7 17.9 %reduce-scatter.5.cloned.1.call-done = bf16[32,256]{1,0:T(8,128)(2,1)} async-done(((bf16[32,1024]{1,0:T(8,128)(2,1)}), bf16[32,256]{1,0:T(8,128)(2,1)}) %reduce-scatter.5.cloned.1.call-update) | async-done | bytes 16400 | tf_op jit(solution)/shard_map/reduce_scatter | solution.py:90
  79.5 1.3 %convert_multiply_fusion = f32[32,256]{1,0:T(8,128)} fusion(bf16[32,256]{1,0:T(8,128)(2,1)} %reduce-scatter.5.cloned.1.call-done), kind=kLoop, calls=%fused_computation.19 | loop fusion | flops 16384 | bytes 49152 | tf_op jit(solution)/shard_map/mul | solution.py:94
  80.9 20.7 %reduce-scatter.3.cloned.1.call-done = bf16[32,256]{1,0:T(8,128)(2,1)} async-done(((bf16[32,1024]{1,0:T(8,128)(2,1)}), bf16[32,256]{1,0:T(8,128)(2,1)}) %reduce-scatter.3.cloned.1.call-update) | async-done | bytes 16400 | tf_op jit(solution)/shard_map/reduce_scatter | solution.py:87
  101.6 1.3 %convert_multiply_fusion.1 = f32[32,256]{1,0:T(8,128)} fusion(bf16[32,256]{1,0:T(8,128)(2,1)} %reduce-scatter.3.cloned.1.call-done), kind=kLoop, calls=%fused_computation.20 | loop fusion | flops 16384 | bytes 49152 | tf_op jit(solution)/shard_map/mul | solution.py:94
  (34 shorter events, 0.3 us)
Async XLA Ops:
  7.2 72.4 %reduce-scatter.5.cloned.1.call-start = ((), (), s32[]{:S(2)}) async-start(), calls=%async_computation.3 | async-start | bytes 81920 | tf_op jit(solution)/shard_map/reduce_scatter | solution.py:90
  7.2 0.9 copy-start.4
  7.2 1.1 %copy-start = (bf16[256,1024]{1,0:T(8,128)(2,1)S(1)}, bf16[256,1024]{1,0:T(8,128)(2,1)}, u32[]{:S(2)}) copy-start(bf16[256,1024]{1,0:T(8,128)(2,1)} %param.11) | copy-start | bytes 1572868
  8.3 0.9 copy-start.1
  8.3 0.9 copy-start.2
  8.3 0.9 copy-start.6
  9.1 6.6 %collective-permute-start.1 = (bf16[32]{0:T(256)(128)(2,1)S(1)}, bf16[32]{0:T(256)(128)(2,1)S(1)}, u32[]{:S(2)}, u32[]{:S(2)}) collective-permute-start(bf16[32]{0:T(256)(128)(2,1)S(1)} %copy.23), channel_id=1, source_target_pairs={{0,4},{4,8},{8,12},{12,0},{1,5},{5,9},{9,13},{13,1},{2,6},{6,10},{... | collective-permute-start | bytes 200 | tf_op jit(solution)/shard_map/while/body/eval_jaxpr/ppermute | solution.py:11
  12.2 6.7 %collective-permute-start = (bf16[32,1024]{1,0:T(8,128)(2,1)S(1)}, bf16[32,1024]{1,0:T(8,128)(2,1)S(1)}, u32[]{:S(2)}, u32[]{:S(2)}) collective-permute-start(bf16[32,1024]{1,0:T(8,128)(2,1)S(1)} %copy.22), channel_id=1, source_target_pairs={{0,4},{4,8},{8,12},{12,0},{1,5},{5,9},{9,13},{13,1},{2,6},{6,10},{... | collective-permute-start | bytes 196616 | tf_op jit(solution)/shard_map/while/body/eval_jaxpr/ppermute | solution.py:11
  13.8 6.1 %collective-permute-start.2 = (bf16[32,1024]{1,0:T(8,128)(2,1)S(1)}, bf16[32,1024]{1,0:T(8,128)(2,1)S(1)}, u32[]{:S(2)}, u32[]{:S(2)}) collective-permute-start(bf16[32,1024]{1,0:T(8,128)(2,1)S(1)} %copy.24), channel_id=1, source_target_pairs={{0,4},{4,8},{8,12},{12,0},{1,5},{5,9},{9,13},{13,1},{2,6},{6,10},{... | collective-permute-start | bytes 196616 | tf_op jit(solution)/shard_map/while/body/eval_jaxpr/ppermute | solution.py:11
  19.9 5.3 %collective-permute-start.1 = (bf16[32]{0:T(256)(128)(2,1)S(1)}, bf16[32]{0:T(256)(128)(2,1)S(1)}, u32[]{:S(2)}, u32[]{:S(2)}) collective-permute-start(bf16[32]{0:T(256)(128)(2,1)S(1)} %copy.23), channel_id=1, source_target_pairs={{0,4},{4,8},{8,12},{12,0},{1,5},{5,9},{9,13},{13,1},{2,6},{6,10},{... | collective-permute-start | bytes 200 | tf_op jit(solution)/shard_map/while/body/eval_jaxpr/ppermute | solution.py:11
  19.9 6.1 %collective-permute-start = (bf16[32,1024]{1,0:T(8,128)(2,1)S(1)}, bf16[32,1024]{1,0:T(8,128)(2,1)S(1)}, u32[]{:S(2)}, u32[]{:S(2)}) collective-permute-start(bf16[32,1024]{1,0:T(8,128)(2,1)S(1)} %copy.22), channel_id=1, source_target_pairs={{0,4},{4,8},{8,12},{12,0},{1,5},{5,9},{9,13},{13,1},{2,6},{6,10},{... | collective-permute-start | bytes 196616 | tf_op jit(solution)/shard_map/while/body/eval_jaxpr/ppermute | solution.py:11
  20.3 6.3 %collective-permute-start.2 = (bf16[32,1024]{1,0:T(8,128)(2,1)S(1)}, bf16[32,1024]{1,0:T(8,128)(2,1)S(1)}, u32[]{:S(2)}, u32[]{:S(2)}) collective-permute-start(bf16[32,1024]{1,0:T(8,128)(2,1)S(1)} %copy.24), channel_id=1, source_target_pairs={{0,4},{4,8},{8,12},{12,0},{1,5},{5,9},{9,13},{13,1},{2,6},{6,10},{... | collective-permute-start | bytes 196616 | tf_op jit(solution)/shard_map/while/body/eval_jaxpr/ppermute | solution.py:11
  26.7 5.3 %collective-permute-start.1 = (bf16[32]{0:T(256)(128)(2,1)S(1)}, bf16[32]{0:T(256)(128)(2,1)S(1)}, u32[]{:S(2)}, u32[]{:S(2)}) collective-permute-start(bf16[32]{0:T(256)(128)(2,1)S(1)} %copy.23), channel_id=1, source_target_pairs={{0,4},{4,8},{8,12},{12,0},{1,5},{5,9},{9,13},{13,1},{2,6},{6,10},{... | collective-permute-start | bytes 200 | tf_op jit(solution)/shard_map/while/body/eval_jaxpr/ppermute | solution.py:11
  26.7 6.1 %collective-permute-start = (bf16[32,1024]{1,0:T(8,128)(2,1)S(1)}, bf16[32,1024]{1,0:T(8,128)(2,1)S(1)}, u32[]{:S(2)}, u32[]{:S(2)}) collective-permute-start(bf16[32,1024]{1,0:T(8,128)(2,1)S(1)} %copy.22), channel_id=1, source_target_pairs={{0,4},{4,8},{8,12},{12,0},{1,5},{5,9},{9,13},{13,1},{2,6},{6,10},{... | collective-permute-start | bytes 196616 | tf_op jit(solution)/shard_map/while/body/eval_jaxpr/ppermute | solution.py:11
  29.1 6.1 %collective-permute-start.2 = (bf16[32,1024]{1,0:T(8,128)(2,1)S(1)}, bf16[32,1024]{1,0:T(8,128)(2,1)S(1)}, u32[]{:S(2)}, u32[]{:S(2)}) collective-permute-start(bf16[32,1024]{1,0:T(8,128)(2,1)S(1)} %copy.24), channel_id=1, source_target_pairs={{0,4},{4,8},{8,12},{12,0},{1,5},{5,9},{9,13},{13,1},{2,6},{6,10},{... | collective-permute-start | bytes 196616 | tf_op jit(solution)/shard_map/while/body/eval_jaxpr/ppermute | solution.py:11
  35.2 0.7 copy-start.5
  35.9 1.1 %copy-start.3 = (bf16[256,1024]{1,0:T(8,128)(2,1)S(1)}, bf16[256,1024]{1,0:T(8,128)(2,1)}, u32[]{:S(2)}) copy-start(bf16[256,1024]{1,0:T(8,128)(2,1)} %param.12) | copy-start | bytes 1572868
  37.9 6.5 %collective-permute-start.3 = (bf16[32,1024]{1,0:T(8,128)(2,1)S(1)}, bf16[32,1024]{1,0:T(8,128)(2,1)S(1)}, u32[]{:S(2)}, u32[]{:S(2)}) collective-permute-start(bf16[32,1024]{1,0:T(8,128)(2,1)S(1)} %fusion.31), channel_id=1, source_target_pairs={{0,4},{4,8},{8,12},{12,0},{1,5},{5,9},{9,13},{13,1},{2,6},{6,10},{... | collective-permute-start | bytes 196616 | tf_op jit(solution)/shard_map/while/body/eval_jaxpr/ppermute | solution.py:11
  38.0 7.9 %collective-permute-start.4 = (bf16[32,1024]{1,0:T(8,128)(2,1)S(1)}, bf16[32,1024]{1,0:T(8,128)(2,1)S(1)}, u32[]{:S(2)}, u32[]{:S(2)}) collective-permute-start(bf16[32,1024]{1,0:T(8,128)(2,1)S(1)} %fusion.32), channel_id=1, source_target_pairs={{0,4},{4,8},{8,12},{12,0},{1,5},{5,9},{9,13},{13,1},{2,6},{6,10},{... | collective-permute-start | bytes 196616 | tf_op jit(solution)/shard_map/while/body/eval_jaxpr/ppermute | solution.py:11
  46.0 6.7 %collective-permute-start.3 = (bf16[32,1024]{1,0:T(8,128)(2,1)S(1)}, bf16[32,1024]{1,0:T(8,128)(2,1)S(1)}, u32[]{:S(2)}, u32[]{:S(2)}) collective-permute-start(bf16[32,1024]{1,0:T(8,128)(2,1)S(1)} %fusion.31), channel_id=1, source_target_pairs={{0,4},{4,8},{8,12},{12,0},{1,5},{5,9},{9,13},{13,1},{2,6},{6,10},{... | collective-permute-start | bytes 196616 | tf_op jit(solution)/shard_map/while/body/eval_jaxpr/ppermute | solution.py:11
  46.1 7.3 %collective-permute-start.4 = (bf16[32,1024]{1,0:T(8,128)(2,1)S(1)}, bf16[32,1024]{1,0:T(8,128)(2,1)S(1)}, u32[]{:S(2)}, u32[]{:S(2)}) collective-permute-start(bf16[32,1024]{1,0:T(8,128)(2,1)S(1)} %fusion.32), channel_id=1, source_target_pairs={{0,4},{4,8},{8,12},{12,0},{1,5},{5,9},{9,13},{13,1},{2,6},{6,10},{... | collective-permute-start | bytes 196616 | tf_op jit(solution)/shard_map/while/body/eval_jaxpr/ppermute | solution.py:11
  53.4 6.1 %collective-permute-start.3 = (bf16[32,1024]{1,0:T(8,128)(2,1)S(1)}, bf16[32,1024]{1,0:T(8,128)(2,1)S(1)}, u32[]{:S(2)}, u32[]{:S(2)}) collective-permute-start(bf16[32,1024]{1,0:T(8,128)(2,1)S(1)} %fusion.31), channel_id=1, source_target_pairs={{0,4},{4,8},{8,12},{12,0},{1,5},{5,9},{9,13},{13,1},{2,6},{6,10},{... | collective-permute-start | bytes 196616 | tf_op jit(solution)/shard_map/while/body/eval_jaxpr/ppermute | solution.py:11
  53.5 6.7 %collective-permute-start.4 = (bf16[32,1024]{1,0:T(8,128)(2,1)S(1)}, bf16[32,1024]{1,0:T(8,128)(2,1)S(1)}, u32[]{:S(2)}, u32[]{:S(2)}) collective-permute-start(bf16[32,1024]{1,0:T(8,128)(2,1)S(1)} %fusion.32), channel_id=1, source_target_pairs={{0,4},{4,8},{8,12},{12,0},{1,5},{5,9},{9,13},{13,1},{2,6},{6,10},{... | collective-permute-start | bytes 196616 | tf_op jit(solution)/shard_map/while/body/eval_jaxpr/ppermute | solution.py:11
  60.9 40.7 %reduce-scatter.3.cloned.1.call-start = ((), (), s32[]{:S(2)}) async-start(), calls=%async_computation.2 | async-start | bytes 81920 | tf_op jit(solution)/shard_map/reduce_scatter | solution.py:87
Sparse Core Ops, SparseCore 0:
  61.1 18.4 reduce-scatter.4
  82.1 19.4 reduce-scatter.2
where the time goes:
time: 110 us
  waiting for transfers between devices  73.7 us (67%)
  between operations  14.2 us (13%)
  starting transfers between devices  12 us (11%)
  other arithmetic  4.17 us (4%)
  matrix products  3.03 us (3%)
  local copies, waits for them, and re-layouts  2.28 us (2%)
    ppermute x15, waiting for transfers between devices, passed_along(): lax.ppermute(array, axis, [(i, (i + by) % peers) for i in range(peers)])  35.1 us
    reduce_scatter x1, waiting for transfers between devices, body(): lax.psum_scatter(enc_accum.astype(jnp.bfloat16), 'tok', scatter_dimension...  20.7 us
    reduce_scatter x1, waiting for transfers between devices, body(): lax.psum_scatter(dec_accum.astype(jnp.bfloat16), 'tok', scatter_dimension...  17.9 us
    ppermute x15, starting transfers between devices, passed_along(): lax.ppermute(array, axis, [(i, (i + by) % peers) for i in range(peers)])  12 us
    mul x2, other arithmetic, body(): return (recon, grad_enc * factor, grad_dec * factor)  2.67 us
  transfers between devices with their start and end apart: 17, of which 17 were waited for; matrix products, arithmetic and copies ran while one was open for 3% of the time, Pallas kernels for 0%

commit v1 on v0

v1 whole, which is shorter than its diff:
```python
import math

import jax
import jax.numpy as jnp
from jax import lax
from jax.experimental import pallas as pl
from jax.experimental.pallas import tpu as pltpu
from jax.sharding import PartitionSpec as P

BF16 = jnp.bfloat16
F32 = jnp.float32
VMEM = pl.BlockSpec(memory_space=pltpu.VMEM)
PAIR = ("blk", "tok")

CORE_0 = ((3, 1), (3, 0), (1, 1), (0, 1))
CORE_1 = ((2, 1), (2, 0), (1, 0), (0, 0))


def in_vmem(array):
    return pltpu.with_memory_space_constraint(array, pltpu.VMEM)


def kernel_call(kernel, outs, *operands, scratch=(), flops=0):
    return pl.pallas_call(
        kernel,
        out_shape=outs,
        in_specs=[VMEM] * len(operands),
        out_specs=[VMEM] * len(outs),
        scratch_shapes=list(scratch),
        cost_estimate=pl.CostEstimate(flops=flops, bytes_accessed=0, transcendentals=0),
        compiler_params=pltpu.CompilerParams(vmem_limit_bytes=32 * 1024 * 1024),
    )(*[in_vmem(operand) for operand in operands])


def move(array, blks, toks, where):
    pairs = []
    for b in range(blks):
        for t in range(toks):
            to = where(b, t)
            if to is not None:
                pairs.append((b * toks + t, to[0] * toks + to[1]))
    return lax.ppermute(array, PAIR, pairs)


def pick(core, a, b):
    return jnp.where(core == 0, a, b)


def pack_kernel(enc, dec, bias, whole, half, sems):
    rows, width = enc.shape
    core = lax.axis_index("tok") % 2
    copies = [
        pltpu.make_async_copy(enc, whole.at[pl.ds(0, rows), pl.ds(0, width)], sems.at[0]),
        pltpu.make_async_copy(dec, whole.at[pl.ds(rows, rows), pl.ds(0, width)], sems.at[1]),
    ]
    for copy in copies:
        copy.start()
    side = jnp.broadcast_to(bias[...].reshape(1, rows), (2 * rows, rows)).astype(F32)
    side = jnp.concatenate([side, jnp.zeros((2 * rows, 128 - rows), F32)], axis=1).astype(BF16)
    whole[:, width:] = side
    half[:, width:] = side[:rows]
    for copy in copies:
        copy.wait()

    @pl.when(core == 0)
    def _():
        half[:, :width] = whole[:rows, :width]

    @pl.when(core == 1)
    def _():
        half[:, :width] = whole[rows:, :width]


def step_kernel(
    inputs, targets, mask, enc, dec, bias, dec_bias, one, one_other, far, far_other,
    recon, send, keep, enc_all, dec_all, bias_all, enc_terms, dec_terms,
):
    rows, width = enc.shape
    latents = mask.shape[1]
    rank = lax.axis_index("blk")
    tok = lax.axis_index("tok")
    core = tok % 2
    chip = tok // 2
    lanes = lax.broadcasted_iota(jnp.int32, (8, latents), 1)

    def at(block):
        return pl.ds(pl.multiple_of(block * rows, rows), rows)

    def put(block, enc_from, dec_from, side):
        enc_all[at(block), :] = enc_from
        dec_all[at(block), :] = dec_from
        mine = (lanes >= block * rows) & (lanes < block * rows + rows)
        moved = pltpu.roll(side.astype(F32), block * rows, axis=1)
        bias_all[...] = jnp.where(mine, moved, bias_all[...])

    bias_all[...] = jnp.zeros_like(bias_all)
    own = jnp.broadcast_to(bias[...].reshape(1, rows), (8, rows)).astype(F32)
    own = jnp.concatenate([own, jnp.zeros((8, latents - rows), F32)], axis=1)
    put(rank, enc[...], dec[...], own)

    def unpack(enc_half, dec_half, first, second):
        put(rank ^ 1, enc_half[:, :width], dec_half[:, :width], enc_half[0:16, width:][:8])
        put(rank ^ 3, first[:rows, :width], first[rows:, :width], first[0:16, width:][:8])
        put(rank ^ 2, second[:rows, :width], second[rows:, :width], second[0:16, width:][:8])

    @pl.when(core == 0)
    def _():
        unpack(one, one_other, far, far_other)

    @pl.when(core == 1)
    def _():
        unpack(one_other, one, far_other, far)

    gate = mask[...].astype(F32)
    pre = lax.dot_general(
        inputs[...], enc_all[...], (((1,), (1,)), ((), ())), preferred_element_type=F32
    )
    act = ((pre + bias_all[0:1, :]) * gate).astype(BF16)
    recon_full = jnp.dot(act, dec_all[...], preferred_element_type=F32)
    recon_full = recon_full + dec_bias[...].reshape(1, width)
    recon[...] = recon_full.astype(BF16)
    error = (recon_full - targets[...].astype(F32)).astype(BF16)
    back = lax.dot_general(
        error, dec_all[...], (((1,), (1,)), ((), ())), preferred_element_type=F32
    )
    dpre = (back * gate).astype(BF16)
    enc_terms[...] = lax.dot_general(
        dpre, inputs[...], (((0,), (0,)), ((), ())), preferred_element_type=F32
    )
    dec_terms[...] = lax.dot_general(
        act, error, (((0,), (0,)), ((), ())), preferred_element_type=F32
    )
    share = send.shape[1]
    for i, (zero, other) in enumerate(zip(CORE_0, CORE_1, strict=True)):
        for out, a, b in ((keep, zero, other), (send, other, zero)):
            block = rank ^ pick(core, a[0], b[0])
            to = chip ^ pick(core, a[1], b[1])
            for quarter in range(2):
                cols = pl.ds(pl.multiple_of((to * 2 + quarter) * share, share), share)
                for k, terms in enumerate((enc_terms, dec_terms)):
                    start = (i * 4 + quarter * 2 + k) * rows
                    out[start : start + rows, :] = terms[at(block), cols].astype(BF16)


def add_kernel(keep, came, *pieces):
    rows = pieces[0].shape[0]
    for i, piece in enumerate(pieces):
        span = slice(i * rows, (i + 1) * rows)
        piece[...] = (keep[span, :].astype(F32) + came[span, :].astype(F32)).astype(BF16)


def owner_kernel(a, b, c, d, own, send, keep):
    rows = keep.shape[0]
    core = lax.axis_index("tok") % 2

    def total(last):
        return (
            a[...].astype(F32) + b[...].astype(F32) + c[...].astype(F32) + last[...].astype(F32)
        )

    @pl.when(core == 0)
    def _():
        whole = total(d)
        keep[...] = whole[:rows]
        send[...] = whole[rows:].astype(BF16)

    @pl.when(core == 1)
    def _():
        whole = total(own)
        keep[...] = whole[rows:]
        send[...] = whole[:rows].astype(BF16)


def last_kernel(factor, keep, came, grad_enc, grad_dec):
    rows = grad_enc.shape[0]
    total = (keep[...] + came[...].astype(F32)) * factor
    grad_enc[...] = total[:rows]
    grad_dec[...] = total[rows:]


def small_body(inputs, targets, mask, enc_weight, enc_bias, dec_weight, dec_bias):
    blks, toks = lax.axis_size("blk"), lax.axis_size("tok")
    rows, width = enc_weight.shape
    tokens, latents = mask.shape
    share = width // toks
    factor = 1.0 / math.sqrt(tokens * blks * toks)

    def swap(array):
        return move(array, blks, toks, lambda b, t: (b, t ^ 1))

    whole, half = pl.pallas_call(
        pack_kernel,
        out_shape=[pltpu.VMEM((2 * rows, width + 128), BF16), pltpu.VMEM((rows, width + 128), BF16)],
        in_specs=[pl.BlockSpec(memory_space=pl.ANY)] * 2 + [VMEM],
        out_specs=[VMEM] * 2,
        scratch_shapes=[pltpu.SemaphoreType.DMA((2,))],
    )(enc_weight, dec_weight, enc_bias)
    far = move(whole, blks, toks, lambda b, t: (b ^ (3, 2)[t % 2], t))
    one = move(half, blks, toks, lambda b, t: (b ^ 1, t))
    one_other = swap(one)
    far_other = swap(far)

    recon, send, keep = kernel_call(
        step_kernel,
        [
            pltpu.VMEM((tokens, width), BF16),
            pltpu.VMEM((16 * rows, share), BF16),
            pltpu.VMEM((16 * rows, share), BF16),
        ],
        inputs, targets, mask, enc_weight, dec_weight, enc_bias, dec_bias, one, one_other, far, far_other,
        scratch=[
            pltpu.VMEM((latents, width), BF16),
            pltpu.VMEM((latents, width), BF16),
            pltpu.VMEM((8, latents), F32),
            pltpu.VMEM((latents, width), F32),
            pltpu.VMEM((latents, width), F32),
        ],
        flops=10 * tokens * latents * width,
    )
    came = swap(send)
    pieces = kernel_call(add_kernel, [pltpu.VMEM((4 * rows, share), BF16)] * 4, keep, came)
    arrived = []
    for i, (zero, other) in enumerate(zip(CORE_0, CORE_1, strict=True)):

        def where(b, t, steps=(zero, other)):
            blk, chip = steps[t % 2]
            return None if (blk, chip) == (0, 0) else (b ^ blk, t ^ (2 * chip))

        arrived.append(move(pieces[i], blks, toks, where))
    send, keep = kernel_call(
        owner_kernel,
        [pltpu.VMEM((2 * rows, share), BF16), pltpu.VMEM((2 * rows, share), F32)],
        *arrived, pieces[3],
    )
    came = swap(send)
    grad_enc, grad_dec = kernel_call(
        lambda *refs: last_kernel(factor, *refs),
        [jax.ShapeDtypeStruct((rows, share), F32)] * 2,
        keep, came,
    )
    return recon, grad_enc, grad_dec


def large_body(inputs, targets, mask, enc_weight, enc_bias, dec_weight, dec_bias):
    gate = mask.astype(F32)
    enc_all = lax.all_gather(enc_weight, "blk", axis=0, tiled=True)
    dec_all = lax.all_gather(dec_weight, "blk", axis=0, tiled=True)
    bias_all = lax.all_gather(enc_bias, "blk", axis=0, tiled=True)
    pre = lax.dot_general(
        inputs, enc_all, (((1,), (1,)), ((), ())), preferred_element_type=F32
    )
    act = ((pre + bias_all.astype(F32)[None, :]) * gate).astype(BF16)
    recon_full = jnp.dot(act, dec_all, preferred_element_type=F32) + dec_bias[None, :]
    error = (recon_full - targets.astype(F32)).astype(BF16)
    back = lax.dot_general(
        error, dec_all, (((1,), (1,)), ((), ())), preferred_element_type=F32
    )
    dpre = (back * gate).astype(BF16)
    total = inputs.shape[0] * lax.axis_size("blk") * lax.axis_size("tok")
    factor = 1.0 / math.sqrt(total)
    grads = []
    for left, right in ((dpre, inputs), (act, error)):
        terms = lax.dot_general(
            left, right, (((0,), (0,)), ((), ())), preferred_element_type=F32
        )
        terms = lax.psum_scatter(terms, "blk", scatter_dimension=0, tiled=True)
        terms = lax.psum_scatter(terms, "tok", scatter_dimension=1, tiled=True)
        grads.append(terms * factor)
    return recon_full.astype(BF16), grads[0], grads[1]


def solution(mesh):
    small = mesh.shape["blk"] == 4 and mesh.shape["tok"] == 4
    tokens = P(("layers", "blk", "tok"), None)
    rows = P(("layers", "blk"), None)
    return jax.shard_map(
        small_body if small else large_body,
        mesh=mesh,
        in_specs=(tokens, tokens, tokens, rows, P(("layers", "blk")), rows, P("layers")),
        out_specs=(tokens, P(("layers", "blk"), "tok"), P(("layers", "blk"), "tok")),
        check_vma=False,
    )
```

time: 110 us -> 36.7 us (0.33)
  waiting for transfers between devices: 73.7 us -> 13.2 us
  between operations: 14.2 us -> 0.73 us
  other arithmetic: 4.17 us -> 0 us
  Pallas kernels: 0 us -> 3.9 us
  matrix products: 3.03 us -> 0 us
  local copies, waits for them, and re-layouts: 2.28 us -> 4.44 us
  starting transfers between devices: 12 us -> 14.1 us
    reduce_scatter x2 -> x0, waiting for transfers between devices: 38.6 us -> none  [the longest x1 20.7 us: body(): lax.psum_scatter(enc_accum.astype(jnp.bfloat16), 'tok', scatter_dimension...]
    ppermute x15 -> x10, waiting for transfers between devices: 35.1 us -> 13.2 us  [move(): return lax.ppermute(array, PAIR, pairs)]
    pallas_call x0 -> x5, Pallas kernels: none -> 3.9 us  [the longest x4 2.31 us: kernel_call(): pl.pallas_call(kernel, out_shape=outs, in_specs=[VMEM] * len(operands), o...]
    dot_general x7 -> x0, matrix products: 3.03 us -> none  [the longest x1 1.11 us: body(): jnp.dot(act_half, dec_all, preferred_element_type=jnp.float32)]
    mul x2 -> x0, other arithmetic: 2.67 us -> none  [body(): return (recon, grad_enc * factor, grad_dec * factor)]
    unnamed x15, local copies, waits for them, and re-layouts: 2.16 us -> 4.44 us
    ppermute x15 -> x10, starting transfers between devices: 12 us -> 14.1 us  [move(): return lax.ppermute(array, PAIR, pairs)]
    convert_element_type x19 -> x0, other arithmetic: 1.5 us -> none  [the longest x1 0.65 us: body(): dec_accum.astype(jnp.bfloat16)]
  transfers between devices with their start and end apart: 17 -> 10, of which waited for: 17 -> 7; matrix products, arithmetic and copies ran while one was open for 3% -> 2% of each run, Pallas kernels for 0% -> 0%
where the time goes in v1:
time: 36.7 us; the launch traced here: 36.4 us
  starting transfers between devices  14.1 us (38%)
  waiting for transfers between devices  13.2 us (36%)
  local copies, waits for them, and re-layouts  4.44 us (12%)
  Pallas kernels  3.9 us (11%)
  between operations  0.73 us (2%)
    ppermute x10, starting transfers between devices, move(): return lax.ppermute(array, PAIR, pairs)  14.1 us
    ppermute x10, waiting for transfers between devices, move(): return lax.ppermute(array, PAIR, pairs)  13.2 us
    unnamed x15, local copies, waits for them, and re-layouts  4.44 us
    pallas_call x4, Pallas kernels, kernel_call(): pl.pallas_call(kernel, out_shape=outs, in_specs=[VMEM] * len(operands), o...  2.31 us
    pallas_call x1, Pallas kernels, small_body(): pl.pallas_call(pack_kernel, out_shape=[pltpu.VMEM((2 * rows, width + 128)...  1.6 us
  transfers between devices with their start and end apart: 10, of which 7 were waited for; matrix products, arithmetic and copies ran while one was open for 2% of the time, Pallas kernels for 0%

profile of v1, /device:TPU:0, one launch (start us, length us, event | category | flops | bytes accessed | tf_op | source)
XLA Modules:
  0.0 36.4 jit_solution(12413039215444614741)
XLA Ops:
  0.6 0.0 copy-start.2
  0.6 0.0 copy-start.3
  0.7 0.0 copy-start.5
  0.7 1.6 %shard_map.94 = (bf16[64,1152]{1,0:T(8,128)(2,1)S(1)}, bf16[32,1152]{1,0:T(8,128)(2,1)S(1)}) custom-call(bf16[32,1024]{1,0:T(8,128)(2,1)} %enc.3, bf16[32,1024]{1,0:T(8,128)(2,1)} %dec.3, bf16[32]{0:T(256)(128)(2,1)} %bias.3), custom_call_target="tpu_custom_call" | custom-call | tf_op jit(solution)/shard_map/pallas_call | solution.py:191
  2.3 5.1 %collective-permute-start.2 = (bf16[64,1152]{1,0:T(8,128)(2,1)S(1)}, bf16[64,1152]{1,0:T(8,128)(2,1)S(1)}, u32[]{:S(2)}, u32[]{:S(2)}) collective-permute-start(bf16[64,1152]{1,0:T(8,128)(2,1)S(1)} %get-tuple-element.17), channel_id=1, source_target_pairs={{0,12},{1,9},{2,14},{3,11},{4,8},{5,13},{6,10},{7,15},{8,4},{9,1},... | collective-permute-start | bytes 442376 | tf_op jit(solution)/shard_map/ppermute | solution.py:42
  7.4 0.0 collective-permute-start
  7.4 4.7 %collective-permute-done.2.far = bf16[64,1152]{1,0:T(8,128)(2,1)S(1)} collective-permute-done((bf16[64,1152]{1,0:T(8,128)(2,1)S(1)}, bf16[64,1152]{1,0:T(8,128)(2,1)S(1)}, u32[]{:S(2)}, u32[]{:S(2)}) %collective-permute-start.2) | collective-permute-done | bytes 147488 | tf_op jit(solution)/shard_map/ppermute | solution.py:42
  12.1 0.1 collective-permute-start.3
  12.2 0.4 %collective-permute-done.one = bf16[32,1152]{1,0:T(8,128)(2,1)S(1)} collective-permute-done((bf16[32,1152]{1,0:T(8,128)(2,1)S(1)}, bf16[32,1152]{1,0:T(8,128)(2,1)S(1)}, u32[]{:S(2)}, u32[]{:S(2)}) %collective-permute-start) | collective-permute-done | bytes 73760 | tf_op jit(solution)/shard_map/ppermute | solution.py:42
  12.6 0.0 collective-permute-start.1
  12.6 1.3 %collective-permute-done.1.one_other = bf16[32,1152]{1,0:T(8,128)(2,1)S(1)} collective-permute-done((bf16[32,1152]{1,0:T(8,128)(2,1)S(1)}, bf16[32,1152]{1,0:T(8,128)(2,1)S(1)}, u32[]{:S(2)}, u32[]{:S(2)}) %collective-permute-start.1) | collective-permute-done | bytes 73760 | tf_op jit(solution)/shard_map/ppermute | solution.py:42
  13.9 0.0 collective-permute-done.3.far_other
  13.9 0.0 copy-done.2
  13.9 0.0 copy-done.3
  13.9 0.0 copy-done.5
  13.9 0.0 copy-start
  13.9 1.0 %copy-done = bf16[256,1024]{1,0:T(8,128)(2,1)S(1)} copy-done((bf16[256,1024]{1,0:T(8,128)(2,1)S(1)}, bf16[256,1024]{1,0:T(8,128)(2,1)}, u32[]{:S(2)}) %copy-start) | copy-done | bytes 524312
  15.0 0.0 copy-start.1
  15.0 1.0 %copy-done.1 = bf16[256,1024]{1,0:T(8,128)(2,1)S(1)} copy-done((bf16[256,1024]{1,0:T(8,128)(2,1)S(1)}, bf16[256,1024]{1,0:T(8,128)(2,1)}, u32[]{:S(2)}) %copy-start.1) | copy-done | bytes 524312
  16.0 0.0 copy-start.4
  16.0 0.9 %copy-done.4 = s32[256,128]{1,0:T(8,128)S(1)} copy-done((s32[256,128]{1,0:T(8,128)S(1)}, s32[256,128]{1,0:T(8,128)}, u32[]{:S(2)}) %copy-start.4) | copy-done | bytes 131096
  16.9 0.0 copy-start.6
  16.9 0.7 %copy-done.6 = bf16[32]{0:T(256)(128)(2,1)S(1)} copy-done((bf16[32]{0:T(256)(128)(2,1)S(1)}, bf16[32]{0:T(256)(128)(2,1)}, u32[]{:S(2)}) %copy-start.6) | copy-done | bytes 88
  17.6 1.6 %shard_map.95 = (bf16[256,1024]{1,0:T(8,128)(2,1)S(1)}, bf16[512,256]{1,0:T(8,128)(2,1)S(1)}, bf16[512,256]{1,0:T(8,128)(2,1)S(1)}) custom-call(bf16[256,1024]{1,0:T(8,128)(2,1)S(1)} %copy-done, bf16[256,1024]{1,0:T(8,128)(2,1)S(1)} %copy-done.1, s32[256,128]{1,0:T(8,128)S(1)} %copy-done.4, bf16[32,1024]{1,0:T(8,128)(2,1)S(1)} %copy-done.2, ...), custom_call_target="tpu_custom_call" | custom-call | flops 335544320 | tf_op jit(solution)/shard_map/pallas_call | solution.py:24
  19.2 0.3 collective-permute-start.4
  19.4 1.3 %collective-permute-done.4.came = bf16[512,256]{1,0:T(8,128)(2,1)S(1)} collective-permute-done((bf16[512,256]{1,0:T(8,128)(2,1)S(1)}, bf16[512,256]{1,0:T(8,128)(2,1)S(1)}, u32[]{:S(2)}, u32[]{:S(2)}) %collective-permute-start.4) | collective-permute-done | bytes 262176 | tf_op jit(solution)/shard_map/ppermute | solution.py:42
  20.8 0.1 shard_map.96
  20.8 3.5 %collective-permute-start.8 = (bf16[128,256]{1,0:T(8,128)(2,1)S(1)}, bf16[128,256]{1,0:T(8,128)(2,1)S(1)}, u32[]{:S(2)}, u32[]{:S(2)}) collective-permute-start(bf16[128,256]{1,0:T(8,128)(2,1)S(1)} %get-tuple-element.24.own), channel_id=1, source_target_pairs={{0,2},{2,0},{4,6},{6,4},{8,10},{10,8},{12,14},{14,12},{16,18},{18,... | collective-permute-start | bytes 196616 | tf_op jit(solution)/shard_map/ppermute | solution.py:42
  24.3 4.0 %collective-permute-start.5 = (bf16[128,256]{1,0:T(8,128)(2,1)S(1)}, bf16[128,256]{1,0:T(8,128)(2,1)S(1)}, u32[]{:S(2)}, u32[]{:S(2)}) collective-permute-start(bf16[128,256]{1,0:T(8,128)(2,1)S(1)} %get-tuple-element.21), channel_id=1, source_target_pairs={{0,14},{1,11},{2,12},{3,9},{4,10},{5,15},{6,8},{7,13},{8,6},{9,3},... | collective-permute-start | bytes 196616 | tf_op jit(solution)/shard_map/ppermute | solution.py:42
  28.4 0.1 collective-permute-start.6
  28.5 0.9 %collective-permute-start.7 = (bf16[128,256]{1,0:T(8,128)(2,1)S(1)}, bf16[128,256]{1,0:T(8,128)(2,1)S(1)}, u32[]{:S(2)}, u32[]{:S(2)}) collective-permute-start(bf16[128,256]{1,0:T(8,128)(2,1)S(1)} %get-tuple-element.23), channel_id=1, source_target_pairs={{0,6},{1,5},{2,4},{3,7},{4,2},{5,1},{6,0},{7,3},{8,14},{9,13},{10,... | collective-permute-start | bytes 196616 | tf_op jit(solution)/shard_map/ppermute | solution.py:42
  29.3 0.0 collective-permute-done.8.d
  29.4 2.7 %collective-permute-done.5.a = bf16[128,256]{1,0:T(8,128)(2,1)S(1)} collective-permute-done((bf16[128,256]{1,0:T(8,128)(2,1)S(1)}, bf16[128,256]{1,0:T(8,128)(2,1)S(1)}, u32[]{:S(2)}, u32[]{:S(2)}) %collective-permute-start.5) | collective-permute-done | bytes 65568 | tf_op jit(solution)/shard_map/ppermute | solution.py:42
  32.0 2.4 %collective-permute-done.6.b = bf16[128,256]{1,0:T(8,128)(2,1)S(1)} collective-permute-done((bf16[128,256]{1,0:T(8,128)(2,1)S(1)}, bf16[128,256]{1,0:T(8,128)(2,1)S(1)}, u32[]{:S(2)}, u32[]{:S(2)}) %collective-permute-start.6) | collective-permute-done | bytes 65568 | tf_op jit(solution)/shard_map/ppermute | solution.py:42
  34.4 0.0 collective-permute-done.7.c
  34.5 0.1 collective-permute-start.9
  34.5 0.8 %copy.10 = bf16[256,1024]{1,0:T(8,128)(2,1)} copy(bf16[256,1024]{1,0:T(8,128)(2,1)S(1)} %get-tuple-element.29) | data formatting | bytes 1048576
  35.3 0.4 %collective-permute-done.9.refs_1_ = bf16[64,256]{1,0:T(8,128)(2,1)S(1)} collective-permute-done((bf16[64,256]{1,0:T(8,128)(2,1)S(1)}, bf16[64,256]{1,0:T(8,128)(2,1)S(1)}, u32[]{:S(2)}, u32[]{:S(2)}) %collective-permute-start.9) | collective-permute-done | bytes 32800 | tf_op jit(solution)/shard_map/ppermute | solution.py:42
  35.7 0.6 %shard_map.98 = (f32[32,256]{1,0:T(8,128)}, f32[32,256]{1,0:T(8,128)}) custom-call(f32[64,256]{1,0:T(8,128)S(1)} %get-tuple-element.25.refs_0_, bf16[64,256]{1,0:T(8,128)(2,1)S(1)} %collective-permute-done.9.refs_1_), custom_call_target="tpu_custom_call" | custom-call | tf_op jit(solution)/shard_map/pallas_call | solution.py:24
  (1 shorter events, 0.0 us)
Async XLA Ops:
  0.6 13.3 %copy-start.2 = (bf16[32,1024]{1,0:T(8,128)(2,1)S(1)}, bf16[32,1024]{1,0:T(8,128)(2,1)}, u32[]{:S(2)}) copy-start(bf16[32,1024]{1,0:T(8,128)(2,1)} %enc.3) | copy-start | bytes 196612
  0.6 13.3 %copy-start.3 = (bf16[32,1024]{1,0:T(8,128)(2,1)S(1)}, bf16[32,1024]{1,0:T(8,128)(2,1)}, u32[]{:S(2)}) copy-start(bf16[32,1024]{1,0:T(8,128)(2,1)} %dec.3) | copy-start | bytes 196612
  0.7 13.3 %copy-start.5 = (f32[1024]{0:T(1024)S(1)}, f32[1024]{0:T(1024)}, u32[]{:S(2)}) copy-start(f32[1024]{0:T(1024)} %dec_bias.1) | copy-start | bytes 12292
  2.3 9.8 %collective-permute-start.2 = (bf16[64,1152]{1,0:T(8,128)(2,1)S(1)}, bf16[64,1152]{1,0:T(8,128)(2,1)S(1)}, u32[]{:S(2)}, u32[]{:S(2)}) collective-permute-start(bf16[64,1152]{1,0:T(8,128)(2,1)S(1)} %get-tuple-element.17), channel_id=1, source_target_pairs={{0,12},{1,9},{2,14},{3,11},{4,8},{5,13},{6,10},{7,15},{8,4},{9,1},... | collective-permute-start | bytes 442376 | tf_op jit(solution)/shard_map/ppermute | solution.py:42
  7.4 5.3 %collective-permute-start = (bf16[32,1152]{1,0:T(8,128)(2,1)S(1)}, bf16[32,1152]{1,0:T(8,128)(2,1)S(1)}, u32[]{:S(2)}, u32[]{:S(2)}) collective-permute-start(bf16[32,1152]{1,0:T(8,128)(2,1)S(1)} %get-tuple-element.16), channel_id=1, source_target_pairs={{0,4},{1,5},{2,6},{3,7},{4,0},{5,1},{6,2},{7,3},{8,12},{9,13},{10,... | collective-permute-start | bytes 221192 | tf_op jit(solution)/shard_map/ppermute | solution.py:42
  12.1 1.8 %collective-permute-start.3 = (bf16[64,1152]{1,0:T(8,128)(2,1)S(1)}, bf16[64,1152]{1,0:T(8,128)(2,1)S(1)}, u32[]{:S(2)}, u32[]{:S(2)}) collective-permute-start(bf16[64,1152]{1,0:T(8,128)(2,1)S(1)} %collective-permute-done.2.far), channel_id=1, source_target_pairs={{0,1},{1,0},{2,3},{3,2},{4,5},{5,4},{6,7},{7,6},{8,9},{9,8},{10,11... | collective-permute-start | bytes 442376 | tf_op jit(solution)/shard_map/ppermute | solution.py:42
  12.6 1.3 %collective-permute-start.1 = (bf16[32,1152]{1,0:T(8,128)(2,1)S(1)}, bf16[32,1152]{1,0:T(8,128)(2,1)S(1)}, u32[]{:S(2)}, u32[]{:S(2)}) collective-permute-start(bf16[32,1152]{1,0:T(8,128)(2,1)S(1)} %collective-permute-done.one), channel_id=1, source_target_pairs={{0,1},{1,0},{2,3},{3,2},{4,5},{5,4},{6,7},{7,6},{8,9},{9,8},{10,11... | collective-permute-start | bytes 221192 | tf_op jit(solution)/shard_map/ppermute | solution.py:42
  13.9 1.0 %copy-start = (bf16[256,1024]{1,0:T(8,128)(2,1)S(1)}, bf16[256,1024]{1,0:T(8,128)(2,1)}, u32[]{:S(2)}) copy-start(bf16[256,1024]{1,0:T(8,128)(2,1)} %inputs.1) | copy-start | bytes 1572868
  15.0 1.0 %copy-start.1 = (bf16[256,1024]{1,0:T(8,128)(2,1)S(1)}, bf16[256,1024]{1,0:T(8,128)(2,1)}, u32[]{:S(2)}) copy-start(bf16[256,1024]{1,0:T(8,128)(2,1)} %targets.1) | copy-start | bytes 1572868
  16.0 0.9 %copy-start.4 = (s32[256,128]{1,0:T(8,128)S(1)}, s32[256,128]{1,0:T(8,128)}, u32[]{:S(2)}) copy-start(s32[256,128]{1,0:T(8,128)} %mask.1) | copy-start | bytes 393220
  16.9 0.7 %copy-start.6 = (bf16[32]{0:T(256)(128)(2,1)S(1)}, bf16[32]{0:T(256)(128)(2,1)}, u32[]{:S(2)}) copy-start(bf16[32]{0:T(256)(128)(2,1)} %bias.3) | copy-start | bytes 196
  19.2 1.6 %collective-permute-start.4 = (bf16[512,256]{1,0:T(8,128)(2,1)S(1)}, bf16[512,256]{1,0:T(8,128)(2,1)S(1)}, u32[]{:S(2)}, u32[]{:S(2)}) collective-permute-start(bf16[512,256]{1,0:T(8,128)(2,1)S(1)} %get-tuple-element.20), channel_id=1, source_target_pairs={{0,1},{1,0},{2,3},{3,2},{4,5},{5,4},{6,7},{7,6},{8,9},{9,8},{10,11... | collective-permute-start | bytes 786440 | tf_op jit(solution)/shard_map/ppermute | solution.py:42
  20.8 8.5 %collective-permute-start.8 = (bf16[128,256]{1,0:T(8,128)(2,1)S(1)}, bf16[128,256]{1,0:T(8,128)(2,1)S(1)}, u32[]{:S(2)}, u32[]{:S(2)}) collective-permute-start(bf16[128,256]{1,0:T(8,128)(2,1)S(1)} %get-tuple-element.24.own), channel_id=1, source_target_pairs={{0,2},{2,0},{4,6},{6,4},{8,10},{10,8},{12,14},{14,12},{16,18},{18,... | collective-permute-start | bytes 196616 | tf_op jit(solution)/shard_map/ppermute | solution.py:42
  24.3 7.7 %collective-permute-start.5 = (bf16[128,256]{1,0:T(8,128)(2,1)S(1)}, bf16[128,256]{1,0:T(8,128)(2,1)S(1)}, u32[]{:S(2)}, u32[]{:S(2)}) collective-permute-start(bf16[128,256]{1,0:T(8,128)(2,1)S(1)} %get-tuple-element.21), channel_id=1, source_target_pairs={{0,14},{1,11},{2,12},{3,9},{4,10},{5,15},{6,8},{7,13},{8,6},{9,3},... | collective-permute-start | bytes 196616 | tf_op jit(solution)/shard_map/ppermute | solution.py:42
  28.4 6.1 %collective-permute-start.6 = (bf16[128,256]{1,0:T(8,128)(2,1)S(1)}, bf16[128,256]{1,0:T(8,128)(2,1)S(1)}, u32[]{:S(2)}, u32[]{:S(2)}) collective-permute-start(bf16[128,256]{1,0:T(8,128)(2,1)S(1)} %get-tuple-element.22), channel_id=1, source_target_pairs={{0,12},{1,9},{2,14},{3,11},{4,8},{5,13},{6,10},{7,15},{8,4},{9,1},... | collective-permute-start | bytes 196616 | tf_op jit(solution)/shard_map/ppermute | solution.py:42
  28.5 6.0 %collective-permute-start.7 = (bf16[128,256]{1,0:T(8,128)(2,1)S(1)}, bf16[128,256]{1,0:T(8,128)(2,1)S(1)}, u32[]{:S(2)}, u32[]{:S(2)}) collective-permute-start(bf16[128,256]{1,0:T(8,128)(2,1)S(1)} %get-tuple-element.23), channel_id=1, source_target_pairs={{0,6},{1,5},{2,4},{3,7},{4,2},{5,1},{6,0},{7,3},{8,14},{9,13},{10,... | collective-permute-start | bytes 196616 | tf_op jit(solution)/shard_map/ppermute | solution.py:42
  34.5 1.3 %collective-permute-start.9 = (bf16[64,256]{1,0:T(8,128)(2,1)S(1)}, bf16[64,256]{1,0:T(8,128)(2,1)S(1)}, u32[]{:S(2)}, u32[]{:S(2)}) collective-permute-start(bf16[64,256]{1,0:T(8,128)(2,1)S(1)} %get-tuple-element.26), channel_id=1, source_target_pairs={{0,1},{1,0},{2,3},{3,2},{4,5},{5,4},{6,7},{7,6},{8,9},{9,8},{10,11... | collective-permute-start | bytes 98312 | tf_op jit(solution)/shard_map/ppermute | solution.py:42

commit v2 on v1

v2 whole, which is shorter than its diff:
```python
import math

import jax
import jax.numpy as jnp
from jax import lax
from jax.experimental import pallas as pl
from jax.experimental.pallas import tpu as pltpu
from jax.sharding import PartitionSpec as P

BF16 = jnp.bfloat16
F32 = jnp.float32
VMEM = pl.BlockSpec(memory_space=pltpu.VMEM)
PAIR = ("blk", "tok")
STRIP = 16
TILE = 128

STEPS = (3, 2, 1, 0)


def in_vmem(array):
    return pltpu.with_memory_space_constraint(array, pltpu.VMEM)


def kernel_call(kernel, outs, *operands, scratch=(), flops=0):
    return pl.pallas_call(
        kernel,
        out_shape=outs,
        in_specs=[VMEM] * len(operands),
        out_specs=[VMEM] * len(outs),
        scratch_shapes=list(scratch),
        cost_estimate=pl.CostEstimate(flops=flops, bytes_accessed=0, transcendentals=0),
        compiler_params=pltpu.CompilerParams(vmem_limit_bytes=32 * 1024 * 1024),
    )(*[in_vmem(operand) for operand in operands])


def move(array, blks, toks, where):
    pairs = []
    for b in range(blks):
        for t in range(toks):
            to = where(b, t)
            if to is not None:
                pairs.append((b * toks + t, to[0] * toks + to[1]))
    return lax.ppermute(array, PAIR, pairs)


def pack_kernel(enc, dec, bias, whole, half, side, sems):
    rows, width = enc.shape
    rank = lax.axis_index("blk")
    core = lax.axis_index("tok") % 2
    strips = rows // STRIP
    copies = [pltpu.make_async_copy(bias, side, sems.at[0])]
    for k, source in enumerate((enc, dec)):
        for i in range(strips):
            j = k * strips + i
            copies.append(
                pltpu.make_async_copy(
                    source.at[pl.ds(i * STRIP, STRIP)], whole.at[:, pl.ds(j * width, width)], sems.at[1 + j]
                )
            )
    for copy in copies:
        copy.start()
    copies[0].wait()
    tile = jnp.broadcast_to(side[...].astype(F32).reshape(1, rows), (STRIP, rows))
    tile = jnp.concatenate([tile, jnp.zeros((STRIP, TILE - rows), F32)], axis=1)
    tile = pltpu.roll(tile, rank * rows, axis=1).astype(BF16)
    whole[:, 2 * strips * width :] = tile
    half[:, strips * width :] = tile
    for copy in copies[1:]:
        copy.wait()

    @pl.when(core == 0)
    def _():
        half[:, : strips * width] = whole[:, : strips * width]

    @pl.when(core == 1)
    def _():
        half[:, : strips * width] = whole[:, strips * width : 2 * strips * width]


def load_kernel(inputs, targets, mask, dec_bias, after, *refs):
    *outs, sems = refs
    parts = (len(outs) - 2) // 2
    copies = []
    for i, source in enumerate((inputs, targets)):
        for j, out in enumerate(outs[i * parts : (i + 1) * parts]):
            rows = out.shape[0]
            copies.append((source.at[pl.ds(j * rows, rows)], out))
    copies += [(mask, outs[-2]), (dec_bias, outs[-1])]
    copies = [pltpu.make_async_copy(*pair, sems.at[i]) for i, pair in enumerate(copies)]
    for copy in copies:
        copy.start()
    for copy in copies:
        copy.wait()


def contract(a, b, over_a, over_b):
    return lax.dot_general(a, b, (((over_a,), (over_b,)), ((), ())), preferred_element_type=F32)


def step_kernel(dec_bias, own, one, one_other, far, far_other, *refs):
    *refs, enc_all, dec_all, error_all, enc_terms, dec_terms = refs
    *refs, own_piece = refs
    refs, pieces = refs[: -len(STEPS)], refs[-len(STEPS) :]
    *refs, recon = refs
    parts = len(refs) // 4
    width = recon.shape[1]
    strips = one.shape[1] // width
    rows = strips * STRIP
    rank = lax.axis_index("blk")
    tok = lax.axis_index("tok")
    core = tok % 2
    chip = tok // 2

    def at(block):
        return pl.ds(pl.multiple_of(block * rows, rows), rows)

    def put(to, block, source, first):
        for i in range(strips):
            span = pl.ds(pl.multiple_of(block * rows + i * STRIP, STRIP), STRIP)
            j = first + i
            to[span, :] = source[:, j * width : (j + 1) * width]

    def unpack(enc_half, dec_half, first, second):
        put(enc_all, rank ^ 1, enc_half, 0)
        put(dec_all, rank ^ 1, dec_half, 0)
        for block, source in ((rank ^ 3, first), (rank ^ 2, second)):
            put(enc_all, block, source, 0)
            put(dec_all, block, source, strips)

    put(enc_all, rank, own, 0)
    put(dec_all, rank, own, strips)

    @pl.when(core == 0)
    def _():
        unpack(one, one_other, far, far_other)

    @pl.when(core == 1)
    def _():
        unpack(one_other, one, far_other, far)

    bias = sum(source[:, -TILE:].astype(F32) for source in (own, one, far, far_other))[0:1, :]
    base = dec_bias[...].reshape(1, width)
    half = pieces[0].shape[1]
    cols = pl.ds(pl.multiple_of((chip ^ core) * half, half), half)
    groups = (refs[: 2 * parts + 1], refs[2 * parts + 1 :])
    tokens = recon.shape[0]
    enc_sum, dec_sum = 0.0, 0.0
    for g, group in enumerate(groups):
        gate_all = group[-1]
        acts, dpres = [], []
        for j in range(parts):
            x, target = group[j], group[parts + j]
            n = x.shape[0]
            span = slice(j * n, (j + 1) * n)
            gate = gate_all[span, :].astype(F32)
            act = ((contract(x[...], enc_all[...], 1, 1) + bias) * gate).astype(BF16)
            recon_full = contract(act, dec_all[...], 1, 0) + base
            if g == 0:
                recon[span, :] = recon_full.astype(BF16)
            error = (recon_full - target[...].astype(F32)).astype(BF16)
            error_all[g * tokens + j * n : g * tokens + (j + 1) * n, :] = error
            dpres.append((contract(error, dec_all[...], 1, 1) * gate).astype(BF16))
            acts.append(act)
        act = jnp.concatenate(acts, axis=0)
        dpre = jnp.concatenate(dpres, axis=0)
        x = jnp.concatenate([part[:, cols] for part in group[:parts]], axis=0)
        dec_sum += contract(act, error_all[g * tokens : (g + 1) * tokens, cols], 0, 0)
        enc_sum += contract(dpre, x, 0, 0)
    enc_terms[...] = enc_sum
    dec_terms[...] = dec_sum
    for step, piece in zip(STEPS, pieces, strict=True):
        piece[:rows, :] = enc_terms[at(rank ^ step), :].astype(BF16)
        piece[rows:, :] = dec_terms[at(rank ^ step), :].astype(BF16)
    own_piece[:rows, :] = enc_terms[at(rank), :]
    own_piece[rows:, :] = dec_terms[at(rank), :]


def owner_kernel(*refs):
    *arrived, own, send, keep = refs
    share = keep.shape[1]
    core = lax.axis_index("tok") % 2
    total = sum(part[...].astype(F32) for part in arrived)

    @pl.when(core == 0)
    def _():
        whole = total + own[...]
        keep[...] = whole[:, :share]
        send[...] = whole[:, share:].astype(BF16)

    @pl.when(core == 1)
    def _():
        keep[...] = total[:, share:]
        send[...] = total[:, :share].astype(BF16)


def last_kernel(factor, keep, came, grad_enc, grad_dec):
    rows = grad_enc.shape[0]
    total = (keep[...] + came[...].astype(F32)) * factor
    grad_enc[...] = total[:rows]
    grad_dec[...] = total[rows:]


def small_body(inputs, targets, mask, enc_weight, enc_bias, dec_weight, dec_bias):
    blks, toks = lax.axis_size("blk"), lax.axis_size("tok")
    rows, width = enc_weight.shape
    tokens, latents = mask.shape
    share = width // toks
    factor = 1.0 / math.sqrt(tokens * blks * toks)

    def swap(array):
        return move(array, blks, toks, lambda b, t: (b, t ^ 1))

    strips = rows // STRIP
    whole, half = pl.pallas_call(
        pack_kernel,
        out_shape=[
            pltpu.VMEM((STRIP, 2 * strips * width + TILE), BF16),
            pltpu.VMEM((STRIP, strips * width + TILE), BF16),
        ],
        in_specs=[pl.BlockSpec(memory_space=pl.ANY)] * 3,
        out_specs=[VMEM] * 2,
        scratch_shapes=[pltpu.VMEM((rows,), BF16), pltpu.SemaphoreType.DMA((1 + 2 * strips,))],
    )(enc_weight, dec_weight, enc_bias)
    far = move(whole, blks, toks, lambda b, t: (b ^ (3, 2)[t % 2], t))
    one = move(half, blks, toks, lambda b, t: (b ^ 1, t))
    parts = 2
    *loaded, dec_bias = pl.pallas_call(
        load_kernel,
        out_shape=[pltpu.VMEM((tokens // parts, width), BF16)] * (2 * parts)
        + [pltpu.VMEM(array.shape, array.dtype) for array in (mask, dec_bias)],
        in_specs=[pl.BlockSpec(memory_space=pl.ANY)] * 4 + [VMEM],
        out_specs=[VMEM] * (2 * parts + 2),
        scratch_shapes=[pltpu.SemaphoreType.DMA((2 * parts + 2,))],
        cost_estimate=pl.CostEstimate(flops=0, bytes_accessed=4 * tokens * width, transcendentals=0),
    )(inputs, targets, mask, dec_bias, in_vmem(one))
    others = [swap(array) for array in loaded]
    one_other = swap(one)
    far_other = swap(far)
    piece = (2 * rows, 2 * share)
    recon, *pieces, own = kernel_call(
        step_kernel,
        [pltpu.VMEM((tokens, width), BF16)]
        + [pltpu.VMEM(piece, BF16)] * len(STEPS)
        + [pltpu.VMEM(piece, F32)],
        dec_bias, whole, one, one_other, far, far_other, *loaded, *others,
        scratch=[
            pltpu.VMEM((latents, width), BF16),
            pltpu.VMEM((latents, width), BF16),
            pltpu.VMEM((2 * tokens, width), BF16),
            pltpu.VMEM((latents, 2 * share), F32),
            pltpu.VMEM((latents, 2 * share), F32),
        ],
        flops=16 * tokens * latents * width,
    )
    arrived = []
    for step, out in zip(STEPS, pieces, strict=True):

        def where(b, t, step=step):
            return None if step == 0 and t % 2 == 0 else (b ^ step, t ^ (2 * (t % 2)))

        arrived.append(move(out, blks, toks, where))
    send, keep = kernel_call(
        owner_kernel,
        [pltpu.VMEM((2 * rows, share), BF16), pltpu.VMEM((2 * rows, share), F32)],
        *arrived, own,
    )
    came = swap(send)
    grad_enc, grad_dec = kernel_call(
        lambda *refs: last_kernel(factor, *refs),
        [jax.ShapeDtypeStruct((rows, share), F32)] * 2,
        keep, came,
    )
    return recon, grad_enc, grad_dec


def large_body(inputs, targets, mask, enc_weight, enc_bias, dec_weight, dec_bias):
    gate = mask.astype(F32)
    enc_all = lax.all_gather(enc_weight, "blk", axis=0, tiled=True)
    dec_all = lax.all_gather(dec_weight, "blk", axis=0, tiled=True)
    bias_all = lax.all_gather(enc_bias, "blk", axis=0, tiled=True)
    pre = lax.dot_general(
        inputs, enc_all, (((1,), (1,)), ((), ())), preferred_element_type=F32
    )
    act = ((pre + bias_all.astype(F32)[None, :]) * gate).astype(BF16)
    recon_full = jnp.dot(act, dec_all, preferred_element_type=F32) + dec_bias[None, :]
    error = (recon_full - targets.astype(F32)).astype(BF16)
    back = lax.dot_general(
        error, dec_all, (((1,), (1,)), ((), ())), preferred_element_type=F32
    )
    dpre = (back * gate).astype(BF16)
    total = inputs.shape[0] * lax.axis_size("blk") * lax.axis_size("tok")
    factor = 1.0 / math.sqrt(total)
    grads = []
    for left, right in ((dpre, inputs), (act, error)):
        terms = lax.dot_general(
            left, right, (((0,), (0,)), ((), ())), preferred_element_type=F32
        )
        terms = lax.psum_scatter(terms, "blk", scatter_dimension=0, tiled=True)
        terms = lax.psum_scatter(terms, "tok", scatter_dimension=1, tiled=True)
        grads.append(terms * factor)
    return recon_full.astype(BF16), grads[0], grads[1]


def solution(mesh):
    small = mesh.shape["blk"] == 4 and mesh.shape["tok"] == 4
    tokens = P(("layers", "blk", "tok"), None)
    rows = P(("layers", "blk"), None)
    return jax.shard_map(
        small_body if small else large_body,
        mesh=mesh,
        in_specs=(tokens, tokens, tokens, rows, P(("layers", "blk")), rows, P("layers")),
        out_specs=(tokens, P(("layers", "blk"), "tok"), P(("layers", "blk"), "tok")),
        check_vma=False,
    )
```

time: 36.7 us -> 28.9 us (0.79)
  waiting for transfers between devices: 13.2 us -> 8.99 us
  local copies, waits for them, and re-layouts: 4.44 us -> 0.79 us
  Pallas kernels: 3.9 us -> 4.61 us
  starting transfers between devices: 14.1 us -> 13.6 us
    ppermute x10 -> x14, waiting for transfers between devices: 13.2 us -> 8.99 us  [move(): return lax.ppermute(array, PAIR, pairs)]
    unnamed x15 -> x1, local copies, waits for them, and re-layouts: 4.44 us -> 0.79 us
    pallas_call x1 -> x2, Pallas kernels: 1.6 us -> 2.14 us  [the longest x1 1.27 us: small_body(): pl.pallas_call(load_kernel, out_shape=[pltpu.VMEM((tokens // parts, width...]
    ppermute x10 -> x14, starting transfers between devices: 14.1 us -> 13.6 us  [move(): return lax.ppermute(array, PAIR, pairs)]
    pallas_call x4 -> x3, Pallas kernels: 2.31 us -> 2.46 us  [kernel_call(): pl.pallas_call(kernel, out_shape=outs, in_specs=[VMEM] * len(operands), o...]
  transfers between devices with their start and end apart: 10 -> 14, of which waited for: 7 -> 5; matrix products, arithmetic and copies ran while one was open for 2% -> 3% of each run, Pallas kernels for 0% -> 4%
where the time goes in v2:
time: 28.9 us; the launch traced here: 28.7 us
  starting transfers between devices  13.6 us (47%)
  waiting for transfers between devices  8.99 us (31%)
  Pallas kernels  4.61 us (16%)
  local copies, waits for them, and re-layouts  0.79 us (3%)
  between operations  0.7 us (2%)
    ppermute x14, starting transfers between devices, move(): return lax.ppermute(array, PAIR, pairs)  13.6 us
    ppermute x14, waiting for transfers between devices, move(): return lax.ppermute(array, PAIR, pairs)  8.99 us
    pallas_call x3, Pallas kernels, kernel_call(): pl.pallas_call(kernel, out_shape=outs, in_specs=[VMEM] * len(operands), o...  2.46 us
    pallas_call x1, Pallas kernels, small_body(): pl.pallas_call(load_kernel, out_shape=[pltpu.VMEM((tokens // parts, width...  1.27 us
    pallas_call x1, Pallas kernels, small_body(): pl.pallas_call(pack_kernel, out_shape=[pltpu.VMEM((STRIP, 2 * strips * wi...  0.87 us
    unnamed x1, local copies, waits for them, and re-layouts  0.79 us
  transfers between devices with their start and end apart: 14, of which 5 were waited for; matrix products, arithmetic and copies ran while one was open for 3% of the time, Pallas kernels for 4%

profile of v2, /device:TPU:0, one launch (start us, length us, event | category | flops | bytes accessed | tf_op | source)
XLA Modules:
  0.0 28.7 jit_solution(1571744444533757063)
XLA Ops:
  0.6 0.9 %shard_map.94 = (bf16[16,4224]{1,0:T(8,128)(2,1)S(1)}, bf16[16,2176]{1,0:T(8,128)(2,1)S(1)}) custom-call(bf16[32,1024]{1,0:T(8,128)(2,1)} %enc.1, bf16[32,1024]{1,0:T(8,128)(2,1)} %dec.1, bf16[32]{0:T(256)(128)(2,1)} %bias.1), custom_call_target="tpu_custom_call" | custom-call | tf_op jit(solution)/shard_map/pallas_call | solution.py:214
  1.5 3.1 %collective-permute-start = (bf16[16,2176]{1,0:T(8,128)(2,1)S(1)}, bf16[16,2176]{1,0:T(8,128)(2,1)S(1)}, u32[]{:S(2)}, u32[]{:S(2)}) collective-permute-start(bf16[16,2176]{1,0:T(8,128)(2,1)S(1)} %get-tuple-element.21), channel_id=1, source_target_pairs={{0,4},{1,5},{2,6},{3,7},{4,0},{5,1},{6,2},{7,3},{8,12},{9,13},{10,... | collective-permute-start | bytes 208904 | tf_op jit(solution)/shard_map/ppermute | solution.py:43
  4.6 2.5 %collective-permute-start.2 = (bf16[16,4224]{1,0:T(8,128)(2,1)S(1)}, bf16[16,4224]{1,0:T(8,128)(2,1)S(1)}, u32[]{:S(2)}, u32[]{:S(2)}) collective-permute-start(bf16[16,4224]{1,0:T(8,128)(2,1)S(1)} %get-tuple-element.23.own), channel_id=1, source_target_pairs={{0,12},{1,9},{2,14},{3,11},{4,8},{5,13},{6,10},{7,15},{8,4},{9,1},... | collective-permute-start | bytes 405512 | tf_op jit(solution)/shard_map/ppermute | solution.py:43
  7.1 0.0 collective-permute-done.after.one
  7.1 0.0 collective-permute-start.1
  7.1 1.3 %shard_map.95 = (bf16[128,1024]{1,0:T(8,128)(2,1)S(1)}, bf16[128,1024]{1,0:T(8,128)(2,1)S(1)}, bf16[128,1024]{1,0:T(8,128)(2,1)S(1)}, bf16[128,1024]{1,0:T(8,128...) custom-call(bf16[256,1024]{1,0:T(8,128)(2,1)} %inputs.1, bf16[256,1024]{1,0:T(8,128)(2,1)} %targets.1, ...), custom_call_target="tpu_custom_call" | custom-call | bytes 1048576 | tf_op jit(solution)/shard_map/pallas_call | solution.py:227
  8.4 0.6 %collective-permute-start.8 = (s32[256,128]{1,0:T(8,128)S(1)}, s32[256,128]{1,0:T(8,128)S(1)}, u32[]{:S(2)}, u32[]{:S(2)}) collective-permute-start(s32[256,128]{1,0:T(8,128)S(1)} %get-tuple-element.28.refs_4_), channel_id=1, source_target_pairs={{0,1},{1,0},{2,3},{3,2},{4,5},{5,4},{6,7},{7,6},{8,9},{9,8},{10,11... | collective-permute-start | bytes 393224 | tf_op jit(solution)/shard_map/ppermute | solution.py:43
  8.9 0.1 collective-permute-start.4
  9.0 0.4 %collective-permute-start.5 = (bf16[128,1024]{1,0:T(8,128)(2,1)S(1)}, bf16[128,1024]{1,0:T(8,128)(2,1)S(1)}, u32[]{:S(2)}, u32[]{:S(2)}) collective-permute-start(bf16[128,1024]{1,0:T(8,128)(2,1)S(1)} %get-tuple-element.25.refs_1_), channel_id=1, source_target_pairs={{0,1},{1,0},{2,3},{3,2},{4,5},{5,4},{6,7},{7,6},{8,9},{9,8},{10,11... | collective-permute-start | bytes 786440 | tf_op jit(solution)/shard_map/ppermute | solution.py:43
  9.4 2.4 %collective-permute-done.2.far = bf16[16,4224]{1,0:T(8,128)(2,1)S(1)} collective-permute-done((bf16[16,4224]{1,0:T(8,128)(2,1)S(1)}, bf16[16,4224]{1,0:T(8,128)(2,1)S(1)}, u32[]{:S(2)}, u32[]{:S(2)}) %collective-permute-start.2) | collective-permute-done | bytes 135200 | tf_op jit(solution)/shard_map/ppermute | solution.py:43
  11.9 0.7 %collective-permute-start.6 = (bf16[128,1024]{1,0:T(8,128)(2,1)S(1)}, bf16[128,1024]{1,0:T(8,128)(2,1)S(1)}, u32[]{:S(2)}, u32[]{:S(2)}) collective-permute-start(bf16[128,1024]{1,0:T(8,128)(2,1)S(1)} %get-tuple-element.26.refs_2_), channel_id=1, source_target_pairs={{0,1},{1,0},{2,3},{3,2},{4,5},{5,4},{6,7},{7,6},{8,9},{9,8},{10,11... | collective-permute-start | bytes 786440 | tf_op jit(solution)/shard_map/ppermute | solution.py:43
  12.6 0.0 collective-permute-done.1.one_other
  12.6 0.0 collective-permute-start.7
  12.6 0.0 collective-permute-done.8.refs_9_
  12.6 0.5 %collective-permute-start.3 = (bf16[16,4224]{1,0:T(8,128)(2,1)S(1)}, bf16[16,4224]{1,0:T(8,128)(2,1)S(1)}, u32[]{:S(2)}, u32[]{:S(2)}) collective-permute-start(bf16[16,4224]{1,0:T(8,128)(2,1)S(1)} %collective-permute-done.2.far), channel_id=1, source_target_pairs={{0,1},{1,0},{2,3},{3,2},{4,5},{5,4},{6,7},{7,6},{8,9},{9,8},{10,11... | collective-permute-start | bytes 405512 | tf_op jit(solution)/shard_map/ppermute | solution.py:43
  13.1 1.2 %collective-permute-done.3.far_other = bf16[16,4224]{1,0:T(8,128)(2,1)S(1)} collective-permute-done((bf16[16,4224]{1,0:T(8,128)(2,1)S(1)}, bf16[16,4224]{1,0:T(8,128)(2,1)S(1)}, u32[]{:S(2)}, u32[]{:S(2)}) %collective-permute-start.3) | collective-permute-done | bytes 135200 | tf_op jit(solution)/shard_map/ppermute | solution.py:43
  14.3 0.0 collective-permute-done.4.refs_5_
  14.3 0.0 collective-permute-done.5.refs_6_
  14.3 0.0 collective-permute-done.6.refs_7_
  14.3 0.0 collective-permute-done.7.refs_8_
  14.3 1.8 %shard_map.96 = (bf16[256,1024]{1,0:T(8,128)(2,1)S(1)}, bf16[64,512]{1,0:T(8,128)(2,1)S(1)}, bf16[64,512]{1,0:T(8,128)(2,1)S(1)}, bf16[64,512]{1,0:T(8,128)(2,1)...) custom-call(f32[1024]{0:T(1024)S(1)} %get-tuple-element.22.dec_bias, ...), custom_call_target="tpu_custom_call" | custom-call | flops 536870912 | tf_op jit(solution)/shard_map/pallas_call | solution.py:25
  16.1 2.5 %collective-permute-start.9 = (bf16[64,512]{1,0:T(8,128)(2,1)S(1)}, bf16[64,512]{1,0:T(8,128)(2,1)S(1)}, u32[]{:S(2)}, u32[]{:S(2)}) collective-permute-start(bf16[64,512]{1,0:T(8,128)(2,1)S(1)} %get-tuple-element.30), channel_id=1, source_target_pairs={{0,12},{1,15},{2,14},{3,13},{4,8},{5,11},{6,10},{7,9},{8,4},{9,7},... | collective-permute-start | bytes 196616 | tf_op jit(solution)/shard_map/ppermute | solution.py:43
  18.6 0.9 %collective-permute-start.10 = (bf16[64,512]{1,0:T(8,128)(2,1)S(1)}, bf16[64,512]{1,0:T(8,128)(2,1)S(1)}, u32[]{:S(2)}, u32[]{:S(2)}) collective-permute-start(bf16[64,512]{1,0:T(8,128)(2,1)S(1)} %get-tuple-element.31), channel_id=1, source_target_pairs={{0,8},{1,11},{2,10},{3,9},{4,12},{5,15},{6,14},{7,13},{8,0},{9,3},... | collective-permute-start | bytes 196616 | tf_op jit(solution)/shard_map/ppermute | solution.py:43
  19.5 1.1 %collective-permute-start.11 = (bf16[64,512]{1,0:T(8,128)(2,1)S(1)}, bf16[64,512]{1,0:T(8,128)(2,1)S(1)}, u32[]{:S(2)}, u32[]{:S(2)}) collective-permute-start(bf16[64,512]{1,0:T(8,128)(2,1)S(1)} %get-tuple-element.32), channel_id=1, source_target_pairs={{0,4},{1,7},{2,6},{3,5},{4,0},{5,3},{6,2},{7,1},{8,12},{9,15},{10,... | collective-permute-start | bytes 196616 | tf_op jit(solution)/shard_map/ppermute | solution.py:43
  20.6 0.7 %collective-permute-start.12 = (bf16[64,512]{1,0:T(8,128)(2,1)S(1)}, bf16[64,512]{1,0:T(8,128)(2,1)S(1)}, u32[]{:S(2)}, u32[]{:S(2)}) collective-permute-start(bf16[64,512]{1,0:T(8,128)(2,1)S(1)} %get-tuple-element.33), channel_id=1, source_target_pairs={{1,3},{3,1},{5,7},{7,5},{9,11},{11,9},{13,15},{15,13},{17,19},{19,... | collective-permute-start | bytes 196616 | tf_op jit(solution)/shard_map/ppermute | solution.py:43
  21.2 1.5 %collective-permute-done.9.refs_0_ = bf16[64,512]{1,0:T(8,128)(2,1)S(1)} collective-permute-done((bf16[64,512]{1,0:T(8,128)(2,1)S(1)}, bf16[64,512]{1,0:T(8,128)(2,1)S(1)}, u32[]{:S(2)}, u32[]{:S(2)}) %collective-permute-start.9) | collective-permute-done | bytes 65568 | tf_op jit(solution)/shard_map/ppermute | solution.py:43
  22.7 3.8 %collective-permute-done.10.refs_1_ = bf16[64,512]{1,0:T(8,128)(2,1)S(1)} collective-permute-done((bf16[64,512]{1,0:T(8,128)(2,1)S(1)}, bf16[64,512]{1,0:T(8,128)(2,1)S(1)}, u32[]{:S(2)}, u32[]{:S(2)}) %collective-permute-start.10) | collective-permute-done | bytes 65568 | tf_op jit(solution)/shard_map/ppermute | solution.py:43
  26.5 0.0 collective-permute-done.11.refs_2_
  26.5 0.0 collective-permute-done.12.refs_3_
  26.6 0.6 %collective-permute-start.13 = (bf16[64,256]{1,0:T(8,128)(2,1)S(1)}, bf16[64,256]{1,0:T(8,128)(2,1)S(1)}, u32[]{:S(2)}, u32[]{:S(2)}) collective-permute-start(bf16[64,256]{1,0:T(8,128)(2,1)S(1)} %get-tuple-element.36), channel_id=1, source_target_pairs={{0,1},{1,0},{2,3},{3,2},{4,5},{5,4},{6,7},{7,6},{8,9},{9,8},{10,11... | collective-permute-start | bytes 98312 | tf_op jit(solution)/shard_map/ppermute | solution.py:43
  27.2 0.8 %copy.10 = bf16[256,1024]{1,0:T(8,128)(2,1)} copy(bf16[256,1024]{1,0:T(8,128)(2,1)S(1)} %get-tuple-element.39) | data formatting | bytes 1048576
  28.0 0.1 collective-permute-done.13.refs_1_
  28.0 0.6 %shard_map.98 = (f32[32,256]{1,0:T(8,128)}, f32[32,256]{1,0:T(8,128)}) custom-call(f32[64,256]{1,0:T(8,128)S(1)} %get-tuple-element.35.refs_0_, bf16[64,256]{1,0:T(8,128)(2,1)S(1)} %collective-permute-done.13.refs_1_), custom_call_target="tpu_custom_call" | custom-call | tf_op jit(solution)/shard_map/pallas_call | solution.py:25
  (1 shorter events, 0.0 us)
Async XLA Ops:
  1.5 5.6 %collective-permute-start = (bf16[16,2176]{1,0:T(8,128)(2,1)S(1)}, bf16[16,2176]{1,0:T(8,128)(2,1)S(1)}, u32[]{:S(2)}, u32[]{:S(2)}) collective-permute-start(bf16[16,2176]{1,0:T(8,128)(2,1)S(1)} %get-tuple-element.21), channel_id=1, source_target_pairs={{0,4},{1,5},{2,6},{3,7},{4,0},{5,1},{6,2},{7,3},{8,12},{9,13},{10,... | collective-permute-start | bytes 208904 | tf_op jit(solution)/shard_map/ppermute | solution.py:43
  4.6 7.3 %collective-permute-start.2 = (bf16[16,4224]{1,0:T(8,128)(2,1)S(1)}, bf16[16,4224]{1,0:T(8,128)(2,1)S(1)}, u32[]{:S(2)}, u32[]{:S(2)}) collective-permute-start(bf16[16,4224]{1,0:T(8,128)(2,1)S(1)} %get-tuple-element.23.own), channel_id=1, source_target_pairs={{0,12},{1,9},{2,14},{3,11},{4,8},{5,13},{6,10},{7,15},{8,4},{9,1},... | collective-permute-start | bytes 405512 | tf_op jit(solution)/shard_map/ppermute | solution.py:43
  7.1 5.5 %collective-permute-start.1 = (bf16[16,2176]{1,0:T(8,128)(2,1)S(1)}, bf16[16,2176]{1,0:T(8,128)(2,1)S(1)}, u32[]{:S(2)}, u32[]{:S(2)}) collective-permute-start(bf16[16,2176]{1,0:T(8,128)(2,1)S(1)} %collective-permute-done.after.one), channel_id=1, source_target_pairs={{0,1},{1,0},{2,3},{3,2},{4,5},{5,4},{6,7},{7,6},{8,9},{9,8},{10,11... | collective-permute-start | bytes 208904 | tf_op jit(solution)/shard_map/ppermute | solution.py:43
  8.4 4.2 %collective-permute-start.8 = (s32[256,128]{1,0:T(8,128)S(1)}, s32[256,128]{1,0:T(8,128)S(1)}, u32[]{:S(2)}, u32[]{:S(2)}) collective-permute-start(s32[256,128]{1,0:T(8,128)S(1)} %get-tuple-element.28.refs_4_), channel_id=1, source_target_pairs={{0,1},{1,0},{2,3},{3,2},{4,5},{5,4},{6,7},{7,6},{8,9},{9,8},{10,11... | collective-permute-start | bytes 393224 | tf_op jit(solution)/shard_map/ppermute | solution.py:43
  8.9 5.4 %collective-permute-start.4 = (bf16[128,1024]{1,0:T(8,128)(2,1)S(1)}, bf16[128,1024]{1,0:T(8,128)(2,1)S(1)}, u32[]{:S(2)}, u32[]{:S(2)}) collective-permute-start(bf16[128,1024]{1,0:T(8,128)(2,1)S(1)} %get-tuple-element.24.refs_0_), channel_id=1, source_target_pairs={{0,1},{1,0},{2,3},{3,2},{4,5},{5,4},{6,7},{7,6},{8,9},{9,8},{10,11... | collective-permute-start | bytes 786440 | tf_op jit(solution)/shard_map/ppermute | solution.py:43
  9.0 5.3 %collective-permute-start.5 = (bf16[128,1024]{1,0:T(8,128)(2,1)S(1)}, bf16[128,1024]{1,0:T(8,128)(2,1)S(1)}, u32[]{:S(2)}, u32[]{:S(2)}) collective-permute-start(bf16[128,1024]{1,0:T(8,128)(2,1)S(1)} %get-tuple-element.25.refs_1_), channel_id=1, source_target_pairs={{0,1},{1,0},{2,3},{3,2},{4,5},{5,4},{6,7},{7,6},{8,9},{9,8},{10,11... | collective-permute-start | bytes 786440 | tf_op jit(solution)/shard_map/ppermute | solution.py:43
  11.9 2.5 %collective-permute-start.6 = (bf16[128,1024]{1,0:T(8,128)(2,1)S(1)}, bf16[128,1024]{1,0:T(8,128)(2,1)S(1)}, u32[]{:S(2)}, u32[]{:S(2)}) collective-permute-start(bf16[128,1024]{1,0:T(8,128)(2,1)S(1)} %get-tuple-element.26.refs_2_), channel_id=1, source_target_pairs={{0,1},{1,0},{2,3},{3,2},{4,5},{5,4},{6,7},{7,6},{8,9},{9,8},{10,11... | collective-permute-start | bytes 786440 | tf_op jit(solution)/shard_map/ppermute | solution.py:43
  12.6 1.7 %collective-permute-start.7 = (bf16[128,1024]{1,0:T(8,128)(2,1)S(1)}, bf16[128,1024]{1,0:T(8,128)(2,1)S(1)}, u32[]{:S(2)}, u32[]{:S(2)}) collective-permute-start(bf16[128,1024]{1,0:T(8,128)(2,1)S(1)} %get-tuple-element.27.refs_3_), channel_id=1, source_target_pairs={{0,1},{1,0},{2,3},{3,2},{4,5},{5,4},{6,7},{7,6},{8,9},{9,8},{10,11... | collective-permute-start | bytes 786440 | tf_op jit(solution)/shard_map/ppermute | solution.py:43
  12.6 1.7 %collective-permute-start.3 = (bf16[16,4224]{1,0:T(8,128)(2,1)S(1)}, bf16[16,4224]{1,0:T(8,128)(2,1)S(1)}, u32[]{:S(2)}, u32[]{:S(2)}) collective-permute-start(bf16[16,4224]{1,0:T(8,128)(2,1)S(1)} %collective-permute-done.2.far), channel_id=1, source_target_pairs={{0,1},{1,0},{2,3},{3,2},{4,5},{5,4},{6,7},{7,6},{8,9},{9,8},{10,11... | collective-permute-start | bytes 405512 | tf_op jit(solution)/shard_map/ppermute | solution.py:43
  16.1 6.6 %collective-permute-start.9 = (bf16[64,512]{1,0:T(8,128)(2,1)S(1)}, bf16[64,512]{1,0:T(8,128)(2,1)S(1)}, u32[]{:S(2)}, u32[]{:S(2)}) collective-permute-start(bf16[64,512]{1,0:T(8,128)(2,1)S(1)} %get-tuple-element.30), channel_id=1, source_target_pairs={{0,12},{1,15},{2,14},{3,13},{4,8},{5,11},{6,10},{7,9},{8,4},{9,7},... | collective-permute-start | bytes 196616 | tf_op jit(solution)/shard_map/ppermute | solution.py:43
  18.6 7.9 %collective-permute-start.10 = (bf16[64,512]{1,0:T(8,128)(2,1)S(1)}, bf16[64,512]{1,0:T(8,128)(2,1)S(1)}, u32[]{:S(2)}, u32[]{:S(2)}) collective-permute-start(bf16[64,512]{1,0:T(8,128)(2,1)S(1)} %get-tuple-element.31), channel_id=1, source_target_pairs={{0,8},{1,11},{2,10},{3,9},{4,12},{5,15},{6,14},{7,13},{8,0},{9,3},... | collective-permute-start | bytes 196616 | tf_op jit(solution)/shard_map/ppermute | solution.py:43
  19.5 7.1 %collective-permute-start.11 = (bf16[64,512]{1,0:T(8,128)(2,1)S(1)}, bf16[64,512]{1,0:T(8,128)(2,1)S(1)}, u32[]{:S(2)}, u32[]{:S(2)}) collective-permute-start(bf16[64,512]{1,0:T(8,128)(2,1)S(1)} %get-tuple-element.32), channel_id=1, source_target_pairs={{0,4},{1,7},{2,6},{3,5},{4,0},{5,3},{6,2},{7,1},{8,12},{9,15},{10,... | collective-permute-start | bytes 196616 | tf_op jit(solution)/shard_map/ppermute | solution.py:43
  20.6 5.9 %collective-permute-start.12 = (bf16[64,512]{1,0:T(8,128)(2,1)S(1)}, bf16[64,512]{1,0:T(8,128)(2,1)S(1)}, u32[]{:S(2)}, u32[]{:S(2)}) collective-permute-start(bf16[64,512]{1,0:T(8,128)(2,1)S(1)} %get-tuple-element.33), channel_id=1, source_target_pairs={{1,3},{3,1},{5,7},{7,5},{9,11},{11,9},{13,15},{15,13},{17,19},{19,... | collective-permute-start | bytes 196616 | tf_op jit(solution)/shard_map/ppermute | solution.py:43
  26.6 1.5 %collective-permute-start.13 = (bf16[64,256]{1,0:T(8,128)(2,1)S(1)}, bf16[64,256]{1,0:T(8,128)(2,1)S(1)}, u32[]{:S(2)}, u32[]{:S(2)}) collective-permute-start(bf16[64,256]{1,0:T(8,128)(2,1)S(1)} %get-tuple-element.36), channel_id=1, source_target_pairs={{0,1},{1,0},{2,3},{3,2},{4,5},{5,4},{6,7},{7,6},{8,9},{9,8},{10,11... | collective-permute-start | bytes 98312 | tf_op jit(solution)/shard_map/ppermute | solution.py:43

commit v3 on v2

--- a/solution.py
+++ b/solution.py
@@ -13,8 +13,22 @@
 PAIR = ("blk", "tok")
 STRIP = 16
 TILE = 128
-
-STEPS = (3, 2, 1, 0)
+CHUNKS = 2
+
+FAR_0, FAR_1, NEAR = ((3, 2, 1, 0), (2, 3, 0, 1), (1, 0, 3, 2))
+CORE_0 = ((2, 3, 0, 1), (3, 2, 1, 0), (1, 0, 3, 2), None)
+CORE_1 = ((2, 3, 0, 1), (3, 2, 1, 0), (1, 0, 3, 2), (0, 1, 2, 3))
+
+
+def look_up(table, index):
+    value = table[-1]
+    for i in range(len(table) - 1):
+        value = jnp.where(index == i, table[i], value)
+    return value
+
+
+def sender(table):
+    return tuple(table.index(i) for i in range(len(table)))
 
 
 def in_vmem(array):
@@ -78,34 +92,45 @@
 
 
 def load_kernel(inputs, targets, mask, dec_bias, after, *refs):
-    *outs, sems = refs
-    parts = (len(outs) - 2) // 2
-    copies = []
+    *outs, dec_bias_out, mask_ints, sems = refs
+    parts = len(outs) // 2
+    width = inputs.shape[1]
+    copies = [(mask, mask_ints), (dec_bias, dec_bias_out)]
     for i, source in enumerate((inputs, targets)):
         for j, out in enumerate(outs[i * parts : (i + 1) * parts]):
             rows = out.shape[0]
-            copies.append((source.at[pl.ds(j * rows, rows)], out))
-    copies += [(mask, outs[-2]), (dec_bias, outs[-1])]
+            copies.append((source.at[pl.ds(j * rows, rows)], out.at[:, pl.ds(0, width)]))
     copies = [pltpu.make_async_copy(*pair, sems.at[i]) for i, pair in enumerate(copies)]
     for copy in copies:
         copy.start()
-    for copy in copies:
+    copies[0].wait()
+    for j, out in enumerate(outs[parts:]):
+        rows = out.shape[0]
+        out[:, width:] = mask_ints[j * rows : (j + 1) * rows, :].astype(F32).astype(BF16)
+    for copy in copies[1:]:
         copy.wait()
+
+
+def join_kernel(far, one, out):
+    out[:, : far.shape[1]] = far[...]
+    out[:, far.shape[1] :] = one[...]
 
 
 def contract(a, b, over_a, over_b):
     return lax.dot_general(a, b, (((over_a,), (over_b,)), ((), ())), preferred_element_type=F32)
 
 
-def step_kernel(dec_bias, own, one, one_other, far, far_other, *refs):
+def step_kernel(dec_bias, own, one, far, other, *refs):
     *refs, enc_all, dec_all, error_all, enc_terms, dec_terms = refs
     *refs, own_piece = refs
-    refs, pieces = refs[: -len(STEPS)], refs[-len(STEPS) :]
+    refs, pieces = refs[: -len(CORE_1)], refs[-len(CORE_1) :]
     *refs, recon = refs
     parts = len(refs) // 4
-    width = recon.shape[1]
+    tokens, width = recon.shape
     strips = one.shape[1] // width
     rows = strips * STRIP
+    far_other = other.at[:, pl.ds(0, far.shape[1])]
+    one_other = other.at[:, pl.ds(far.shape[1], one.shape[1])]
     rank = lax.axis_index("blk")
     tok = lax.axis_index("tok")
     core = tok % 2
@@ -121,9 +146,11 @@
             to[span, :] = source[:, j * width : (j + 1) * width]
 
     def unpack(enc_half, dec_half, first, second):
-        put(enc_all, rank ^ 1, enc_half, 0)
-        put(dec_all, rank ^ 1, dec_half, 0)
-        for block, source in ((rank ^ 3, first), (rank ^ 2, second)):
+        near = look_up(sender(NEAR), rank)
+        put(enc_all, near, enc_half, 0)
+        put(dec_all, near, dec_half, 0)
+        for table, source in ((FAR_0, first), (FAR_1, second)):
+            block = look_up(sender(table), rank)
             put(enc_all, block, source, 0)
             put(dec_all, block, source, strips)
 
@@ -142,22 +169,23 @@
     base = dec_bias[...].reshape(1, width)
     half = pieces[0].shape[1]
     cols = pl.ds(pl.multiple_of((chip ^ core) * half, half), half)
-    groups = (refs[: 2 * parts + 1], refs[2 * parts + 1 :])
-    tokens = recon.shape[0]
+    groups = (refs[: 2 * parts], refs[2 * parts :])
     enc_sum, dec_sum = 0.0, 0.0
     for g, group in enumerate(groups):
-        gate_all = group[-1]
         acts, dpres = [], []
-        for j in range(parts):
-            x, target = group[j], group[parts + j]
-            n = x.shape[0]
+        n = tokens // CHUNKS
+        x_all = jnp.concatenate([part[...] for part in group[:parts]], axis=0)
+        target_all = jnp.concatenate([part[:, :width] for part in group[parts:]], axis=0)
+        gate_all = jnp.concatenate([part[:, width:] for part in group[parts:]], axis=0)
+        for j in range(CHUNKS):
             span = slice(j * n, (j + 1) * n)
-            gate = gate_all[span, :].astype(F32)
-            act = ((contract(x[...], enc_all[...], 1, 1) + bias) * gate).astype(BF16)
+            x, target = x_all[span], target_all[span]
+            gate = gate_all[span].astype(F32)
+            act = ((contract(x, enc_all[...], 1, 1) + bias) * gate).astype(BF16)
             recon_full = contract(act, dec_all[...], 1, 0) + base
             if g == 0:
                 recon[span, :] = recon_full.astype(BF16)
-            error = (recon_full - target[...].astype(F32)).astype(BF16)
+            error = (recon_full - target.astype(F32)).astype(BF16)
             error_all[g * tokens + j * n : g * tokens + (j + 1) * n, :] = error
             dpres.append((contract(error, dec_all[...], 1, 1) * gate).astype(BF16))
             acts.append(act)
@@ -168,9 +196,12 @@
         enc_sum += contract(dpre, x, 0, 0)
     enc_terms[...] = enc_sum
     dec_terms[...] = dec_sum
-    for step, piece in zip(STEPS, pieces, strict=True):
-        piece[:rows, :] = enc_terms[at(rank ^ step), :].astype(BF16)
-        piece[rows:, :] = dec_terms[at(rank ^ step), :].astype(BF16)
+    for zero, one_table, piece in zip(CORE_0, CORE_1, pieces, strict=True):
+        to = look_up(one_table, rank)
+        if zero is not None:
+            to = jnp.where(core == 0, look_up(zero, rank), to)
+        piece[:rows, :] = enc_terms[at(to), :].astype(BF16)
+        piece[rows:, :] = dec_terms[at(to), :].astype(BF16)
     own_piece[:rows, :] = enc_terms[at(rank), :]
     own_piece[rows:, :] = dec_terms[at(rank), :]
 
@@ -221,28 +252,31 @@
         out_specs=[VMEM] * 2,
         scratch_shapes=[pltpu.VMEM((rows,), BF16), pltpu.SemaphoreType.DMA((1 + 2 * strips,))],
     )(enc_weight, dec_weight, enc_bias)
-    far = move(whole, blks, toks, lambda b, t: (b ^ (3, 2)[t % 2], t))
-    one = move(half, blks, toks, lambda b, t: (b ^ 1, t))
+    far = move(whole, blks, toks, lambda b, t: ((FAR_0, FAR_1)[t % 2][b], t))
+    one = move(half, blks, toks, lambda b, t: (NEAR[b], t))
     parts = 2
     *loaded, dec_bias = pl.pallas_call(
         load_kernel,
-        out_shape=[pltpu.VMEM((tokens // parts, width), BF16)] * (2 * parts)
-        + [pltpu.VMEM(array.shape, array.dtype) for array in (mask, dec_bias)],
+        out_shape=[pltpu.VMEM((tokens // parts, width), BF16)] * parts
+        + [pltpu.VMEM((tokens // parts, width + latents), BF16)] * parts
+        + [pltpu.VMEM(dec_bias.shape, F32)],
         in_specs=[pl.BlockSpec(memory_space=pl.ANY)] * 4 + [VMEM],
-        out_specs=[VMEM] * (2 * parts + 2),
-        scratch_shapes=[pltpu.SemaphoreType.DMA((2 * parts + 2,))],
+        out_specs=[VMEM] * (2 * parts + 1),
+        scratch_shapes=[pltpu.VMEM(mask.shape, mask.dtype), pltpu.SemaphoreType.DMA((2 * parts + 2,))],
         cost_estimate=pl.CostEstimate(flops=0, bytes_accessed=4 * tokens * width, transcendentals=0),
-    )(inputs, targets, mask, dec_bias, in_vmem(one))
+    )(inputs, targets, mask, dec_bias, in_vmem(half))
     others = [swap(array) for array in loaded]
-    one_other = swap(one)
-    far_other = swap(far)
+    joined = kernel_call(
+        join_kernel, [pltpu.VMEM((STRIP, 3 * strips * width + 2 * TILE), BF16)], far, one
+    )
+    other = swap(*joined)
     piece = (2 * rows, 2 * share)
     recon, *pieces, own = kernel_call(
         step_kernel,
         [pltpu.VMEM((tokens, width), BF16)]
-        + [pltpu.VMEM(piece, BF16)] * len(STEPS)
+        + [pltpu.VMEM(piece, BF16)] * len(CORE_1)
         + [pltpu.VMEM(piece, F32)],
-        dec_bias, whole, one, one_other, far, far_other, *loaded, *others,
+        dec_bias, whole, one, far, other, *loaded, *others,
         scratch=[
             pltpu.VMEM((latents, width), BF16),
             pltpu.VMEM((latents, width), BF16),
@@ -253,10 +287,11 @@
         flops=16 * tokens * latents * width,
     )
     arrived = []
-    for step, out in zip(STEPS, pieces, strict=True):
-
-        def where(b, t, step=step):
-            return None if step == 0 and t % 2 == 0 else (b ^ step, t ^ (2 * (t % 2)))
+    for zero, one_table, out in zip(CORE_0, CORE_1, pieces, strict=True):
+
+        def where(b, t, tables=(zero, one_table)):
+            table = tables[t % 2]
+            return None if table is None else (table[b], t ^ (2 * (t % 2)))
 
         arrived.append(move(out, blks, toks, where))
     send, keep = kernel_call(

time: 28.9 us -> 27.5 us (0.952)
  starting transfers between devices: 13.6 us -> 11.5 us
  waiting for transfers between devices: 8.99 us -> 9.6 us
    ppermute x14 -> x12, starting transfers between devices: 13.6 us -> 11.5 us  [move(): return lax.ppermute(array, PAIR, pairs)]
    ppermute x14 -> x12, waiting for transfers between devices: 8.99 us -> 9.6 us  [move(): return lax.ppermute(array, PAIR, pairs)]
    pallas_call x3 -> x4, Pallas kernels: 2.46 us -> 2.5 us  [kernel_call(): pl.pallas_call(kernel, out_shape=outs, in_specs=[VMEM] * len(operands), o...]
  transfers between devices with their start and end apart: 14 -> 12, of which waited for: 5 -> 7; matrix products, arithmetic and copies ran while one was open for 3% -> 3% of each run, Pallas kernels for 4% -> 5%
where the time goes in v3:
time: 27.5 us; the launch traced here: 27.3 us
  starting transfers between devices  11.5 us (42%)
  waiting for transfers between devices  9.6 us (35%)
  Pallas kernels  4.7 us (17%)
  local copies, waits for them, and re-layouts  0.79 us (3%)
  between operations  0.7 us (3%)
    ppermute x12, starting transfers between devices, move(): return lax.ppermute(array, PAIR, pairs)  11.5 us
    ppermute x12, waiting for transfers between devices, move(): return lax.ppermute(array, PAIR, pairs)  9.6 us
    pallas_call x4, Pallas kernels, kernel_call(): pl.pallas_call(kernel, out_shape=outs, in_specs=[VMEM] * len(operands), o...  2.5 us
    pallas_call x1, Pallas kernels, small_body(): pl.pallas_call(load_kernel, out_shape=[pltpu.VMEM((tokens // parts, width...  1.32 us
    pallas_call x1, Pallas kernels, small_body(): pl.pallas_call(pack_kernel, out_shape=[pltpu.VMEM((STRIP, 2 * strips * wi...  0.87 us
    unnamed x1, local copies, waits for them, and re-layouts  0.79 us
  transfers between devices with their start and end apart: 12, of which 7 were waited for; matrix products, arithmetic and copies ran while one was open for 3% of the time, Pallas kernels for 5%

profile of v3, /device:TPU:0, one launch (start us, length us, event | category | flops | bytes accessed | tf_op | source)
XLA Modules:
  0.0 27.3 jit_solution(8802708208961877402)
XLA Ops:
  0.6 0.9 %shard_map.94 = (bf16[16,4224]{1,0:T(8,128)(2,1)S(1)}, bf16[16,2176]{1,0:T(8,128)(2,1)S(1)}) custom-call(bf16[32,1024]{1,0:T(8,128)(2,1)} %enc.1, bf16[32,1024]{1,0:T(8,128)(2,1)} %dec.1, bf16[32]{0:T(256)(128)(2,1)} %bias.1), custom_call_target="tpu_custom_call" | custom-call | tf_op jit(solution)/shard_map/pallas_call | solution.py:245
  1.5 5.1 %collective-permute-start.1 = (bf16[16,4224]{1,0:T(8,128)(2,1)S(1)}, bf16[16,4224]{1,0:T(8,128)(2,1)S(1)}, u32[]{:S(2)}, u32[]{:S(2)}) collective-permute-start(bf16[16,4224]{1,0:T(8,128)(2,1)S(1)} %get-tuple-element.22.own), channel_id=1, source_target_pairs={{0,12},{1,9},{2,14},{3,11},{4,8},{5,13},{6,10},{7,15},{8,4},{9,1},... | collective-permute-start | bytes 405512 | tf_op jit(solution)/shard_map/ppermute | solution.py:57
  6.6 0.0 collective-permute-start
  6.6 1.3 %shard_map.95 = (bf16[128,1024]{1,0:T(8,128)(2,1)S(1)}, bf16[128,1024]{1,0:T(8,128)(2,1)S(1)}, bf16[128,1152]{1,0:T(8,128)(2,1)S(1)}, bf16[128,1152]{1,0:T(8,128)(2,1)S(1)}, f32[1024]{0:T(1024)S(1)}) custom-call(bf16[256,1024]{1,0:T(8,128)(2,1)} %inputs.1, bf16[256,1024]{1,0:T(8,128)(2,1)} %targets.1, s32[256,128]{1,0:T(8,128)} %mask.1, f32[1024]{0:T(1024)} %dec_bias.1, ...), custom_call_target="tpu_custom_call" | custom-call | bytes 1048576 | tf_op jit(solution)/shard_map/pallas_call | solution.py:258
  8.0 0.1 collective-permute-start.5
  8.0 0.5 %collective-permute-start.6 = (bf16[128,1152]{1,0:T(8,128)(2,1)S(1)}, bf16[128,1152]{1,0:T(8,128)(2,1)S(1)}, u32[]{:S(2)}, u32[]{:S(2)}) collective-permute-start(bf16[128,1152]{1,0:T(8,128)(2,1)S(1)} %get-tuple-element.26.refs_3_), channel_id=1, source_target_pairs={{0,1},{1,0},{2,3},{3,2},{4,5},{5,4},{6,7},{7,6},{8,9},{9,8},{10,11... | collective-permute-start | bytes 884744 | tf_op jit(solution)/shard_map/ppermute | solution.py:57
  8.5 0.1 collective-permute-start.3
  8.6 2.9 %collective-permute-done.one = bf16[16,2176]{1,0:T(8,128)(2,1)S(1)} collective-permute-done((bf16[16,2176]{1,0:T(8,128)(2,1)S(1)}, bf16[16,2176]{1,0:T(8,128)(2,1)S(1)}, u32[]{:S(2)}, u32[]{:S(2)}) %collective-permute-start) | collective-permute-done | bytes 69664 | tf_op jit(solution)/shard_map/ppermute | solution.py:57
  11.5 0.0 collective-permute-start.4
  11.5 0.0 collective-permute-done.1.far
  11.5 0.6 %collective-permute-start.2 = (bf16[16,6400]{1,0:T(8,128)(2,1)S(1)}, bf16[16,6400]{1,0:T(8,128)(2,1)S(1)}, u32[]{:S(2)}, u32[]{:S(2)}) collective-permute-start(bf16[16,6400]{1,0:T(8,128)(2,1)S(1)} %shard_map.96), channel_id=1, source_target_pairs={{0,1},{1,0},{2,3},{3,2},{4,5},{5,4},{6,7},{7,6},{8,9},{9,8},{10,11... | collective-permute-start | bytes 614408 | tf_op jit(solution)/shard_map/ppermute | solution.py:57
  12.1 0.0 collective-permute-done.3.refs_4_
  12.1 0.9 %collective-permute-done.4.refs_5_ = bf16[128,1024]{1,0:T(8,128)(2,1)S(1)} collective-permute-done((bf16[128,1024]{1,0:T(8,128)(2,1)S(1)}, bf16[128,1024]{1,0:T(8,128)(2,1)S(1)}, u32[]{:S(2)}, u32[]{:S(2)}) %collective-permute-start.4) | collective-permute-done | bytes 262176 | tf_op jit(solution)/shard_map/ppermute | solution.py:57
  13.0 0.0 collective-permute-done.5.refs_6_
  13.1 0.0 collective-permute-done.6.refs_7_
  13.1 0.3 %collective-permute-done.2.other = bf16[16,6400]{1,0:T(8,128)(2,1)S(1)} collective-permute-done((bf16[16,6400]{1,0:T(8,128)(2,1)S(1)}, bf16[16,6400]{1,0:T(8,128)(2,1)S(1)}, u32[]{:S(2)}, u32[]{:S(2)}) %collective-permute-start.2) | collective-permute-done | bytes 204832 | tf_op jit(solution)/shard_map/ppermute | solution.py:57
  13.3 1.8 %shard_map.97 = (bf16[256,1024]{1,0:T(8,128)(2,1)S(1)}, bf16[64,512]{1,0:T(8,128)(2,1)S(1)}, bf16[64,512]{1,0:T(8,128)(2,1)S(1)}, bf16[64,512]{1,0:T(8,128)(2,1)...) custom-call(f32[1024]{0:T(1024)S(1)} %get-tuple-element.21.dec_bias, ...), custom_call_target="tpu_custom_call" | custom-call | flops 536870912 | tf_op jit(solution)/shard_map/pallas_call | solution.py:39
  15.2 3.0 %collective-permute-start.7 = (bf16[64,512]{1,0:T(8,128)(2,1)S(1)}, bf16[64,512]{1,0:T(8,128)(2,1)S(1)}, u32[]{:S(2)}, u32[]{:S(2)}) collective-permute-start(bf16[64,512]{1,0:T(8,128)(2,1)S(1)} %get-tuple-element.28), channel_id=1, source_target_pairs={{0,8},{1,11},{2,10},{3,9},{4,12},{5,15},{6,14},{7,13},{8,0},{9,3},... | collective-permute-start | bytes 196616 | tf_op jit(solution)/shard_map/ppermute | solution.py:57
  18.2 0.4 %collective-permute-start.8 = (bf16[64,512]{1,0:T(8,128)(2,1)S(1)}, bf16[64,512]{1,0:T(8,128)(2,1)S(1)}, u32[]{:S(2)}, u32[]{:S(2)}) collective-permute-start(bf16[64,512]{1,0:T(8,128)(2,1)S(1)} %get-tuple-element.29), channel_id=1, source_target_pairs={{0,12},{1,15},{2,14},{3,13},{4,8},{5,11},{6,10},{7,9},{8,4},{9,7},... | collective-permute-start | bytes 196616 | tf_op jit(solution)/shard_map/ppermute | solution.py:57
  18.6 0.5 %collective-permute-start.9 = (bf16[64,512]{1,0:T(8,128)(2,1)S(1)}, bf16[64,512]{1,0:T(8,128)(2,1)S(1)}, u32[]{:S(2)}, u32[]{:S(2)}) collective-permute-start(bf16[64,512]{1,0:T(8,128)(2,1)S(1)} %get-tuple-element.30), channel_id=1, source_target_pairs={{0,4},{1,7},{2,6},{3,5},{4,0},{5,3},{6,2},{7,1},{8,12},{9,15},{10,... | collective-permute-start | bytes 196616 | tf_op jit(solution)/shard_map/ppermute | solution.py:57
  19.1 0.7 %collective-permute-start.10 = (bf16[64,512]{1,0:T(8,128)(2,1)S(1)}, bf16[64,512]{1,0:T(8,128)(2,1)S(1)}, u32[]{:S(2)}, u32[]{:S(2)}) collective-permute-start(bf16[64,512]{1,0:T(8,128)(2,1)S(1)} %get-tuple-element.31), channel_id=1, source_target_pairs={{1,3},{3,1},{5,7},{7,5},{9,11},{11,9},{13,15},{15,13},{17,19},{19,... | collective-permute-start | bytes 196616 | tf_op jit(solution)/shard_map/ppermute | solution.py:57
  19.7 2.5 %collective-permute-done.7.refs_0_ = bf16[64,512]{1,0:T(8,128)(2,1)S(1)} collective-permute-done((bf16[64,512]{1,0:T(8,128)(2,1)S(1)}, bf16[64,512]{1,0:T(8,128)(2,1)S(1)}, u32[]{:S(2)}, u32[]{:S(2)}) %collective-permute-start.7) | collective-permute-done | bytes 65568 | tf_op jit(solution)/shard_map/ppermute | solution.py:57
  22.2 2.7 %collective-permute-done.8.refs_1_ = bf16[64,512]{1,0:T(8,128)(2,1)S(1)} collective-permute-done((bf16[64,512]{1,0:T(8,128)(2,1)S(1)}, bf16[64,512]{1,0:T(8,128)(2,1)S(1)}, u32[]{:S(2)}, u32[]{:S(2)}) %collective-permute-start.8) | collective-permute-done | bytes 65568 | tf_op jit(solution)/shard_map/ppermute | solution.py:57
  25.0 0.2 collective-permute-done.9.refs_2_
  25.1 0.0 collective-permute-done.10.refs_3_
  25.2 0.6 %collective-permute-start.11 = (bf16[64,256]{1,0:T(8,128)(2,1)S(1)}, bf16[64,256]{1,0:T(8,128)(2,1)S(1)}, u32[]{:S(2)}, u32[]{:S(2)}) collective-permute-start(bf16[64,256]{1,0:T(8,128)(2,1)S(1)} %get-tuple-element.34), channel_id=1, source_target_pairs={{0,1},{1,0},{2,3},{3,2},{4,5},{5,4},{6,7},{7,6},{8,9},{9,8},{10,11... | collective-permute-start | bytes 98312 | tf_op jit(solution)/shard_map/ppermute | solution.py:57
  25.8 0.8 %copy.10 = bf16[256,1024]{1,0:T(8,128)(2,1)} copy(bf16[256,1024]{1,0:T(8,128)(2,1)S(1)} %get-tuple-element.37) | data formatting | bytes 1048576
  26.6 0.1 collective-permute-done.11.refs_1_
  26.6 0.6 %shard_map.99 = (f32[32,256]{1,0:T(8,128)}, f32[32,256]{1,0:T(8,128)}) custom-call(f32[64,256]{1,0:T(8,128)S(1)} %get-tuple-element.33.refs_0_, bf16[64,256]{1,0:T(8,128)(2,1)S(1)} %collective-permute-done.11.refs_1_), custom_call_target="tpu_custom_call" | custom-call | tf_op jit(solution)/shard_map/pallas_call | solution.py:39
  (2 shorter events, 0.1 us)
Async XLA Ops:
  1.5 10.0 %collective-permute-start.1 = (bf16[16,4224]{1,0:T(8,128)(2,1)S(1)}, bf16[16,4224]{1,0:T(8,128)(2,1)S(1)}, u32[]{:S(2)}, u32[]{:S(2)}) collective-permute-start(bf16[16,4224]{1,0:T(8,128)(2,1)S(1)} %get-tuple-element.22.own), channel_id=1, source_target_pairs={{0,12},{1,9},{2,14},{3,11},{4,8},{5,13},{6,10},{7,15},{8,4},{9,1},... | collective-permute-start | bytes 405512 | tf_op jit(solution)/shard_map/ppermute | solution.py:57
  6.6 4.9 %collective-permute-start = (bf16[16,2176]{1,0:T(8,128)(2,1)S(1)}, bf16[16,2176]{1,0:T(8,128)(2,1)S(1)}, u32[]{:S(2)}, u32[]{:S(2)}) collective-permute-start(bf16[16,2176]{1,0:T(8,128)(2,1)S(1)} %get-tuple-element.20.after), channel_id=1, source_target_pairs={{0,4},{1,5},{2,6},{3,7},{4,0},{5,1},{6,2},{7,3},{8,12},{9,13},{10,... | collective-permute-start | bytes 208904 | tf_op jit(solution)/shard_map/ppermute | solution.py:57
  8.0 5.1 %collective-permute-start.5 = (bf16[128,1152]{1,0:T(8,128)(2,1)S(1)}, bf16[128,1152]{1,0:T(8,128)(2,1)S(1)}, u32[]{:S(2)}, u32[]{:S(2)}) collective-permute-start(bf16[128,1152]{1,0:T(8,128)(2,1)S(1)} %get-tuple-element.25.refs_2_), channel_id=1, source_target_pairs={{0,1},{1,0},{2,3},{3,2},{4,5},{5,4},{6,7},{7,6},{8,9},{9,8},{10,11... | collective-permute-start | bytes 884744 | tf_op jit(solution)/shard_map/ppermute | solution.py:57
  8.0 5.0 %collective-permute-start.6 = (bf16[128,1152]{1,0:T(8,128)(2,1)S(1)}, bf16[128,1152]{1,0:T(8,128)(2,1)S(1)}, u32[]{:S(2)}, u32[]{:S(2)}) collective-permute-start(bf16[128,1152]{1,0:T(8,128)(2,1)S(1)} %get-tuple-element.26.refs_3_), channel_id=1, source_target_pairs={{0,1},{1,0},{2,3},{3,2},{4,5},{5,4},{6,7},{7,6},{8,9},{9,8},{10,11... | collective-permute-start | bytes 884744 | tf_op jit(solution)/shard_map/ppermute | solution.py:57
  8.5 3.6 %collective-permute-start.3 = (bf16[128,1024]{1,0:T(8,128)(2,1)S(1)}, bf16[128,1024]{1,0:T(8,128)(2,1)S(1)}, u32[]{:S(2)}, u32[]{:S(2)}) collective-permute-start(bf16[128,1024]{1,0:T(8,128)(2,1)S(1)} %get-tuple-element.23.refs_0_), channel_id=1, source_target_pairs={{0,1},{1,0},{2,3},{3,2},{4,5},{5,4},{6,7},{7,6},{8,9},{9,8},{10,11... | collective-permute-start | bytes 786440 | tf_op jit(solution)/shard_map/ppermute | solution.py:57
  11.5 1.5 %collective-permute-start.4 = (bf16[128,1024]{1,0:T(8,128)(2,1)S(1)}, bf16[128,1024]{1,0:T(8,128)(2,1)S(1)}, u32[]{:S(2)}, u32[]{:S(2)}) collective-permute-start(bf16[128,1024]{1,0:T(8,128)(2,1)S(1)} %get-tuple-element.24.refs_1_), channel_id=1, source_target_pairs={{0,1},{1,0},{2,3},{3,2},{4,5},{5,4},{6,7},{7,6},{8,9},{9,8},{10,11... | collective-permute-start | bytes 786440 | tf_op jit(solution)/shard_map/ppermute | solution.py:57
  11.5 1.8 %collective-permute-start.2 = (bf16[16,6400]{1,0:T(8,128)(2,1)S(1)}, bf16[16,6400]{1,0:T(8,128)(2,1)S(1)}, u32[]{:S(2)}, u32[]{:S(2)}) collective-permute-start(bf16[16,6400]{1,0:T(8,128)(2,1)S(1)} %shard_map.96), channel_id=1, source_target_pairs={{0,1},{1,0},{2,3},{3,2},{4,5},{5,4},{6,7},{7,6},{8,9},{9,8},{10,11... | collective-permute-start | bytes 614408 | tf_op jit(solution)/shard_map/ppermute | solution.py:57
  15.2 7.1 %collective-permute-start.7 = (bf16[64,512]{1,0:T(8,128)(2,1)S(1)}, bf16[64,512]{1,0:T(8,128)(2,1)S(1)}, u32[]{:S(2)}, u32[]{:S(2)}) collective-permute-start(bf16[64,512]{1,0:T(8,128)(2,1)S(1)} %get-tuple-element.28), channel_id=1, source_target_pairs={{0,8},{1,11},{2,10},{3,9},{4,12},{5,15},{6,14},{7,13},{8,0},{9,3},... | collective-permute-start | bytes 196616 | tf_op jit(solution)/shard_map/ppermute | solution.py:57
  18.2 6.8 %collective-permute-start.8 = (bf16[64,512]{1,0:T(8,128)(2,1)S(1)}, bf16[64,512]{1,0:T(8,128)(2,1)S(1)}, u32[]{:S(2)}, u32[]{:S(2)}) collective-permute-start(bf16[64,512]{1,0:T(8,128)(2,1)S(1)} %get-tuple-element.29), channel_id=1, source_target_pairs={{0,12},{1,15},{2,14},{3,13},{4,8},{5,11},{6,10},{7,9},{8,4},{9,7},... | collective-permute-start | bytes 196616 | tf_op jit(solution)/shard_map/ppermute | solution.py:57
  18.6 6.5 %collective-permute-start.9 = (bf16[64,512]{1,0:T(8,128)(2,1)S(1)}, bf16[64,512]{1,0:T(8,128)(2,1)S(1)}, u32[]{:S(2)}, u32[]{:S(2)}) collective-permute-start(bf16[64,512]{1,0:T(8,128)(2,1)S(1)} %get-tuple-element.30), channel_id=1, source_target_pairs={{0,4},{1,7},{2,6},{3,5},{4,0},{5,3},{6,2},{7,1},{8,12},{9,15},{10,... | collective-permute-start | bytes 196616 | tf_op jit(solution)/shard_map/ppermute | solution.py:57
  19.1 6.1 %collective-permute-start.10 = (bf16[64,512]{1,0:T(8,128)(2,1)S(1)}, bf16[64,512]{1,0:T(8,128)(2,1)S(1)}, u32[]{:S(2)}, u32[]{:S(2)}) collective-permute-start(bf16[64,512]{1,0:T(8,128)(2,1)S(1)} %get-tuple-element.31), channel_id=1, source_target_pairs={{1,3},{3,1},{5,7},{7,5},{9,11},{11,9},{13,15},{15,13},{17,19},{19,... | collective-permute-start | bytes 196616 | tf_op jit(solution)/shard_map/ppermute | solution.py:57
  25.2 1.5 %collective-permute-start.11 = (bf16[64,256]{1,0:T(8,128)(2,1)S(1)}, bf16[64,256]{1,0:T(8,128)(2,1)S(1)}, u32[]{:S(2)}, u32[]{:S(2)}) collective-permute-start(bf16[64,256]{1,0:T(8,128)(2,1)S(1)} %get-tuple-element.34), channel_id=1, source_target_pairs={{0,1},{1,0},{2,3},{3,2},{4,5},{5,4},{6,7},{7,6},{8,9},{9,8},{10,11... | collective-permute-start | bytes 98312 | tf_op jit(solution)/shard_map/ppermute | solution.py:57

commit v4 on v3

--- a/solution.py
+++ b/solution.py
@@ -13,7 +13,6 @@
 PAIR = ("blk", "tok")
 STRIP = 16
 TILE = 128
-CHUNKS = 2
 
 FAR_0, FAR_1, NEAR = ((3, 2, 1, 0), (2, 3, 0, 1), (1, 0, 3, 2))
 CORE_0 = ((2, 3, 0, 1), (3, 2, 1, 0), (1, 0, 3, 2), None)
@@ -106,7 +105,7 @@
     copies[0].wait()
     for j, out in enumerate(outs[parts:]):
         rows = out.shape[0]
-        out[:, width:] = mask_ints[j * rows : (j + 1) * rows, :].astype(F32).astype(BF16)
+        out[:, width:] = mask_ints[j * rows : (j + 1) * rows, :].astype(F32).T.astype(BF16)
     for copy in copies[1:]:
         copy.wait()
 
@@ -121,12 +120,12 @@
 
 
 def step_kernel(dec_bias, own, one, far, other, *refs):
-    *refs, enc_all, dec_all, error_all, enc_terms, dec_terms = refs
+    *refs, enc_all, dec_all, error_all, act_all, dpre_all, inputs_all, enc_terms, dec_terms = refs
     *refs, own_piece = refs
     refs, pieces = refs[: -len(CORE_1)], refs[-len(CORE_1) :]
     *refs, recon = refs
     parts = len(refs) // 4
-    tokens, width = recon.shape
+    width = recon.shape[1]
     strips = one.shape[1] // width
     rows = strips * STRIP
     far_other = other.at[:, pl.ds(0, far.shape[1])]
@@ -166,36 +165,40 @@
         unpack(one_other, one, far_other, far)
 
     bias = sum(source[:, -TILE:].astype(F32) for source in (own, one, far, far_other))[0:1, :]
+    bias_col = jnp.broadcast_to(bias, (TILE, TILE)).T
     base = dec_bias[...].reshape(1, width)
     half = pieces[0].shape[1]
     cols = pl.ds(pl.multiple_of((chip ^ core) * half, half), half)
-    groups = (refs[: 2 * parts], refs[2 * parts :])
-    enc_sum, dec_sum = 0.0, 0.0
-    for g, group in enumerate(groups):
-        acts, dpres = [], []
-        n = tokens // CHUNKS
-        x_all = jnp.concatenate([part[...] for part in group[:parts]], axis=0)
-        target_all = jnp.concatenate([part[:, :width] for part in group[parts:]], axis=0)
-        gate_all = jnp.concatenate([part[:, width:] for part in group[parts:]], axis=0)
-        for j in range(CHUNKS):
-            span = slice(j * n, (j + 1) * n)
-            x, target = x_all[span], target_all[span]
-            gate = gate_all[span].astype(F32)
-            act = ((contract(x, enc_all[...], 1, 1) + bias) * gate).astype(BF16)
-            recon_full = contract(act, dec_all[...], 1, 0) + base
-            if g == 0:
-                recon[span, :] = recon_full.astype(BF16)
-            error = (recon_full - target.astype(F32)).astype(BF16)
-            error_all[g * tokens + j * n : g * tokens + (j + 1) * n, :] = error
-            dpres.append((contract(error, dec_all[...], 1, 1) * gate).astype(BF16))
-            acts.append(act)
-        act = jnp.concatenate(acts, axis=0)
-        dpre = jnp.concatenate(dpres, axis=0)
-        x = jnp.concatenate([part[:, cols] for part in group[:parts]], axis=0)
-        dec_sum += contract(act, error_all[g * tokens : (g + 1) * tokens, cols], 0, 0)
-        enc_sum += contract(dpre, x, 0, 0)
-    enc_terms[...] = enc_sum
-    dec_terms[...] = dec_sum
+    chunks = []
+    for group in (refs[: 2 * parts], refs[2 * parts :]):
+        chunks += list(zip(group[:parts], group[parts:], strict=True))
+    n = chunks[0][0].shape[0]
+    merge = 512 // n
+    for i in range(0, len(chunks), merge):
+        span = slice(i * n, (i + merge) * n)
+        some = chunks[i : i + merge]
+
+        def stack(values):
+            return values[0] if len(values) == 1 else jnp.concatenate(values, axis=0)
+
+        x = stack([part[:, :width] for part, _ in some])
+        target = stack([part[:, :width] for _, part in some]).astype(F32)
+        gate = [part[:, width:] for _, part in some]
+        gate = (gate[0] if len(gate) == 1 else jnp.concatenate(gate, axis=1)).astype(F32)
+        pre = contract(enc_all[...], x, 1, 1)
+        bias_cols = jnp.concatenate([bias_col] * (pre.shape[1] // TILE), axis=1)
+        act = ((pre + bias_cols) * gate).astype(BF16)
+        recon_full = contract(act, dec_all[...], 0, 0) + base
+        if i < parts:
+            recon[...] = recon_full[: recon.shape[0]].astype(BF16)
+        error = (recon_full - target).astype(BF16)
+        error_all[span, :] = error
+        act_all[:, span] = act
+        dpre_all[:, span] = (contract(dec_all[...], error, 1, 1) * gate).astype(BF16)
+        for j, (part, _) in enumerate(some):
+            inputs_all[(i + j) * n : (i + j + 1) * n, :] = part[:, cols]
+    dec_terms[...] = contract(act_all[...], error_all[:, cols], 1, 0)
+    enc_terms[...] = contract(dpre_all[...], inputs_all[...], 1, 0)
     for zero, one_table, piece in zip(CORE_0, CORE_1, pieces, strict=True):
         to = look_up(one_table, rank)
         if zero is not None:
@@ -281,6 +284,9 @@
             pltpu.VMEM((latents, width), BF16),
             pltpu.VMEM((latents, width), BF16),
             pltpu.VMEM((2 * tokens, width), BF16),
+            pltpu.VMEM((latents, 2 * tokens), BF16),
+            pltpu.VMEM((latents, 2 * tokens), BF16),
+            pltpu.VMEM((2 * tokens, 2 * share), BF16),
             pltpu.VMEM((latents, 2 * share), F32),
             pltpu.VMEM((latents, 2 * share), F32),
         ],

time: 27.5 us -> 27.2 us (0.989)
  Pallas kernels: 4.7 us -> 4.39 us
    pallas_call x4, Pallas kernels: 2.5 us -> 2.2 us  [kernel_call(): pl.pallas_call(kernel, out_shape=outs, in_specs=[VMEM] * len(operands), o...]
where the time goes in v4:
time: 27.2 us; the launch traced here: 27 us
  starting transfers between devices  11.5 us (42%)
  waiting for transfers between devices  9.59 us (35%)
  Pallas kernels  4.39 us (16%)
  local copies, waits for them, and re-layouts  0.79 us (3%)
  between operations  0.7 us (3%)
    ppermute x12, starting transfers between devices, move(): return lax.ppermute(array, PAIR, pairs)  11.5 us
    ppermute x12, waiting for transfers between devices, move(): return lax.ppermute(array, PAIR, pairs)  9.59 us
    pallas_call x4, Pallas kernels, kernel_call(): pl.pallas_call(kernel, out_shape=outs, in_specs=[VMEM] * len(operands), o...  2.2 us
    pallas_call x1, Pallas kernels, small_body(): pl.pallas_call(load_kernel, out_shape=[pltpu.VMEM((tokens // parts, width...  1.32 us
    pallas_call x1, Pallas kernels, small_body(): pl.pallas_call(pack_kernel, out_shape=[pltpu.VMEM((STRIP, 2 * strips * wi...  0.87 us
    unnamed x1, local copies, waits for them, and re-layouts  0.79 us
  transfers between devices with their start and end apart: 12, of which 7 were waited for; matrix products, arithmetic and copies ran while one was open for 3% of the time, Pallas kernels for 5%

profile of v4, /device:TPU:0, one launch (start us, length us, event | category | flops | bytes accessed | tf_op | source)
XLA Modules:
  0.0 27.0 jit_solution(5784028370489665067)
XLA Ops:
  0.6 0.9 %shard_map.94 = (bf16[16,4224]{1,0:T(8,128)(2,1)S(1)}, bf16[16,2176]{1,0:T(8,128)(2,1)S(1)}) custom-call(bf16[32,1024]{1,0:T(8,128)(2,1)} %enc.1, bf16[32,1024]{1,0:T(8,128)(2,1)} %dec.1, bf16[32]{0:T(256)(128)(2,1)} %bias.1), custom_call_target="tpu_custom_call" | custom-call | tf_op jit(solution)/shard_map/pallas_call | solution.py:248
  1.5 5.1 %collective-permute-start.1 = (bf16[16,4224]{1,0:T(8,128)(2,1)S(1)}, bf16[16,4224]{1,0:T(8,128)(2,1)S(1)}, u32[]{:S(2)}, u32[]{:S(2)}) collective-permute-start(bf16[16,4224]{1,0:T(8,128)(2,1)S(1)} %get-tuple-element.22.own), channel_id=1, source_target_pairs={{0,12},{1,9},{2,14},{3,11},{4,8},{5,13},{6,10},{7,15},{8,4},{9,1},... | collective-permute-start | bytes 405512 | tf_op jit(solution)/shard_map/ppermute | solution.py:56
  6.6 0.0 collective-permute-start
  6.6 1.3 %shard_map.95 = (bf16[128,1024]{1,0:T(8,128)(2,1)S(1)}, bf16[128,1024]{1,0:T(8,128)(2,1)S(1)}, bf16[128,1152]{1,0:T(8,128)(2,1)S(1)}, bf16[128,1152]{1,0:T(8,128)(2,1)S(1)}, f32[1024]{0:T(1024)S(1)}) custom-call(bf16[256,1024]{1,0:T(8,128)(2,1)} %inputs.1, bf16[256,1024]{1,0:T(8,128)(2,1)} %targets.1, s32[256,128]{1,0:T(8,128)} %mask.1, f32[1024]{0:T(1024)} %dec_bias.1, ...), custom_call_target="tpu_custom_call" | custom-call | bytes 1048576 | tf_op jit(solution)/shard_map/pallas_call | solution.py:261
  8.0 0.1 collective-permute-start.5
  8.0 0.5 %collective-permute-start.6 = (bf16[128,1152]{1,0:T(8,128)(2,1)S(1)}, bf16[128,1152]{1,0:T(8,128)(2,1)S(1)}, u32[]{:S(2)}, u32[]{:S(2)}) collective-permute-start(bf16[128,1152]{1,0:T(8,128)(2,1)S(1)} %get-tuple-element.26.refs_3_), channel_id=1, source_target_pairs={{0,1},{1,0},{2,3},{3,2},{4,5},{5,4},{6,7},{7,6},{8,9},{9,8},{10,11... | collective-permute-start | bytes 884744 | tf_op jit(solution)/shard_map/ppermute | solution.py:56
  8.5 0.1 collective-permute-start.3
  8.6 2.9 %collective-permute-done.one = bf16[16,2176]{1,0:T(8,128)(2,1)S(1)} collective-permute-done((bf16[16,2176]{1,0:T(8,128)(2,1)S(1)}, bf16[16,2176]{1,0:T(8,128)(2,1)S(1)}, u32[]{:S(2)}, u32[]{:S(2)}) %collective-permute-start) | collective-permute-done | bytes 69664 | tf_op jit(solution)/shard_map/ppermute | solution.py:56
  11.5 0.0 collective-permute-start.4
  11.5 0.0 collective-permute-done.1.far
  11.5 0.6 %collective-permute-start.2 = (bf16[16,6400]{1,0:T(8,128)(2,1)S(1)}, bf16[16,6400]{1,0:T(8,128)(2,1)S(1)}, u32[]{:S(2)}, u32[]{:S(2)}) collective-permute-start(bf16[16,6400]{1,0:T(8,128)(2,1)S(1)} %shard_map.96), channel_id=1, source_target_pairs={{0,1},{1,0},{2,3},{3,2},{4,5},{5,4},{6,7},{7,6},{8,9},{9,8},{10,11... | collective-permute-start | bytes 614408 | tf_op jit(solution)/shard_map/ppermute | solution.py:56
  12.1 0.0 collective-permute-done.3.refs_4_
  12.1 0.9 %collective-permute-done.4.refs_5_ = bf16[128,1024]{1,0:T(8,128)(2,1)S(1)} collective-permute-done((bf16[128,1024]{1,0:T(8,128)(2,1)S(1)}, bf16[128,1024]{1,0:T(8,128)(2,1)S(1)}, u32[]{:S(2)}, u32[]{:S(2)}) %collective-permute-start.4) | collective-permute-done | bytes 262176 | tf_op jit(solution)/shard_map/ppermute | solution.py:56
  13.0 0.0 collective-permute-done.5.refs_6_
  13.1 0.0 collective-permute-done.6.refs_7_
  13.1 0.3 %collective-permute-done.2.other = bf16[16,6400]{1,0:T(8,128)(2,1)S(1)} collective-permute-done((bf16[16,6400]{1,0:T(8,128)(2,1)S(1)}, bf16[16,6400]{1,0:T(8,128)(2,1)S(1)}, u32[]{:S(2)}, u32[]{:S(2)}) %collective-permute-start.2) | collective-permute-done | bytes 204832 | tf_op jit(solution)/shard_map/ppermute | solution.py:56
  13.3 1.5 %shard_map.97 = (bf16[256,1024]{1,0:T(8,128)(2,1)S(1)}, bf16[64,512]{1,0:T(8,128)(2,1)S(1)}, bf16[64,512]{1,0:T(8,128)(2,1)S(1)}, bf16[64,512]{1,0:T(8,128)(2,1)...) custom-call(f32[1024]{0:T(1024)S(1)} %get-tuple-element.21.dec_bias, ...), custom_call_target="tpu_custom_call" | custom-call | flops 536870912 | tf_op jit(solution)/shard_map/pallas_call | solution.py:38
  14.9 3.0 %collective-permute-start.7 = (bf16[64,512]{1,0:T(8,128)(2,1)S(1)}, bf16[64,512]{1,0:T(8,128)(2,1)S(1)}, u32[]{:S(2)}, u32[]{:S(2)}) collective-permute-start(bf16[64,512]{1,0:T(8,128)(2,1)S(1)} %get-tuple-element.28), channel_id=1, source_target_pairs={{0,8},{1,11},{2,10},{3,9},{4,12},{5,15},{6,14},{7,13},{8,0},{9,3},... | collective-permute-start | bytes 196616 | tf_op jit(solution)/shard_map/ppermute | solution.py:56
  17.8 0.4 %collective-permute-start.8 = (bf16[64,512]{1,0:T(8,128)(2,1)S(1)}, bf16[64,512]{1,0:T(8,128)(2,1)S(1)}, u32[]{:S(2)}, u32[]{:S(2)}) collective-permute-start(bf16[64,512]{1,0:T(8,128)(2,1)S(1)} %get-tuple-element.29), channel_id=1, source_target_pairs={{0,12},{1,15},{2,14},{3,13},{4,8},{5,11},{6,10},{7,9},{8,4},{9,7},... | collective-permute-start | bytes 196616 | tf_op jit(solution)/shard_map/ppermute | solution.py:56
  18.3 0.5 %collective-permute-start.9 = (bf16[64,512]{1,0:T(8,128)(2,1)S(1)}, bf16[64,512]{1,0:T(8,128)(2,1)S(1)}, u32[]{:S(2)}, u32[]{:S(2)}) collective-permute-start(bf16[64,512]{1,0:T(8,128)(2,1)S(1)} %get-tuple-element.30), channel_id=1, source_target_pairs={{0,4},{1,7},{2,6},{3,5},{4,0},{5,3},{6,2},{7,1},{8,12},{9,15},{10,... | collective-permute-start | bytes 196616 | tf_op jit(solution)/shard_map/ppermute | solution.py:56
  18.8 0.7 %collective-permute-start.10 = (bf16[64,512]{1,0:T(8,128)(2,1)S(1)}, bf16[64,512]{1,0:T(8,128)(2,1)S(1)}, u32[]{:S(2)}, u32[]{:S(2)}) collective-permute-start(bf16[64,512]{1,0:T(8,128)(2,1)S(1)} %get-tuple-element.31), channel_id=1, source_target_pairs={{1,3},{3,1},{5,7},{7,5},{9,11},{11,9},{13,15},{15,13},{17,19},{19,... | collective-permute-start | bytes 196616 | tf_op jit(solution)/shard_map/ppermute | solution.py:56
  19.4 2.5 %collective-permute-done.7.refs_0_ = bf16[64,512]{1,0:T(8,128)(2,1)S(1)} collective-permute-done((bf16[64,512]{1,0:T(8,128)(2,1)S(1)}, bf16[64,512]{1,0:T(8,128)(2,1)S(1)}, u32[]{:S(2)}, u32[]{:S(2)}) %collective-permute-start.7) | collective-permute-done | bytes 65568 | tf_op jit(solution)/shard_map/ppermute | solution.py:56
  21.9 2.7 %collective-permute-done.8.refs_1_ = bf16[64,512]{1,0:T(8,128)(2,1)S(1)} collective-permute-done((bf16[64,512]{1,0:T(8,128)(2,1)S(1)}, bf16[64,512]{1,0:T(8,128)(2,1)S(1)}, u32[]{:S(2)}, u32[]{:S(2)}) %collective-permute-start.8) | collective-permute-done | bytes 65568 | tf_op jit(solution)/shard_map/ppermute | solution.py:56
  24.7 0.2 collective-permute-done.9.refs_2_
  24.8 0.0 collective-permute-done.10.refs_3_
  24.9 0.6 %collective-permute-start.11 = (bf16[64,256]{1,0:T(8,128)(2,1)S(1)}, bf16[64,256]{1,0:T(8,128)(2,1)S(1)}, u32[]{:S(2)}, u32[]{:S(2)}) collective-permute-start(bf16[64,256]{1,0:T(8,128)(2,1)S(1)} %get-tuple-element.34), channel_id=1, source_target_pairs={{0,1},{1,0},{2,3},{3,2},{4,5},{5,4},{6,7},{7,6},{8,9},{9,8},{10,11... | collective-permute-start | bytes 98312 | tf_op jit(solution)/shard_map/ppermute | solution.py:56
  25.5 0.8 %copy.10 = bf16[256,1024]{1,0:T(8,128)(2,1)} copy(bf16[256,1024]{1,0:T(8,128)(2,1)S(1)} %get-tuple-element.37) | data formatting | bytes 1048576
  26.3 0.1 collective-permute-done.11.refs_1_
  26.3 0.6 %shard_map.99 = (f32[32,256]{1,0:T(8,128)}, f32[32,256]{1,0:T(8,128)}) custom-call(f32[64,256]{1,0:T(8,128)S(1)} %get-tuple-element.33.refs_0_, bf16[64,256]{1,0:T(8,128)(2,1)S(1)} %collective-permute-done.11.refs_1_), custom_call_target="tpu_custom_call" | custom-call | tf_op jit(solution)/shard_map/pallas_call | solution.py:38
  (2 shorter events, 0.1 us)
Async XLA Ops:
  1.5 10.0 %collective-permute-start.1 = (bf16[16,4224]{1,0:T(8,128)(2,1)S(1)}, bf16[16,4224]{1,0:T(8,128)(2,1)S(1)}, u32[]{:S(2)}, u32[]{:S(2)}) collective-permute-start(bf16[16,4224]{1,0:T(8,128)(2,1)S(1)} %get-tuple-element.22.own), channel_id=1, source_target_pairs={{0,12},{1,9},{2,14},{3,11},{4,8},{5,13},{6,10},{7,15},{8,4},{9,1},... | collective-permute-start | bytes 405512 | tf_op jit(solution)/shard_map/ppermute | solution.py:56
  6.6 4.9 %collective-permute-start = (bf16[16,2176]{1,0:T(8,128)(2,1)S(1)}, bf16[16,2176]{1,0:T(8,128)(2,1)S(1)}, u32[]{:S(2)}, u32[]{:S(2)}) collective-permute-start(bf16[16,2176]{1,0:T(8,128)(2,1)S(1)} %get-tuple-element.20.after), channel_id=1, source_target_pairs={{0,4},{1,5},{2,6},{3,7},{4,0},{5,1},{6,2},{7,3},{8,12},{9,13},{10,... | collective-permute-start | bytes 208904 | tf_op jit(solution)/shard_map/ppermute | solution.py:56
  8.0 5.1 %collective-permute-start.5 = (bf16[128,1152]{1,0:T(8,128)(2,1)S(1)}, bf16[128,1152]{1,0:T(8,128)(2,1)S(1)}, u32[]{:S(2)}, u32[]{:S(2)}) collective-permute-start(bf16[128,1152]{1,0:T(8,128)(2,1)S(1)} %get-tuple-element.25.refs_2_), channel_id=1, source_target_pairs={{0,1},{1,0},{2,3},{3,2},{4,5},{5,4},{6,7},{7,6},{8,9},{9,8},{10,11... | collective-permute-start | bytes 884744 | tf_op jit(solution)/shard_map/ppermute | solution.py:56
  8.0 5.0 %collective-permute-start.6 = (bf16[128,1152]{1,0:T(8,128)(2,1)S(1)}, bf16[128,1152]{1,0:T(8,128)(2,1)S(1)}, u32[]{:S(2)}, u32[]{:S(2)}) collective-permute-start(bf16[128,1152]{1,0:T(8,128)(2,1)S(1)} %get-tuple-element.26.refs_3_), channel_id=1, source_target_pairs={{0,1},{1,0},{2,3},{3,2},{4,5},{5,4},{6,7},{7,6},{8,9},{9,8},{10,11... | collective-permute-start | bytes 884744 | tf_op jit(solution)/shard_map/ppermute | solution.py:56
  8.5 3.6 %collective-permute-start.3 = (bf16[128,1024]{1,0:T(8,128)(2,1)S(1)}, bf16[128,1024]{1,0:T(8,128)(2,1)S(1)}, u32[]{:S(2)}, u32[]{:S(2)}) collective-permute-start(bf16[128,1024]{1,0:T(8,128)(2,1)S(1)} %get-tuple-element.23.refs_0_), channel_id=1, source_target_pairs={{0,1},{1,0},{2,3},{3,2},{4,5},{5,4},{6,7},{7,6},{8,9},{9,8},{10,11... | collective-permute-start | bytes 786440 | tf_op jit(solution)/shard_map/ppermute | solution.py:56
  11.5 1.5 %collective-permute-start.4 = (bf16[128,1024]{1,0:T(8,128)(2,1)S(1)}, bf16[128,1024]{1,0:T(8,128)(2,1)S(1)}, u32[]{:S(2)}, u32[]{:S(2)}) collective-permute-start(bf16[128,1024]{1,0:T(8,128)(2,1)S(1)} %get-tuple-element.24.refs_1_), channel_id=1, source_target_pairs={{0,1},{1,0},{2,3},{3,2},{4,5},{5,4},{6,7},{7,6},{8,9},{9,8},{10,11... | collective-permute-start | bytes 786440 | tf_op jit(solution)/shard_map/ppermute | solution.py:56
  11.5 1.8 %collective-permute-start.2 = (bf16[16,6400]{1,0:T(8,128)(2,1)S(1)}, bf16[16,6400]{1,0:T(8,128)(2,1)S(1)}, u32[]{:S(2)}, u32[]{:S(2)}) collective-permute-start(bf16[16,6400]{1,0:T(8,128)(2,1)S(1)} %shard_map.96), channel_id=1, source_target_pairs={{0,1},{1,0},{2,3},{3,2},{4,5},{5,4},{6,7},{7,6},{8,9},{9,8},{10,11... | collective-permute-start | bytes 614408 | tf_op jit(solution)/shard_map/ppermute | solution.py:56
  14.9 7.1 %collective-permute-start.7 = (bf16[64,512]{1,0:T(8,128)(2,1)S(1)}, bf16[64,512]{1,0:T(8,128)(2,1)S(1)}, u32[]{:S(2)}, u32[]{:S(2)}) collective-permute-start(bf16[64,512]{1,0:T(8,128)(2,1)S(1)} %get-tuple-element.28), channel_id=1, source_target_pairs={{0,8},{1,11},{2,10},{3,9},{4,12},{5,15},{6,14},{7,13},{8,0},{9,3},... | collective-permute-start | bytes 196616 | tf_op jit(solution)/shard_map/ppermute | solution.py:56
  17.8 6.8 %collective-permute-start.8 = (bf16[64,512]{1,0:T(8,128)(2,1)S(1)}, bf16[64,512]{1,0:T(8,128)(2,1)S(1)}, u32[]{:S(2)}, u32[]{:S(2)}) collective-permute-start(bf16[64,512]{1,0:T(8,128)(2,1)S(1)} %get-tuple-element.29), channel_id=1, source_target_pairs={{0,12},{1,15},{2,14},{3,13},{4,8},{5,11},{6,10},{7,9},{8,4},{9,7},... | collective-permute-start | bytes 196616 | tf_op jit(solution)/shard_map/ppermute | solution.py:56
  18.3 6.5 %collective-permute-start.9 = (bf16[64,512]{1,0:T(8,128)(2,1)S(1)}, bf16[64,512]{1,0:T(8,128)(2,1)S(1)}, u32[]{:S(2)}, u32[]{:S(2)}) collective-permute-start(bf16[64,512]{1,0:T(8,128)(2,1)S(1)} %get-tuple-element.30), channel_id=1, source_target_pairs={{0,4},{1,7},{2,6},{3,5},{4,0},{5,3},{6,2},{7,1},{8,12},{9,15},{10,... | collective-permute-start | bytes 196616 | tf_op jit(solution)/shard_map/ppermute | solution.py:56
  18.8 6.1 %collective-permute-start.10 = (bf16[64,512]{1,0:T(8,128)(2,1)S(1)}, bf16[64,512]{1,0:T(8,128)(2,1)S(1)}, u32[]{:S(2)}, u32[]{:S(2)}) collective-permute-start(bf16[64,512]{1,0:T(8,128)(2,1)S(1)} %get-tuple-element.31), channel_id=1, source_target_pairs={{1,3},{3,1},{5,7},{7,5},{9,11},{11,9},{13,15},{15,13},{17,19},{19,... | collective-permute-start | bytes 196616 | tf_op jit(solution)/shard_map/ppermute | solution.py:56
  24.9 1.5 %collective-permute-start.11 = (bf16[64,256]{1,0:T(8,128)(2,1)S(1)}, bf16[64,256]{1,0:T(8,128)(2,1)S(1)}, u32[]{:S(2)}, u32[]{:S(2)}) collective-permute-start(bf16[64,256]{1,0:T(8,128)(2,1)S(1)} %get-tuple-element.34), channel_id=1, source_target_pairs={{0,1},{1,0},{2,3},{3,2},{4,5},{5,4},{6,7},{7,6},{8,9},{9,8},{10,11... | collective-permute-start | bytes 98312 | tf_op jit(solution)/shard_map/ppermute | solution.py:56

commit v5 on v4

--- a/solution.py
+++ b/solution.py
@@ -15,8 +15,8 @@
 TILE = 128
 
 FAR_0, FAR_1, NEAR = ((3, 2, 1, 0), (2, 3, 0, 1), (1, 0, 3, 2))
-CORE_0 = ((2, 3, 0, 1), (3, 2, 1, 0), (1, 0, 3, 2), None)
-CORE_1 = ((2, 3, 0, 1), (3, 2, 1, 0), (1, 0, 3, 2), (0, 1, 2, 3))
+CORE_0 = ((2, 3, 0, 1), (3, 2, 1, 0), (1, 0, 3, 2), (0, 1, 2, 3))
+CORE_1 = ((1, 3, 0, 2), (3, 2, 1, 0), (2, 0, 3, 1), (0, 1, 2, 3))
 
 
 def look_up(table, index):
@@ -51,8 +51,7 @@
     for b in range(blks):
         for t in range(toks):
             to = where(b, t)
-            if to is not None:
-                pairs.append((b * toks + t, to[0] * toks + to[1]))
+            pairs.append((b * toks + t, to[0] * toks + to[1]))
     return lax.ppermute(array, PAIR, pairs)
 
 
@@ -169,40 +168,27 @@
     base = dec_bias[...].reshape(1, width)
     half = pieces[0].shape[1]
     cols = pl.ds(pl.multiple_of((chip ^ core) * half, half), half)
-    chunks = []
-    for group in (refs[: 2 * parts], refs[2 * parts :]):
-        chunks += list(zip(group[:parts], group[parts:], strict=True))
-    n = chunks[0][0].shape[0]
-    merge = 512 // n
-    for i in range(0, len(chunks), merge):
-        span = slice(i * n, (i + merge) * n)
-        some = chunks[i : i + merge]
-
-        def stack(values):
-            return values[0] if len(values) == 1 else jnp.concatenate(values, axis=0)
-
-        x = stack([part[:, :width] for part, _ in some])
-        target = stack([part[:, :width] for _, part in some]).astype(F32)
-        gate = [part[:, width:] for _, part in some]
-        gate = (gate[0] if len(gate) == 1 else jnp.concatenate(gate, axis=1)).astype(F32)
-        pre = contract(enc_all[...], x, 1, 1)
-        bias_cols = jnp.concatenate([bias_col] * (pre.shape[1] // TILE), axis=1)
-        act = ((pre + bias_cols) * gate).astype(BF16)
-        recon_full = contract(act, dec_all[...], 0, 0) + base
-        if i < parts:
-            recon[...] = recon_full[: recon.shape[0]].astype(BF16)
-        error = (recon_full - target).astype(BF16)
-        error_all[span, :] = error
-        act_all[:, span] = act
-        dpre_all[:, span] = (contract(dec_all[...], error, 1, 1) * gate).astype(BF16)
-        for j, (part, _) in enumerate(some):
-            inputs_all[(i + j) * n : (i + j + 1) * n, :] = part[:, cols]
+    input_parts = (*refs[:parts], *refs[2 * parts : 3 * parts])
+    target_parts = (*refs[parts : 2 * parts], *refs[3 * parts :])
+    x = jnp.concatenate([part[...] for part in input_parts], axis=0)
+    target = jnp.concatenate([part[:, :width] for part in target_parts], axis=0).astype(F32)
+    gate = jnp.concatenate([part[:, width:] for part in target_parts], axis=1).astype(F32)
+    pre = contract(enc_all[...], x, 1, 1)
+    pre = pre + jnp.concatenate([bias_col] * (pre.shape[1] // TILE), axis=1)
+    act = (pre * gate).astype(BF16)
+    recon_full = contract(act, dec_all[...], 0, 0) + base
+    recon[...] = recon_full[: recon.shape[0]].astype(BF16)
+    error = (recon_full - target).astype(BF16)
+    error_all[...] = error
+    act_all[...] = act
+    dpre_all[...] = (contract(dec_all[...], error, 1, 1) * gate).astype(BF16)
+    n = input_parts[0].shape[0]
+    for i, part in enumerate(input_parts):
+        inputs_all[i * n : (i + 1) * n, :] = part[:, cols]
     dec_terms[...] = contract(act_all[...], error_all[:, cols], 1, 0)
     enc_terms[...] = contract(dpre_all[...], inputs_all[...], 1, 0)
     for zero, one_table, piece in zip(CORE_0, CORE_1, pieces, strict=True):
-        to = look_up(one_table, rank)
-        if zero is not None:
-            to = jnp.where(core == 0, look_up(zero, rank), to)
+        to = jnp.where(core == 0, look_up(zero, rank), look_up(one_table, rank))
         piece[:rows, :] = enc_terms[at(to), :].astype(BF16)
         piece[rows:, :] = dec_terms[at(to), :].astype(BF16)
     own_piece[:rows, :] = enc_terms[at(rank), :]
@@ -213,7 +199,7 @@
     *arrived, own, send, keep = refs
     share = keep.shape[1]
     core = lax.axis_index("tok") % 2
-    total = sum(part[...].astype(F32) for part in arrived)
+    total = sum(part[...].astype(F32) for part in arrived[:-1])
 
     @pl.when(core == 0)
     def _():
@@ -223,8 +209,9 @@
 
     @pl.when(core == 1)
     def _():
-        keep[...] = total[:, share:]
-        send[...] = total[:, :share].astype(BF16)
+        whole = total + arrived[-1][...].astype(F32)
+        keep[...] = whole[:, share:]
+        send[...] = whole[:, :share].astype(BF16)
 
 
 def last_kernel(factor, keep, came, grad_enc, grad_dec):
@@ -296,8 +283,8 @@
     for zero, one_table, out in zip(CORE_0, CORE_1, pieces, strict=True):
 
         def where(b, t, tables=(zero, one_table)):
-            table = tables[t % 2]
-            return None if table is None else (table[b], t ^ (2 * (t % 2)))
+            to = tables[t % 2][b]
+            return (to, t ^ 2 if t % 2 or to == b else t)
 
         arrived.append(move(out, blks, toks, where))
     send, keep = kernel_call(

time: 27.2 us -> 26.7 us (0.982)
  waiting for transfers between devices: 9.59 us -> 8.57 us
  starting transfers between devices: 11.5 us -> 12 us
    ppermute x12, waiting for transfers between devices: 9.59 us -> 8.57 us  [move(): return lax.ppermute(array, PAIR, pairs)]
    ppermute x12, starting transfers between devices: 11.5 us -> 12 us  [move(): return lax.ppermute(array, PAIR, pairs)]
  transfers between devices with their start and end apart: 12 -> 12, of which waited for: 7 -> 6; matrix products, arithmetic and copies ran while one was open for 3% -> 3% of each run, Pallas kernels for 5% -> 5%
where the time goes in v5:
time: 26.7 us; the launch traced here: 26.5 us
  starting transfers between devices  12 us (45%)
  waiting for transfers between devices  8.57 us (32%)
  Pallas kernels  4.38 us (16%)
  local copies, waits for them, and re-layouts  0.79 us (3%)
  between operations  0.69 us (3%)
    ppermute x12, starting transfers between devices, move(): return lax.ppermute(array, PAIR, pairs)  12 us
    ppermute x12, waiting for transfers between devices, move(): return lax.ppermute(array, PAIR, pairs)  8.57 us
    pallas_call x4, Pallas kernels, kernel_call(): pl.pallas_call(kernel, out_shape=outs, in_specs=[VMEM] * len(operands), o...  2.19 us
    pallas_call x1, Pallas kernels, small_body(): pl.pallas_call(load_kernel, out_shape=[pltpu.VMEM((tokens // parts, width...  1.32 us
    pallas_call x1, Pallas kernels, small_body(): pl.pallas_call(pack_kernel, out_shape=[pltpu.VMEM((STRIP, 2 * strips * wi...  0.87 us
    unnamed x1, local copies, waits for them, and re-layouts  0.79 us
  transfers between devices with their start and end apart: 12, of which 6 were waited for; matrix products, arithmetic and copies ran while one was open for 3% of the time, Pallas kernels for 5%

profile of v5, /device:TPU:0, one launch (start us, length us, event | category | flops | bytes accessed | tf_op | source)
XLA Modules:
  0.0 26.5 jit_solution(9236598153217443167)
XLA Ops:
  0.6 0.9 %shard_map.94 = (bf16[16,4224]{1,0:T(8,128)(2,1)S(1)}, bf16[16,2176]{1,0:T(8,128)(2,1)S(1)}) custom-call(bf16[32,1024]{1,0:T(8,128)(2,1)} %enc.1, bf16[32,1024]{1,0:T(8,128)(2,1)} %dec.1, bf16[32]{0:T(256)(128)(2,1)} %bias.1), custom_call_target="tpu_custom_call" | custom-call | tf_op jit(solution)/shard_map/pallas_call | solution.py:235
  1.5 5.1 %collective-permute-start.1 = (bf16[16,4224]{1,0:T(8,128)(2,1)S(1)}, bf16[16,4224]{1,0:T(8,128)(2,1)S(1)}, u32[]{:S(2)}, u32[]{:S(2)}) collective-permute-start(bf16[16,4224]{1,0:T(8,128)(2,1)S(1)} %get-tuple-element.22.own), channel_id=1, source_target_pairs={{0,12},{1,9},{2,14},{3,11},{4,8},{5,13},{6,10},{7,15},{8,4},{9,1},... | collective-permute-start | bytes 405512 | tf_op jit(solution)/shard_map/ppermute | solution.py:55
  6.6 0.0 collective-permute-start
  6.6 1.3 %shard_map.95 = (bf16[128,1024]{1,0:T(8,128)(2,1)S(1)}, bf16[128,1024]{1,0:T(8,128)(2,1)S(1)}, bf16[128,1152]{1,0:T(8,128)(2,1)S(1)}, bf16[128,1152]{1,0:T(8,128)(2,1)S(1)}, f32[1024]{0:T(1024)S(1)}) custom-call(bf16[256,1024]{1,0:T(8,128)(2,1)} %inputs.1, bf16[256,1024]{1,0:T(8,128)(2,1)} %targets.1, s32[256,128]{1,0:T(8,128)} %mask.1, f32[1024]{0:T(1024)} %dec_bias.1, ...), custom_call_target="tpu_custom_call" | custom-call | bytes 1048576 | tf_op jit(solution)/shard_map/pallas_call | solution.py:248
  8.0 0.1 collective-permute-start.5
  8.0 0.5 %collective-permute-start.6 = (bf16[128,1152]{1,0:T(8,128)(2,1)S(1)}, bf16[128,1152]{1,0:T(8,128)(2,1)S(1)}, u32[]{:S(2)}, u32[]{:S(2)}) collective-permute-start(bf16[128,1152]{1,0:T(8,128)(2,1)S(1)} %get-tuple-element.26.refs_3_), channel_id=1, source_target_pairs={{0,1},{1,0},{2,3},{3,2},{4,5},{5,4},{6,7},{7,6},{8,9},{9,8},{10,11... | collective-permute-start | bytes 884744 | tf_op jit(solution)/shard_map/ppermute | solution.py:55
  8.5 0.1 collective-permute-start.3
  8.6 2.9 %collective-permute-done.one = bf16[16,2176]{1,0:T(8,128)(2,1)S(1)} collective-permute-done((bf16[16,2176]{1,0:T(8,128)(2,1)S(1)}, bf16[16,2176]{1,0:T(8,128)(2,1)S(1)}, u32[]{:S(2)}, u32[]{:S(2)}) %collective-permute-start) | collective-permute-done | bytes 69664 | tf_op jit(solution)/shard_map/ppermute | solution.py:55
  11.5 0.0 collective-permute-start.4
  11.5 0.0 collective-permute-done.1.far
  11.5 0.6 %collective-permute-start.2 = (bf16[16,6400]{1,0:T(8,128)(2,1)S(1)}, bf16[16,6400]{1,0:T(8,128)(2,1)S(1)}, u32[]{:S(2)}, u32[]{:S(2)}) collective-permute-start(bf16[16,6400]{1,0:T(8,128)(2,1)S(1)} %shard_map.96), channel_id=1, source_target_pairs={{0,1},{1,0},{2,3},{3,2},{4,5},{5,4},{6,7},{7,6},{8,9},{9,8},{10,11... | collective-permute-start | bytes 614408 | tf_op jit(solution)/shard_map/ppermute | solution.py:55
  12.1 0.0 collective-permute-done.3.refs_4_
  12.1 0.9 %collective-permute-done.4.refs_5_ = bf16[128,1024]{1,0:T(8,128)(2,1)S(1)} collective-permute-done((bf16[128,1024]{1,0:T(8,128)(2,1)S(1)}, bf16[128,1024]{1,0:T(8,128)(2,1)S(1)}, u32[]{:S(2)}, u32[]{:S(2)}) %collective-permute-start.4) | collective-permute-done | bytes 262176 | tf_op jit(solution)/shard_map/ppermute | solution.py:55
  13.0 0.0 collective-permute-done.5.refs_6_
  13.1 0.0 collective-permute-done.6.refs_7_
  13.1 0.3 %collective-permute-done.2.other = bf16[16,6400]{1,0:T(8,128)(2,1)S(1)} collective-permute-done((bf16[16,6400]{1,0:T(8,128)(2,1)S(1)}, bf16[16,6400]{1,0:T(8,128)(2,1)S(1)}, u32[]{:S(2)}, u32[]{:S(2)}) %collective-permute-start.2) | collective-permute-done | bytes 204832 | tf_op jit(solution)/shard_map/ppermute | solution.py:55
  13.3 1.5 %shard_map.97 = (bf16[256,1024]{1,0:T(8,128)(2,1)S(1)}, bf16[64,512]{1,0:T(8,128)(2,1)S(1)}, bf16[64,512]{1,0:T(8,128)(2,1)S(1)}, bf16[64,512]{1,0:T(8,128)(2,1)...) custom-call(f32[1024]{0:T(1024)S(1)} %get-tuple-element.21.dec_bias, ...), custom_call_target="tpu_custom_call" | custom-call | flops 536870912 | tf_op jit(solution)/shard_map/pallas_call | solution.py:38
  14.9 3.0 %collective-permute-start.7 = (bf16[64,512]{1,0:T(8,128)(2,1)S(1)}, bf16[64,512]{1,0:T(8,128)(2,1)S(1)}, u32[]{:S(2)}, u32[]{:S(2)}) collective-permute-start(bf16[64,512]{1,0:T(8,128)(2,1)S(1)} %get-tuple-element.28), channel_id=1, source_target_pairs={{0,8},{1,7},{2,10},{3,5},{4,12},{5,15},{6,14},{7,13},{8,0},{9,3},{... | collective-permute-start | bytes 196616 | tf_op jit(solution)/shard_map/ppermute | solution.py:55
  17.8 0.4 %collective-permute-start.8 = (bf16[64,512]{1,0:T(8,128)(2,1)S(1)}, bf16[64,512]{1,0:T(8,128)(2,1)S(1)}, u32[]{:S(2)}, u32[]{:S(2)}) collective-permute-start(bf16[64,512]{1,0:T(8,128)(2,1)S(1)} %get-tuple-element.29), channel_id=1, source_target_pairs={{0,12},{1,15},{2,14},{3,13},{4,8},{5,11},{6,10},{7,9},{8,4},{9,7},... | collective-permute-start | bytes 196616 | tf_op jit(solution)/shard_map/ppermute | solution.py:55
  18.3 0.5 %collective-permute-start.9 = (bf16[64,512]{1,0:T(8,128)(2,1)S(1)}, bf16[64,512]{1,0:T(8,128)(2,1)S(1)}, u32[]{:S(2)}, u32[]{:S(2)}) collective-permute-start(bf16[64,512]{1,0:T(8,128)(2,1)S(1)} %get-tuple-element.30), channel_id=1, source_target_pairs={{0,4},{1,11},{2,6},{3,9},{4,0},{5,3},{6,2},{7,1},{8,12},{9,15},{10... | collective-permute-start | bytes 196616 | tf_op jit(solution)/shard_map/ppermute | solution.py:55
  18.7 1.5 %collective-permute-start.10 = (bf16[64,512]{1,0:T(8,128)(2,1)S(1)}, bf16[64,512]{1,0:T(8,128)(2,1)S(1)}, u32[]{:S(2)}, u32[]{:S(2)}) collective-permute-start(bf16[64,512]{1,0:T(8,128)(2,1)S(1)} %get-tuple-element.31), channel_id=1, source_target_pairs={{0,2},{1,3},{2,0},{3,1},{4,6},{5,7},{6,4},{7,5},{8,10},{9,11},{10,... | collective-permute-start | bytes 196616 | tf_op jit(solution)/shard_map/ppermute | solution.py:55
  20.2 1.0 %collective-permute-done.7.refs_0_ = bf16[64,512]{1,0:T(8,128)(2,1)S(1)} collective-permute-done((bf16[64,512]{1,0:T(8,128)(2,1)S(1)}, bf16[64,512]{1,0:T(8,128)(2,1)S(1)}, u32[]{:S(2)}, u32[]{:S(2)}) %collective-permute-start.7) | collective-permute-done | bytes 65568 | tf_op jit(solution)/shard_map/ppermute | solution.py:55
  21.2 3.3 %collective-permute-done.8.refs_1_ = bf16[64,512]{1,0:T(8,128)(2,1)S(1)} collective-permute-done((bf16[64,512]{1,0:T(8,128)(2,1)S(1)}, bf16[64,512]{1,0:T(8,128)(2,1)S(1)}, u32[]{:S(2)}, u32[]{:S(2)}) %collective-permute-start.8) | collective-permute-done | bytes 65568 | tf_op jit(solution)/shard_map/ppermute | solution.py:55
  24.5 0.0 collective-permute-done.9.refs_2_
  24.5 0.0 collective-permute-done.10.refs_3_
  24.6 0.3 %collective-permute-start.11 = (bf16[64,256]{1,0:T(8,128)(2,1)S(1)}, bf16[64,256]{1,0:T(8,128)(2,1)S(1)}, u32[]{:S(2)}, u32[]{:S(2)}) collective-permute-start(bf16[64,256]{1,0:T(8,128)(2,1)S(1)} %get-tuple-element.34), channel_id=1, source_target_pairs={{0,1},{1,0},{2,3},{3,2},{4,5},{5,4},{6,7},{7,6},{8,9},{9,8},{10,11... | collective-permute-start | bytes 98312 | tf_op jit(solution)/shard_map/ppermute | solution.py:55
  24.9 0.8 %copy.10 = bf16[256,1024]{1,0:T(8,128)(2,1)} copy(bf16[256,1024]{1,0:T(8,128)(2,1)S(1)} %get-tuple-element.37) | data formatting | bytes 1048576
  25.7 0.2 collective-permute-done.11.refs_1_
  25.8 0.6 %shard_map.99 = (f32[32,256]{1,0:T(8,128)}, f32[32,256]{1,0:T(8,128)}) custom-call(f32[64,256]{1,0:T(8,128)S(1)} %get-tuple-element.33.refs_0_, bf16[64,256]{1,0:T(8,128)(2,1)S(1)} %collective-permute-done.11.refs_1_), custom_call_target="tpu_custom_call" | custom-call | tf_op jit(solution)/shard_map/pallas_call | solution.py:38
  (2 shorter events, 0.1 us)
Async XLA Ops:
  1.5 10.0 %collective-permute-start.1 = (bf16[16,4224]{1,0:T(8,128)(2,1)S(1)}, bf16[16,4224]{1,0:T(8,128)(2,1)S(1)}, u32[]{:S(2)}, u32[]{:S(2)}) collective-permute-start(bf16[16,4224]{1,0:T(8,128)(2,1)S(1)} %get-tuple-element.22.own), channel_id=1, source_target_pairs={{0,12},{1,9},{2,14},{3,11},{4,8},{5,13},{6,10},{7,15},{8,4},{9,1},... | collective-permute-start | bytes 405512 | tf_op jit(solution)/shard_map/ppermute | solution.py:55
  6.6 4.9 %collective-permute-start = (bf16[16,2176]{1,0:T(8,128)(2,1)S(1)}, bf16[16,2176]{1,0:T(8,128)(2,1)S(1)}, u32[]{:S(2)}, u32[]{:S(2)}) collective-permute-start(bf16[16,2176]{1,0:T(8,128)(2,1)S(1)} %get-tuple-element.20.after), channel_id=1, source_target_pairs={{0,4},{1,5},{2,6},{3,7},{4,0},{5,1},{6,2},{7,3},{8,12},{9,13},{10,... | collective-permute-start | bytes 208904 | tf_op jit(solution)/shard_map/ppermute | solution.py:55
  8.0 5.1 %collective-permute-start.5 = (bf16[128,1152]{1,0:T(8,128)(2,1)S(1)}, bf16[128,1152]{1,0:T(8,128)(2,1)S(1)}, u32[]{:S(2)}, u32[]{:S(2)}) collective-permute-start(bf16[128,1152]{1,0:T(8,128)(2,1)S(1)} %get-tuple-element.25.refs_2_), channel_id=1, source_target_pairs={{0,1},{1,0},{2,3},{3,2},{4,5},{5,4},{6,7},{7,6},{8,9},{9,8},{10,11... | collective-permute-start | bytes 884744 | tf_op jit(solution)/shard_map/ppermute | solution.py:55
  8.0 5.0 %collective-permute-start.6 = (bf16[128,1152]{1,0:T(8,128)(2,1)S(1)}, bf16[128,1152]{1,0:T(8,128)(2,1)S(1)}, u32[]{:S(2)}, u32[]{:S(2)}) collective-permute-start(bf16[128,1152]{1,0:T(8,128)(2,1)S(1)} %get-tuple-element.26.refs_3_), channel_id=1, source_target_pairs={{0,1},{1,0},{2,3},{3,2},{4,5},{5,4},{6,7},{7,6},{8,9},{9,8},{10,11... | collective-permute-start | bytes 884744 | tf_op jit(solution)/shard_map/ppermute | solution.py:55
  8.5 3.6 %collective-permute-start.3 = (bf16[128,1024]{1,0:T(8,128)(2,1)S(1)}, bf16[128,1024]{1,0:T(8,128)(2,1)S(1)}, u32[]{:S(2)}, u32[]{:S(2)}) collective-permute-start(bf16[128,1024]{1,0:T(8,128)(2,1)S(1)} %get-tuple-element.23.refs_0_), channel_id=1, source_target_pairs={{0,1},{1,0},{2,3},{3,2},{4,5},{5,4},{6,7},{7,6},{8,9},{9,8},{10,11... | collective-permute-start | bytes 786440 | tf_op jit(solution)/shard_map/ppermute | solution.py:55
  11.5 1.5 %collective-permute-start.4 = (bf16[128,1024]{1,0:T(8,128)(2,1)S(1)}, bf16[128,1024]{1,0:T(8,128)(2,1)S(1)}, u32[]{:S(2)}, u32[]{:S(2)}) collective-permute-start(bf16[128,1024]{1,0:T(8,128)(2,1)S(1)} %get-tuple-element.24.refs_1_), channel_id=1, source_target_pairs={{0,1},{1,0},{2,3},{3,2},{4,5},{5,4},{6,7},{7,6},{8,9},{9,8},{10,11... | collective-permute-start | bytes 786440 | tf_op jit(solution)/shard_map/ppermute | solution.py:55
  11.5 1.8 %collective-permute-start.2 = (bf16[16,6400]{1,0:T(8,128)(2,1)S(1)}, bf16[16,6400]{1,0:T(8,128)(2,1)S(1)}, u32[]{:S(2)}, u32[]{:S(2)}) collective-permute-start(bf16[16,6400]{1,0:T(8,128)(2,1)S(1)} %shard_map.96), channel_id=1, source_target_pairs={{0,1},{1,0},{2,3},{3,2},{4,5},{5,4},{6,7},{7,6},{8,9},{9,8},{10,11... | collective-permute-start | bytes 614408 | tf_op jit(solution)/shard_map/ppermute | solution.py:55
  14.9 6.4 %collective-permute-start.7 = (bf16[64,512]{1,0:T(8,128)(2,1)S(1)}, bf16[64,512]{1,0:T(8,128)(2,1)S(1)}, u32[]{:S(2)}, u32[]{:S(2)}) collective-permute-start(bf16[64,512]{1,0:T(8,128)(2,1)S(1)} %get-tuple-element.28), channel_id=1, source_target_pairs={{0,8},{1,7},{2,10},{3,5},{4,12},{5,15},{6,14},{7,13},{8,0},{9,3},{... | collective-permute-start | bytes 196616 | tf_op jit(solution)/shard_map/ppermute | solution.py:55
  17.8 6.7 %collective-permute-start.8 = (bf16[64,512]{1,0:T(8,128)(2,1)S(1)}, bf16[64,512]{1,0:T(8,128)(2,1)S(1)}, u32[]{:S(2)}, u32[]{:S(2)}) collective-permute-start(bf16[64,512]{1,0:T(8,128)(2,1)S(1)} %get-tuple-element.29), channel_id=1, source_target_pairs={{0,12},{1,15},{2,14},{3,13},{4,8},{5,11},{6,10},{7,9},{8,4},{9,7},... | collective-permute-start | bytes 196616 | tf_op jit(solution)/shard_map/ppermute | solution.py:55
  18.3 6.2 %collective-permute-start.9 = (bf16[64,512]{1,0:T(8,128)(2,1)S(1)}, bf16[64,512]{1,0:T(8,128)(2,1)S(1)}, u32[]{:S(2)}, u32[]{:S(2)}) collective-permute-start(bf16[64,512]{1,0:T(8,128)(2,1)S(1)} %get-tuple-element.30), channel_id=1, source_target_pairs={{0,4},{1,11},{2,6},{3,9},{4,0},{5,3},{6,2},{7,1},{8,12},{9,15},{10... | collective-permute-start | bytes 196616 | tf_op jit(solution)/shard_map/ppermute | solution.py:55
  18.7 5.8 %collective-permute-start.10 = (bf16[64,512]{1,0:T(8,128)(2,1)S(1)}, bf16[64,512]{1,0:T(8,128)(2,1)S(1)}, u32[]{:S(2)}, u32[]{:S(2)}) collective-permute-start(bf16[64,512]{1,0:T(8,128)(2,1)S(1)} %get-tuple-element.31), channel_id=1, source_target_pairs={{0,2},{1,3},{2,0},{3,1},{4,6},{5,7},{6,4},{7,5},{8,10},{9,11},{10,... | collective-permute-start | bytes 196616 | tf_op jit(solution)/shard_map/ppermute | solution.py:55
  24.6 1.3 %collective-permute-start.11 = (bf16[64,256]{1,0:T(8,128)(2,1)S(1)}, bf16[64,256]{1,0:T(8,128)(2,1)S(1)}, u32[]{:S(2)}, u32[]{:S(2)}) collective-permute-start(bf16[64,256]{1,0:T(8,128)(2,1)S(1)} %get-tuple-element.34), channel_id=1, source_target_pairs={{0,1},{1,0},{2,3},{3,2},{4,5},{5,4},{6,7},{7,6},{8,9},{9,8},{10,11... | collective-permute-start | bytes 98312 | tf_op jit(solution)/shard_map/ppermute | solution.py:55

commit v6 on v5

--- a/solution.py
+++ b/solution.py
@@ -55,10 +55,9 @@
     return lax.ppermute(array, PAIR, pairs)
 
 
-def pack_kernel(enc, dec, bias, whole, half, side, sems):
+def pack_kernel(enc, dec, bias, whole, side, sems):
     rows, width = enc.shape
     rank = lax.axis_index("blk")
-    core = lax.axis_index("tok") % 2
     strips = rows // STRIP
     copies = [pltpu.make_async_copy(bias, side, sems.at[0])]
     for k, source in enumerate((enc, dec)):
@@ -76,17 +75,23 @@
     tile = jnp.concatenate([tile, jnp.zeros((STRIP, TILE - rows), F32)], axis=1)
     tile = pltpu.roll(tile, rank * rows, axis=1).astype(BF16)
     whole[:, 2 * strips * width :] = tile
-    half[:, strips * width :] = tile
     for copy in copies[1:]:
         copy.wait()
 
+
+def half_kernel(whole, half):
+    core = lax.axis_index("tok") % 2
+    size = half.shape[1] - TILE
+
     @pl.when(core == 0)
     def _():
-        half[:, : strips * width] = whole[:, : strips * width]
+        half[:, :size] = whole[:, :size]
 
     @pl.when(core == 1)
     def _():
-        half[:, : strips * width] = whole[:, strips * width : 2 * strips * width]
+        half[:, :size] = whole[:, size : 2 * size]
+
+    half[:, size:] = whole[:, 2 * size :]
 
 
 def load_kernel(inputs, targets, mask, dec_bias, after, *refs):
@@ -119,7 +124,7 @@
 
 
 def step_kernel(dec_bias, own, one, far, other, *refs):
-    *refs, enc_all, dec_all, error_all, act_all, dpre_all, inputs_all, enc_terms, dec_terms = refs
+    *refs, enc_all, dec_all, error_all, dpre_all, inputs_all, enc_terms, dec_terms = refs
     *refs, own_piece = refs
     refs, pieces = refs[: -len(CORE_1)], refs[-len(CORE_1) :]
     *refs, recon = refs
@@ -180,12 +185,11 @@
     recon[...] = recon_full[: recon.shape[0]].astype(BF16)
     error = (recon_full - target).astype(BF16)
     error_all[...] = error
-    act_all[...] = act
     dpre_all[...] = (contract(dec_all[...], error, 1, 1) * gate).astype(BF16)
     n = input_parts[0].shape[0]
     for i, part in enumerate(input_parts):
         inputs_all[i * n : (i + 1) * n, :] = part[:, cols]
-    dec_terms[...] = contract(act_all[...], error_all[:, cols], 1, 0)
+    dec_terms[...] = contract(act, error_all[:, cols], 1, 0)
     enc_terms[...] = contract(dpre_all[...], inputs_all[...], 1, 0)
     for zero, one_table, piece in zip(CORE_0, CORE_1, pieces, strict=True):
         to = jnp.where(core == 0, look_up(zero, rank), look_up(one_table, rank))
@@ -232,17 +236,15 @@
         return move(array, blks, toks, lambda b, t: (b, t ^ 1))
 
     strips = rows // STRIP
-    whole, half = pl.pallas_call(
+    whole = pl.pallas_call(
         pack_kernel,
-        out_shape=[
-            pltpu.VMEM((STRIP, 2 * strips * width + TILE), BF16),
-            pltpu.VMEM((STRIP, strips * width + TILE), BF16),
-        ],
+        out_shape=pltpu.VMEM((STRIP, 2 * strips * width + TILE), BF16),
         in_specs=[pl.BlockSpec(memory_space=pl.ANY)] * 3,
-        out_specs=[VMEM] * 2,
+        out_specs=VMEM,
         scratch_shapes=[pltpu.VMEM((rows,), BF16), pltpu.SemaphoreType.DMA((1 + 2 * strips,))],
     )(enc_weight, dec_weight, enc_bias)
     far = move(whole, blks, toks, lambda b, t: ((FAR_0, FAR_1)[t % 2][b], t))
+    (half,) = kernel_call(half_kernel, [pltpu.VMEM((STRIP, strips * width + TILE), BF16)], whole)
     one = move(half, blks, toks, lambda b, t: (NEAR[b], t))
     parts = 2
     *loaded, dec_bias = pl.pallas_call(
@@ -272,7 +274,6 @@
             pltpu.VMEM((latents, width), BF16),
             pltpu.VMEM((2 * tokens, width), BF16),
             pltpu.VMEM((latents, 2 * tokens), BF16),
-            pltpu.VMEM((latents, 2 * tokens), BF16),
             pltpu.VMEM((2 * tokens, 2 * share), BF16),
             pltpu.VMEM((latents, 2 * share), F32),
             pltpu.VMEM((latents, 2 * share), F32),

time: 26.7 us -> 26.7 us (level)
    pallas_call x4 -> x5, Pallas kernels: 2.19 us -> 2.19 us  [kernel_call(): pl.pallas_call(kernel, out_shape=outs, in_specs=[VMEM] * len(operands), o...]
where the time goes in v6:
time: 26.7 us; the launch traced here: 26.5 us
  starting transfers between devices  12 us (45%)
  waiting for transfers between devices  8.56 us (32%)
  Pallas kernels  4.39 us (16%)
  local copies, waits for them, and re-layouts  0.79 us (3%)
  between operations  0.69 us (3%)
    ppermute x12, starting transfers between devices, move(): return lax.ppermute(array, PAIR, pairs)  12 us
    ppermute x12, waiting for transfers between devices, move(): return lax.ppermute(array, PAIR, pairs)  8.56 us
    pallas_call x5, Pallas kernels, kernel_call(): pl.pallas_call(kernel, out_shape=outs, in_specs=[VMEM] * len(operands), o...  2.19 us
    pallas_call x1, Pallas kernels, small_body(): pl.pallas_call(load_kernel, out_shape=[pltpu.VMEM((tokens // parts, width...  1.33 us
    pallas_call x1, Pallas kernels, small_body(): pl.pallas_call(pack_kernel, out_shape=pltpu.VMEM((STRIP, 2 * strips * wid...  0.87 us
    unnamed x1, local copies, waits for them, and re-layouts  0.79 us
  transfers between devices with their start and end apart: 12, of which 6 were waited for; matrix products, arithmetic and copies ran while one was open for 3% of the time, Pallas kernels for 5%

profile of v6, /device:TPU:0, one launch (start us, length us, event | category | flops | bytes accessed | tf_op | source)
XLA Modules:
  0.0 26.5 jit_solution(14376031365637789439)
XLA Ops:
  0.6 0.9 %shard_map.94.whole.own = bf16[16,4224]{1,0:T(8,128)(2,1)S(1)} custom-call(bf16[32,1024]{1,0:T(8,128)(2,1)} %enc.1, bf16[32,1024]{1,0:T(8,128)(2,1)} %dec.1, bf16[32]{0:T(256)(128)(2,1)} %bias.1), custom_call_target="tpu_custom_call" | custom-call | tf_op jit(solution)/shard_map/pallas_call | solution.py:239
  1.5 5.1 %collective-permute-start.1 = (bf16[16,4224]{1,0:T(8,128)(2,1)S(1)}, bf16[16,4224]{1,0:T(8,128)(2,1)S(1)}, u32[]{:S(2)}, u32[]{:S(2)}) collective-permute-start(bf16[16,4224]{1,0:T(8,128)(2,1)S(1)} %shard_map.94.whole.own), channel_id=1, source_target_pairs={{0,12},{1,9},{2,14},{3,11},{4,8},{5,13},{6,10},{7,15},{8,4},{9,1},... | collective-permute-start | bytes 405512 | tf_op jit(solution)/shard_map/ppermute | solution.py:55
  6.6 0.0 collective-permute-start
  6.6 1.3 %shard_map.96 = (bf16[128,1024]{1,0:T(8,128)(2,1)S(1)}, bf16[128,1024]{1,0:T(8,128)(2,1)S(1)}, bf16[128,1152]{1,0:T(8,128)(2,1)S(1)}, bf16[128,1152]{1,0:T(8,128)(2,1)S(1)}, f32[1024]{0:T(1024)S(1)}) custom-call(bf16[256,1024]{1,0:T(8,128)(2,1)} %inputs.1, bf16[256,1024]{1,0:T(8,128)(2,1)} %targets.1, s32[256,128]{1,0:T(8,128)} %mask.1, f32[1024]{0:T(1024)} %dec_bias.1, ...), custom_call_target="tpu_custom_call" | custom-call | bytes 1048576 | tf_op jit(solution)/shard_map/pallas_call | solution.py:250
  8.0 0.1 collective-permute-start.5
  8.1 0.5 %collective-permute-start.6 = (bf16[128,1152]{1,0:T(8,128)(2,1)S(1)}, bf16[128,1152]{1,0:T(8,128)(2,1)S(1)}, u32[]{:S(2)}, u32[]{:S(2)}) collective-permute-start(bf16[128,1152]{1,0:T(8,128)(2,1)S(1)} %get-tuple-element.22.refs_3_), channel_id=1, source_target_pairs={{0,1},{1,0},{2,3},{3,2},{4,5},{5,4},{6,7},{7,6},{8,9},{9,8},{10,11... | collective-permute-start | bytes 884744 | tf_op jit(solution)/shard_map/ppermute | solution.py:55
  8.6 0.1 collective-permute-start.3
  8.6 2.9 %collective-permute-done.one = bf16[16,2176]{1,0:T(8,128)(2,1)S(1)} collective-permute-done((bf16[16,2176]{1,0:T(8,128)(2,1)S(1)}, bf16[16,2176]{1,0:T(8,128)(2,1)S(1)}, u32[]{:S(2)}, u32[]{:S(2)}) %collective-permute-start) | collective-permute-done | bytes 69664 | tf_op jit(solution)/shard_map/ppermute | solution.py:55
  11.5 0.0 collective-permute-start.4
  11.5 0.0 collective-permute-done.1.far
  11.5 0.6 %collective-permute-start.2 = (bf16[16,6400]{1,0:T(8,128)(2,1)S(1)}, bf16[16,6400]{1,0:T(8,128)(2,1)S(1)}, u32[]{:S(2)}, u32[]{:S(2)}) collective-permute-start(bf16[16,6400]{1,0:T(8,128)(2,1)S(1)} %shard_map.97), channel_id=1, source_target_pairs={{0,1},{1,0},{2,3},{3,2},{4,5},{5,4},{6,7},{7,6},{8,9},{9,8},{10,11... | collective-permute-start | bytes 614408 | tf_op jit(solution)/shard_map/ppermute | solution.py:55
  12.1 0.0 collective-permute-done.3.refs_4_
  12.1 0.9 %collective-permute-done.4.refs_5_ = bf16[128,1024]{1,0:T(8,128)(2,1)S(1)} collective-permute-done((bf16[128,1024]{1,0:T(8,128)(2,1)S(1)}, bf16[128,1024]{1,0:T(8,128)(2,1)S(1)}, u32[]{:S(2)}, u32[]{:S(2)}) %collective-permute-start.4) | collective-permute-done | bytes 262176 | tf_op jit(solution)/shard_map/ppermute | solution.py:55
  13.0 0.0 collective-permute-done.5.refs_6_
  13.0 0.0 collective-permute-done.6.refs_7_
  13.1 0.3 %collective-permute-done.2.other = bf16[16,6400]{1,0:T(8,128)(2,1)S(1)} collective-permute-done((bf16[16,6400]{1,0:T(8,128)(2,1)S(1)}, bf16[16,6400]{1,0:T(8,128)(2,1)S(1)}, u32[]{:S(2)}, u32[]{:S(2)}) %collective-permute-start.2) | collective-permute-done | bytes 204832 | tf_op jit(solution)/shard_map/ppermute | solution.py:55
  13.3 1.5 %shard_map.98 = (bf16[256,1024]{1,0:T(8,128)(2,1)S(1)}, bf16[64,512]{1,0:T(8,128)(2,1)S(1)}, bf16[64,512]{1,0:T(8,128)(2,1)S(1)}, bf16[64,512]{1,0:T(8,128)(2,1)...) custom-call(f32[1024]{0:T(1024)S(1)} %get-tuple-element.18.dec_bias, bf16[16,4224]{1,0:T(8,128)(2,1)S(1)} %shard_map.94.whole.own, ...), custom_call_target="tpu_custom_call" | custom-call | flops 536870912 | tf_op jit(solution)/shard_map/pallas_call | solution.py:38
  14.8 3.0 %collective-permute-start.7 = (bf16[64,512]{1,0:T(8,128)(2,1)S(1)}, bf16[64,512]{1,0:T(8,128)(2,1)S(1)}, u32[]{:S(2)}, u32[]{:S(2)}) collective-permute-start(bf16[64,512]{1,0:T(8,128)(2,1)S(1)} %get-tuple-element.24), channel_id=1, source_target_pairs={{0,8},{1,7},{2,10},{3,5},{4,12},{5,15},{6,14},{7,13},{8,0},{9,3},{... | collective-permute-start | bytes 196616 | tf_op jit(solution)/shard_map/ppermute | solution.py:55
  17.8 0.5 %collective-permute-start.8 = (bf16[64,512]{1,0:T(8,128)(2,1)S(1)}, bf16[64,512]{1,0:T(8,128)(2,1)S(1)}, u32[]{:S(2)}, u32[]{:S(2)}) collective-permute-start(bf16[64,512]{1,0:T(8,128)(2,1)S(1)} %get-tuple-element.25), channel_id=1, source_target_pairs={{0,12},{1,15},{2,14},{3,13},{4,8},{5,11},{6,10},{7,9},{8,4},{9,7},... | collective-permute-start | bytes 196616 | tf_op jit(solution)/shard_map/ppermute | solution.py:55
  18.3 0.5 %collective-permute-start.9 = (bf16[64,512]{1,0:T(8,128)(2,1)S(1)}, bf16[64,512]{1,0:T(8,128)(2,1)S(1)}, u32[]{:S(2)}, u32[]{:S(2)}) collective-permute-start(bf16[64,512]{1,0:T(8,128)(2,1)S(1)} %get-tuple-element.26), channel_id=1, source_target_pairs={{0,4},{1,11},{2,6},{3,9},{4,0},{5,3},{6,2},{7,1},{8,12},{9,15},{10... | collective-permute-start | bytes 196616 | tf_op jit(solution)/shard_map/ppermute | solution.py:55
  18.7 1.5 %collective-permute-start.10 = (bf16[64,512]{1,0:T(8,128)(2,1)S(1)}, bf16[64,512]{1,0:T(8,128)(2,1)S(1)}, u32[]{:S(2)}, u32[]{:S(2)}) collective-permute-start(bf16[64,512]{1,0:T(8,128)(2,1)S(1)} %get-tuple-element.27), channel_id=1, source_target_pairs={{0,2},{1,3},{2,0},{3,1},{4,6},{5,7},{6,4},{7,5},{8,10},{9,11},{10,... | collective-permute-start | bytes 196616 | tf_op jit(solution)/shard_map/ppermute | solution.py:55
  20.2 1.0 %collective-permute-done.7.refs_0_ = bf16[64,512]{1,0:T(8,128)(2,1)S(1)} collective-permute-done((bf16[64,512]{1,0:T(8,128)(2,1)S(1)}, bf16[64,512]{1,0:T(8,128)(2,1)S(1)}, u32[]{:S(2)}, u32[]{:S(2)}) %collective-permute-start.7) | collective-permute-done | bytes 65568 | tf_op jit(solution)/shard_map/ppermute | solution.py:55
  21.2 3.3 %collective-permute-done.8.refs_1_ = bf16[64,512]{1,0:T(8,128)(2,1)S(1)} collective-permute-done((bf16[64,512]{1,0:T(8,128)(2,1)S(1)}, bf16[64,512]{1,0:T(8,128)(2,1)S(1)}, u32[]{:S(2)}, u32[]{:S(2)}) %collective-permute-start.8) | collective-permute-done | bytes 65568 | tf_op jit(solution)/shard_map/ppermute | solution.py:55
  24.5 0.0 collective-permute-done.9.refs_2_
  24.5 0.0 collective-permute-done.10.refs_3_
  24.6 0.3 %collective-permute-start.11 = (bf16[64,256]{1,0:T(8,128)(2,1)S(1)}, bf16[64,256]{1,0:T(8,128)(2,1)S(1)}, u32[]{:S(2)}, u32[]{:S(2)}) collective-permute-start(bf16[64,256]{1,0:T(8,128)(2,1)S(1)} %get-tuple-element.30), channel_id=1, source_target_pairs={{0,1},{1,0},{2,3},{3,2},{4,5},{5,4},{6,7},{7,6},{8,9},{9,8},{10,11... | collective-permute-start | bytes 98312 | tf_op jit(solution)/shard_map/ppermute | solution.py:55
  24.9 0.8 %copy.10 = bf16[256,1024]{1,0:T(8,128)(2,1)} copy(bf16[256,1024]{1,0:T(8,128)(2,1)S(1)} %get-tuple-element.33) | data formatting | bytes 1048576
  25.7 0.2 collective-permute-done.11.refs_1_
  25.8 0.6 %shard_map.100 = (f32[32,256]{1,0:T(8,128)}, f32[32,256]{1,0:T(8,128)}) custom-call(f32[64,256]{1,0:T(8,128)S(1)} %get-tuple-element.29.refs_0_, bf16[64,256]{1,0:T(8,128)(2,1)S(1)} %collective-permute-done.11.refs_1_), custom_call_target="tpu_custom_call" | custom-call | tf_op jit(solution)/shard_map/pallas_call | solution.py:38
  (3 shorter events, 0.1 us)
Async XLA Ops:
  1.5 10.0 %collective-permute-start.1 = (bf16[16,4224]{1,0:T(8,128)(2,1)S(1)}, bf16[16,4224]{1,0:T(8,128)(2,1)S(1)}, u32[]{:S(2)}, u32[]{:S(2)}) collective-permute-start(bf16[16,4224]{1,0:T(8,128)(2,1)S(1)} %shard_map.94.whole.own), channel_id=1, source_target_pairs={{0,12},{1,9},{2,14},{3,11},{4,8},{5,13},{6,10},{7,15},{8,4},{9,1},... | collective-permute-start | bytes 405512 | tf_op jit(solution)/shard_map/ppermute | solution.py:55
  6.6 4.9 %collective-permute-start = (bf16[16,2176]{1,0:T(8,128)(2,1)S(1)}, bf16[16,2176]{1,0:T(8,128)(2,1)S(1)}, u32[]{:S(2)}, u32[]{:S(2)}) collective-permute-start(bf16[16,2176]{1,0:T(8,128)(2,1)S(1)} %shard_map.95.after), channel_id=1, source_target_pairs={{0,4},{1,5},{2,6},{3,7},{4,0},{5,1},{6,2},{7,3},{8,12},{9,13},{10,... | collective-permute-start | bytes 208904 | tf_op jit(solution)/shard_map/ppermute | solution.py:55
  8.0 5.1 %collective-permute-start.5 = (bf16[128,1152]{1,0:T(8,128)(2,1)S(1)}, bf16[128,1152]{1,0:T(8,128)(2,1)S(1)}, u32[]{:S(2)}, u32[]{:S(2)}) collective-permute-start(bf16[128,1152]{1,0:T(8,128)(2,1)S(1)} %get-tuple-element.21.refs_2_), channel_id=1, source_target_pairs={{0,1},{1,0},{2,3},{3,2},{4,5},{5,4},{6,7},{7,6},{8,9},{9,8},{10,11... | collective-permute-start | bytes 884744 | tf_op jit(solution)/shard_map/ppermute | solution.py:55
  8.1 5.0 %collective-permute-start.6 = (bf16[128,1152]{1,0:T(8,128)(2,1)S(1)}, bf16[128,1152]{1,0:T(8,128)(2,1)S(1)}, u32[]{:S(2)}, u32[]{:S(2)}) collective-permute-start(bf16[128,1152]{1,0:T(8,128)(2,1)S(1)} %get-tuple-element.22.refs_3_), channel_id=1, source_target_pairs={{0,1},{1,0},{2,3},{3,2},{4,5},{5,4},{6,7},{7,6},{8,9},{9,8},{10,11... | collective-permute-start | bytes 884744 | tf_op jit(solution)/shard_map/ppermute | solution.py:55
  8.6 3.6 %collective-permute-start.3 = (bf16[128,1024]{1,0:T(8,128)(2,1)S(1)}, bf16[128,1024]{1,0:T(8,128)(2,1)S(1)}, u32[]{:S(2)}, u32[]{:S(2)}) collective-permute-start(bf16[128,1024]{1,0:T(8,128)(2,1)S(1)} %get-tuple-element.19.refs_0_), channel_id=1, source_target_pairs={{0,1},{1,0},{2,3},{3,2},{4,5},{5,4},{6,7},{7,6},{8,9},{9,8},{10,11... | collective-permute-start | bytes 786440 | tf_op jit(solution)/shard_map/ppermute | solution.py:55
  11.5 1.5 %collective-permute-start.4 = (bf16[128,1024]{1,0:T(8,128)(2,1)S(1)}, bf16[128,1024]{1,0:T(8,128)(2,1)S(1)}, u32[]{:S(2)}, u32[]{:S(2)}) collective-permute-start(bf16[128,1024]{1,0:T(8,128)(2,1)S(1)} %get-tuple-element.20.refs_1_), channel_id=1, source_target_pairs={{0,1},{1,0},{2,3},{3,2},{4,5},{5,4},{6,7},{7,6},{8,9},{9,8},{10,11... | collective-permute-start | bytes 786440 | tf_op jit(solution)/shard_map/ppermute | solution.py:55
  11.5 1.8 %collective-permute-start.2 = (bf16[16,6400]{1,0:T(8,128)(2,1)S(1)}, bf16[16,6400]{1,0:T(8,128)(2,1)S(1)}, u32[]{:S(2)}, u32[]{:S(2)}) collective-permute-start(bf16[16,6400]{1,0:T(8,128)(2,1)S(1)} %shard_map.97), channel_id=1, source_target_pairs={{0,1},{1,0},{2,3},{3,2},{4,5},{5,4},{6,7},{7,6},{8,9},{9,8},{10,11... | collective-permute-start | bytes 614408 | tf_op jit(solution)/shard_map/ppermute | solution.py:55
  14.8 6.3 %collective-permute-start.7 = (bf16[64,512]{1,0:T(8,128)(2,1)S(1)}, bf16[64,512]{1,0:T(8,128)(2,1)S(1)}, u32[]{:S(2)}, u32[]{:S(2)}) collective-permute-start(bf16[64,512]{1,0:T(8,128)(2,1)S(1)} %get-tuple-element.24), channel_id=1, source_target_pairs={{0,8},{1,7},{2,10},{3,5},{4,12},{5,15},{6,14},{7,13},{8,0},{9,3},{... | collective-permute-start | bytes 196616 | tf_op jit(solution)/shard_map/ppermute | solution.py:55
  17.8 6.7 %collective-permute-start.8 = (bf16[64,512]{1,0:T(8,128)(2,1)S(1)}, bf16[64,512]{1,0:T(8,128)(2,1)S(1)}, u32[]{:S(2)}, u32[]{:S(2)}) collective-permute-start(bf16[64,512]{1,0:T(8,128)(2,1)S(1)} %get-tuple-element.25), channel_id=1, source_target_pairs={{0,12},{1,15},{2,14},{3,13},{4,8},{5,11},{6,10},{7,9},{8,4},{9,7},... | collective-permute-start | bytes 196616 | tf_op jit(solution)/shard_map/ppermute | solution.py:55
  18.3 6.2 %collective-permute-start.9 = (bf16[64,512]{1,0:T(8,128)(2,1)S(1)}, bf16[64,512]{1,0:T(8,128)(2,1)S(1)}, u32[]{:S(2)}, u32[]{:S(2)}) collective-permute-start(bf16[64,512]{1,0:T(8,128)(2,1)S(1)} %get-tuple-element.26), channel_id=1, source_target_pairs={{0,4},{1,11},{2,6},{3,9},{4,0},{5,3},{6,2},{7,1},{8,12},{9,15},{10... | collective-permute-start | bytes 196616 | tf_op jit(solution)/shard_map/ppermute | solution.py:55
  18.7 5.8 %collective-permute-start.10 = (bf16[64,512]{1,0:T(8,128)(2,1)S(1)}, bf16[64,512]{1,0:T(8,128)(2,1)S(1)}, u32[]{:S(2)}, u32[]{:S(2)}) collective-permute-start(bf16[64,512]{1,0:T(8,128)(2,1)S(1)} %get-tuple-element.27), channel_id=1, source_target_pairs={{0,2},{1,3},{2,0},{3,1},{4,6},{5,7},{6,4},{7,5},{8,10},{9,11},{10,... | collective-permute-start | bytes 196616 | tf_op jit(solution)/shard_map/ppermute | solution.py:55
  24.6 1.3 %collective-permute-start.11 = (bf16[64,256]{1,0:T(8,128)(2,1)S(1)}, bf16[64,256]{1,0:T(8,128)(2,1)S(1)}, u32[]{:S(2)}, u32[]{:S(2)}) collective-permute-start(bf16[64,256]{1,0:T(8,128)(2,1)S(1)} %get-tuple-element.30), channel_id=1, source_target_pairs={{0,1},{1,0},{2,3},{3,2},{4,5},{5,4},{6,7},{7,6},{8,9},{9,8},{10,11... | collective-permute-start | bytes 98312 | tf_op jit(solution)/shard_map/ppermute | solution.py:55

commit v7 on v6

--- a/solution.py
+++ b/solution.py
@@ -124,7 +124,7 @@
 
 
 def step_kernel(dec_bias, own, one, far, other, *refs):
-    *refs, enc_all, dec_all, error_all, dpre_all, inputs_all, enc_terms, dec_terms = refs
+    *refs, enc_all, dec_all, error_all, dpre_all, tokens_all, enc_terms, dec_terms = refs
     *refs, own_piece = refs
     refs, pieces = refs[: -len(CORE_1)], refs[-len(CORE_1) :]
     *refs, recon = refs
@@ -175,10 +175,12 @@
     cols = pl.ds(pl.multiple_of((chip ^ core) * half, half), half)
     input_parts = (*refs[:parts], *refs[2 * parts : 3 * parts])
     target_parts = (*refs[parts : 2 * parts], *refs[3 * parts :])
-    x = jnp.concatenate([part[...] for part in input_parts], axis=0)
+    n = input_parts[0].shape[0]
+    for i, part in enumerate(input_parts):
+        tokens_all[i * n : (i + 1) * n, :] = part[...]
     target = jnp.concatenate([part[:, :width] for part in target_parts], axis=0).astype(F32)
     gate = jnp.concatenate([part[:, width:] for part in target_parts], axis=1).astype(F32)
-    pre = contract(enc_all[...], x, 1, 1)
+    pre = contract(enc_all[...], tokens_all[...], 1, 1)
     pre = pre + jnp.concatenate([bias_col] * (pre.shape[1] // TILE), axis=1)
     act = (pre * gate).astype(BF16)
     recon_full = contract(act, dec_all[...], 0, 0) + base
@@ -186,11 +188,8 @@
     error = (recon_full - target).astype(BF16)
     error_all[...] = error
     dpre_all[...] = (contract(dec_all[...], error, 1, 1) * gate).astype(BF16)
-    n = input_parts[0].shape[0]
-    for i, part in enumerate(input_parts):
-        inputs_all[i * n : (i + 1) * n, :] = part[:, cols]
     dec_terms[...] = contract(act, error_all[:, cols], 1, 0)
-    enc_terms[...] = contract(dpre_all[...], inputs_all[...], 1, 0)
+    enc_terms[...] = contract(dpre_all[...], tokens_all[:, cols], 1, 0)
     for zero, one_table, piece in zip(CORE_0, CORE_1, pieces, strict=True):
         to = jnp.where(core == 0, look_up(zero, rank), look_up(one_table, rank))
         piece[:rows, :] = enc_terms[at(to), :].astype(BF16)
@@ -257,7 +256,7 @@
         scratch_shapes=[pltpu.VMEM(mask.shape, mask.dtype), pltpu.SemaphoreType.DMA((2 * parts + 2,))],
         cost_estimate=pl.CostEstimate(flops=0, bytes_accessed=4 * tokens * width, transcendentals=0),
     )(inputs, targets, mask, dec_bias, in_vmem(half))
-    others = [swap(array) for array in loaded]
+    others = [swap(array) for array in loaded[::-1]][::-1]
     joined = kernel_call(
         join_kernel, [pltpu.VMEM((STRIP, 3 * strips * width + 2 * TILE), BF16)], far, one
     )
@@ -274,7 +273,7 @@
             pltpu.VMEM((latents, width), BF16),
             pltpu.VMEM((2 * tokens, width), BF16),
             pltpu.VMEM((latents, 2 * tokens), BF16),
-            pltpu.VMEM((2 * tokens, 2 * share), BF16),
+            pltpu.VMEM((2 * tokens, width), BF16),
             pltpu.VMEM((latents, 2 * share), F32),
             pltpu.VMEM((latents, 2 * share), F32),
         ],

time: 26.7 us -> 26.7 us (level)
  no operation moved by 1% of the time
where the time goes in v7:
time: 26.7 us; the launch traced here: 26.5 us
  starting transfers between devices  12 us (45%)
  waiting for transfers between devices  8.56 us (32%)
  Pallas kernels  4.41 us (17%)
  local copies, waits for them, and re-layouts  0.79 us (3%)
  between operations  0.69 us (3%)
    ppermute x12, starting transfers between devices, move(): return lax.ppermute(array, PAIR, pairs)  12 us
    ppermute x12, waiting for transfers between devices, move(): return lax.ppermute(array, PAIR, pairs)  8.56 us
    pallas_call x5, Pallas kernels, kernel_call(): pl.pallas_call(kernel, out_shape=outs, in_specs=[VMEM] * len(operands), o...  2.21 us
    pallas_call x1, Pallas kernels, small_body(): pl.pallas_call(load_kernel, out_shape=[pltpu.VMEM((tokens // parts, width...  1.33 us
    pallas_call x1, Pallas kernels, small_body(): pl.pallas_call(pack_kernel, out_shape=pltpu.VMEM((STRIP, 2 * strips * wid...  0.87 us
    unnamed x1, local copies, waits for them, and re-layouts  0.79 us
  transfers between devices with their start and end apart: 12, of which 6 were waited for; matrix products, arithmetic and copies ran while one was open for 3% of the time, Pallas kernels for 5%

profile of v7, /device:TPU:0, one launch (start us, length us, event | category | flops | bytes accessed | tf_op | source)
XLA Modules:
  0.0 26.5 jit_solution(15461567464617179862)
XLA Ops:
  0.6 0.9 %shard_map.94.whole.own = bf16[16,4224]{1,0:T(8,128)(2,1)S(1)} custom-call(bf16[32,1024]{1,0:T(8,128)(2,1)} %enc.1, bf16[32,1024]{1,0:T(8,128)(2,1)} %dec.1, bf16[32]{0:T(256)(128)(2,1)} %bias.1), custom_call_target="tpu_custom_call" | custom-call | tf_op jit(solution)/shard_map/pallas_call | solution.py:238
  1.5 5.1 %collective-permute-start.1 = (bf16[16,4224]{1,0:T(8,128)(2,1)S(1)}, bf16[16,4224]{1,0:T(8,128)(2,1)S(1)}, u32[]{:S(2)}, u32[]{:S(2)}) collective-permute-start(bf16[16,4224]{1,0:T(8,128)(2,1)S(1)} %shard_map.94.whole.own), channel_id=1, source_target_pairs={{0,12},{1,9},{2,14},{3,11},{4,8},{5,13},{6,10},{7,15},{8,4},{9,1},... | collective-permute-start | bytes 405512 | tf_op jit(solution)/shard_map/ppermute | solution.py:55
  6.6 0.0 collective-permute-start
  6.6 1.3 %shard_map.96 = (bf16[128,1024]{1,0:T(8,128)(2,1)S(1)}, bf16[128,1024]{1,0:T(8,128)(2,1)S(1)}, bf16[128,1152]{1,0:T(8,128)(2,1)S(1)}, bf16[128,1152]{1,0:T(8,128)(2,1)S(1)}, f32[1024]{0:T(1024)S(1)}) custom-call(bf16[256,1024]{1,0:T(8,128)(2,1)} %inputs.1, bf16[256,1024]{1,0:T(8,128)(2,1)} %targets.1, s32[256,128]{1,0:T(8,128)} %mask.1, f32[1024]{0:T(1024)} %dec_bias.1, ...), custom_call_target="tpu_custom_call" | custom-call | bytes 1048576 | tf_op jit(solution)/shard_map/pallas_call | solution.py:249
  8.0 0.1 collective-permute-start.5
  8.1 0.5 %collective-permute-start.6 = (bf16[128,1152]{1,0:T(8,128)(2,1)S(1)}, bf16[128,1152]{1,0:T(8,128)(2,1)S(1)}, u32[]{:S(2)}, u32[]{:S(2)}) collective-permute-start(bf16[128,1152]{1,0:T(8,128)(2,1)S(1)} %get-tuple-element.22.refs_3_), channel_id=1, source_target_pairs={{0,1},{1,0},{2,3},{3,2},{4,5},{5,4},{6,7},{7,6},{8,9},{9,8},{10,11... | collective-permute-start | bytes 884744 | tf_op jit(solution)/shard_map/ppermute | solution.py:55
  8.6 0.1 collective-permute-start.3
  8.6 2.9 %collective-permute-done.one = bf16[16,2176]{1,0:T(8,128)(2,1)S(1)} collective-permute-done((bf16[16,2176]{1,0:T(8,128)(2,1)S(1)}, bf16[16,2176]{1,0:T(8,128)(2,1)S(1)}, u32[]{:S(2)}, u32[]{:S(2)}) %collective-permute-start) | collective-permute-done | bytes 69664 | tf_op jit(solution)/shard_map/ppermute | solution.py:55
  11.5 0.0 collective-permute-start.4
  11.5 0.0 collective-permute-done.1.far
  11.5 0.6 %collective-permute-start.2 = (bf16[16,6400]{1,0:T(8,128)(2,1)S(1)}, bf16[16,6400]{1,0:T(8,128)(2,1)S(1)}, u32[]{:S(2)}, u32[]{:S(2)}) collective-permute-start(bf16[16,6400]{1,0:T(8,128)(2,1)S(1)} %shard_map.97), channel_id=1, source_target_pairs={{0,1},{1,0},{2,3},{3,2},{4,5},{5,4},{6,7},{7,6},{8,9},{9,8},{10,11... | collective-permute-start | bytes 614408 | tf_op jit(solution)/shard_map/ppermute | solution.py:55
  12.1 0.0 collective-permute-done.3.refs_4_
  12.1 0.9 %collective-permute-done.4.refs_5_ = bf16[128,1024]{1,0:T(8,128)(2,1)S(1)} collective-permute-done((bf16[128,1024]{1,0:T(8,128)(2,1)S(1)}, bf16[128,1024]{1,0:T(8,128)(2,1)S(1)}, u32[]{:S(2)}, u32[]{:S(2)}) %collective-permute-start.4) | collective-permute-done | bytes 262176 | tf_op jit(solution)/shard_map/ppermute | solution.py:55
  13.0 0.0 collective-permute-done.5.refs_6_
  13.0 0.0 collective-permute-done.6.refs_7_
  13.1 0.3 %collective-permute-done.2.other = bf16[16,6400]{1,0:T(8,128)(2,1)S(1)} collective-permute-done((bf16[16,6400]{1,0:T(8,128)(2,1)S(1)}, bf16[16,6400]{1,0:T(8,128)(2,1)S(1)}, u32[]{:S(2)}, u32[]{:S(2)}) %collective-permute-start.2) | collective-permute-done | bytes 204832 | tf_op jit(solution)/shard_map/ppermute | solution.py:55
  13.3 1.5 %shard_map.98 = (bf16[256,1024]{1,0:T(8,128)(2,1)S(1)}, bf16[64,512]{1,0:T(8,128)(2,1)S(1)}, bf16[64,512]{1,0:T(8,128)(2,1)S(1)}, bf16[64,512]{1,0:T(8,128)(2,1)...) custom-call(f32[1024]{0:T(1024)S(1)} %get-tuple-element.18.dec_bias, bf16[16,4224]{1,0:T(8,128)(2,1)S(1)} %shard_map.94.whole.own, ...), custom_call_target="tpu_custom_call" | custom-call | flops 536870912 | tf_op jit(solution)/shard_map/pallas_call | solution.py:38
  14.9 3.0 %collective-permute-start.7 = (bf16[64,512]{1,0:T(8,128)(2,1)S(1)}, bf16[64,512]{1,0:T(8,128)(2,1)S(1)}, u32[]{:S(2)}, u32[]{:S(2)}) collective-permute-start(bf16[64,512]{1,0:T(8,128)(2,1)S(1)} %get-tuple-element.24), channel_id=1, source_target_pairs={{0,8},{1,7},{2,10},{3,5},{4,12},{5,15},{6,14},{7,13},{8,0},{9,3},{... | collective-permute-start | bytes 196616 | tf_op jit(solution)/shard_map/ppermute | solution.py:55
  17.8 0.5 %collective-permute-start.8 = (bf16[64,512]{1,0:T(8,128)(2,1)S(1)}, bf16[64,512]{1,0:T(8,128)(2,1)S(1)}, u32[]{:S(2)}, u32[]{:S(2)}) collective-permute-start(bf16[64,512]{1,0:T(8,128)(2,1)S(1)} %get-tuple-element.25), channel_id=1, source_target_pairs={{0,12},{1,15},{2,14},{3,13},{4,8},{5,11},{6,10},{7,9},{8,4},{9,7},... | collective-permute-start | bytes 196616 | tf_op jit(solution)/shard_map/ppermute | solution.py:55
  18.3 0.5 %collective-permute-start.9 = (bf16[64,512]{1,0:T(8,128)(2,1)S(1)}, bf16[64,512]{1,0:T(8,128)(2,1)S(1)}, u32[]{:S(2)}, u32[]{:S(2)}) collective-permute-start(bf16[64,512]{1,0:T(8,128)(2,1)S(1)} %get-tuple-element.26), channel_id=1, source_target_pairs={{0,4},{1,11},{2,6},{3,9},{4,0},{5,3},{6,2},{7,1},{8,12},{9,15},{10... | collective-permute-start | bytes 196616 | tf_op jit(solution)/shard_map/ppermute | solution.py:55
  18.7 1.5 %collective-permute-start.10 = (bf16[64,512]{1,0:T(8,128)(2,1)S(1)}, bf16[64,512]{1,0:T(8,128)(2,1)S(1)}, u32[]{:S(2)}, u32[]{:S(2)}) collective-permute-start(bf16[64,512]{1,0:T(8,128)(2,1)S(1)} %get-tuple-element.27), channel_id=1, source_target_pairs={{0,2},{1,3},{2,0},{3,1},{4,6},{5,7},{6,4},{7,5},{8,10},{9,11},{10,... | collective-permute-start | bytes 196616 | tf_op jit(solution)/shard_map/ppermute | solution.py:55
  20.2 1.0 %collective-permute-done.7.refs_0_ = bf16[64,512]{1,0:T(8,128)(2,1)S(1)} collective-permute-done((bf16[64,512]{1,0:T(8,128)(2,1)S(1)}, bf16[64,512]{1,0:T(8,128)(2,1)S(1)}, u32[]{:S(2)}, u32[]{:S(2)}) %collective-permute-start.7) | collective-permute-done | bytes 65568 | tf_op jit(solution)/shard_map/ppermute | solution.py:55
  21.2 3.3 %collective-permute-done.8.refs_1_ = bf16[64,512]{1,0:T(8,128)(2,1)S(1)} collective-permute-done((bf16[64,512]{1,0:T(8,128)(2,1)S(1)}, bf16[64,512]{1,0:T(8,128)(2,1)S(1)}, u32[]{:S(2)}, u32[]{:S(2)}) %collective-permute-start.8) | collective-permute-done | bytes 65568 | tf_op jit(solution)/shard_map/ppermute | solution.py:55
  24.5 0.0 collective-permute-done.9.refs_2_
  24.5 0.0 collective-permute-done.10.refs_3_
  24.6 0.3 %collective-permute-start.11 = (bf16[64,256]{1,0:T(8,128)(2,1)S(1)}, bf16[64,256]{1,0:T(8,128)(2,1)S(1)}, u32[]{:S(2)}, u32[]{:S(2)}) collective-permute-start(bf16[64,256]{1,0:T(8,128)(2,1)S(1)} %get-tuple-element.30), channel_id=1, source_target_pairs={{0,1},{1,0},{2,3},{3,2},{4,5},{5,4},{6,7},{7,6},{8,9},{9,8},{10,11... | collective-permute-start | bytes 98312 | tf_op jit(solution)/shard_map/ppermute | solution.py:55
  24.9 0.8 %copy.10 = bf16[256,1024]{1,0:T(8,128)(2,1)} copy(bf16[256,1024]{1,0:T(8,128)(2,1)S(1)} %get-tuple-element.33) | data formatting | bytes 1048576
  25.7 0.2 collective-permute-done.11.refs_1_
  25.9 0.6 %shard_map.100 = (f32[32,256]{1,0:T(8,128)}, f32[32,256]{1,0:T(8,128)}) custom-call(f32[64,256]{1,0:T(8,128)S(1)} %get-tuple-element.29.refs_0_, bf16[64,256]{1,0:T(8,128)(2,1)S(1)} %collective-permute-done.11.refs_1_), custom_call_target="tpu_custom_call" | custom-call | tf_op jit(solution)/shard_map/pallas_call | solution.py:38
  (3 shorter events, 0.1 us)
Async XLA Ops:
  1.5 10.0 %collective-permute-start.1 = (bf16[16,4224]{1,0:T(8,128)(2,1)S(1)}, bf16[16,4224]{1,0:T(8,128)(2,1)S(1)}, u32[]{:S(2)}, u32[]{:S(2)}) collective-permute-start(bf16[16,4224]{1,0:T(8,128)(2,1)S(1)} %shard_map.94.whole.own), channel_id=1, source_target_pairs={{0,12},{1,9},{2,14},{3,11},{4,8},{5,13},{6,10},{7,15},{8,4},{9,1},... | collective-permute-start | bytes 405512 | tf_op jit(solution)/shard_map/ppermute | solution.py:55
  6.6 4.9 %collective-permute-start = (bf16[16,2176]{1,0:T(8,128)(2,1)S(1)}, bf16[16,2176]{1,0:T(8,128)(2,1)S(1)}, u32[]{:S(2)}, u32[]{:S(2)}) collective-permute-start(bf16[16,2176]{1,0:T(8,128)(2,1)S(1)} %shard_map.95.after), channel_id=1, source_target_pairs={{0,4},{1,5},{2,6},{3,7},{4,0},{5,1},{6,2},{7,3},{8,12},{9,13},{10,... | collective-permute-start | bytes 208904 | tf_op jit(solution)/shard_map/ppermute | solution.py:55
  8.0 5.1 %collective-permute-start.5 = (bf16[128,1152]{1,0:T(8,128)(2,1)S(1)}, bf16[128,1152]{1,0:T(8,128)(2,1)S(1)}, u32[]{:S(2)}, u32[]{:S(2)}) collective-permute-start(bf16[128,1152]{1,0:T(8,128)(2,1)S(1)} %get-tuple-element.21.refs_2_), channel_id=1, source_target_pairs={{0,1},{1,0},{2,3},{3,2},{4,5},{5,4},{6,7},{7,6},{8,9},{9,8},{10,11... | collective-permute-start | bytes 884744 | tf_op jit(solution)/shard_map/ppermute | solution.py:55
  8.1 5.0 %collective-permute-start.6 = (bf16[128,1152]{1,0:T(8,128)(2,1)S(1)}, bf16[128,1152]{1,0:T(8,128)(2,1)S(1)}, u32[]{:S(2)}, u32[]{:S(2)}) collective-permute-start(bf16[128,1152]{1,0:T(8,128)(2,1)S(1)} %get-tuple-element.22.refs_3_), channel_id=1, source_target_pairs={{0,1},{1,0},{2,3},{3,2},{4,5},{5,4},{6,7},{7,6},{8,9},{9,8},{10,11... | collective-permute-start | bytes 884744 | tf_op jit(solution)/shard_map/ppermute | solution.py:55
  8.6 3.6 %collective-permute-start.3 = (bf16[128,1024]{1,0:T(8,128)(2,1)S(1)}, bf16[128,1024]{1,0:T(8,128)(2,1)S(1)}, u32[]{:S(2)}, u32[]{:S(2)}) collective-permute-start(bf16[128,1024]{1,0:T(8,128)(2,1)S(1)} %get-tuple-element.19.refs_0_), channel_id=1, source_target_pairs={{0,1},{1,0},{2,3},{3,2},{4,5},{5,4},{6,7},{7,6},{8,9},{9,8},{10,11... | collective-permute-start | bytes 786440 | tf_op jit(solution)/shard_map/ppermute | solution.py:55
  11.5 1.5 %collective-permute-start.4 = (bf16[128,1024]{1,0:T(8,128)(2,1)S(1)}, bf16[128,1024]{1,0:T(8,128)(2,1)S(1)}, u32[]{:S(2)}, u32[]{:S(2)}) collective-permute-start(bf16[128,1024]{1,0:T(8,128)(2,1)S(1)} %get-tuple-element.20.refs_1_), channel_id=1, source_target_pairs={{0,1},{1,0},{2,3},{3,2},{4,5},{5,4},{6,7},{7,6},{8,9},{9,8},{10,11... | collective-permute-start | bytes 786440 | tf_op jit(solution)/shard_map/ppermute | solution.py:55
  11.5 1.8 %collective-permute-start.2 = (bf16[16,6400]{1,0:T(8,128)(2,1)S(1)}, bf16[16,6400]{1,0:T(8,128)(2,1)S(1)}, u32[]{:S(2)}, u32[]{:S(2)}) collective-permute-start(bf16[16,6400]{1,0:T(8,128)(2,1)S(1)} %shard_map.97), channel_id=1, source_target_pairs={{0,1},{1,0},{2,3},{3,2},{4,5},{5,4},{6,7},{7,6},{8,9},{9,8},{10,11... | collective-permute-start | bytes 614408 | tf_op jit(solution)/shard_map/ppermute | solution.py:55
  14.9 6.3 %collective-permute-start.7 = (bf16[64,512]{1,0:T(8,128)(2,1)S(1)}, bf16[64,512]{1,0:T(8,128)(2,1)S(1)}, u32[]{:S(2)}, u32[]{:S(2)}) collective-permute-start(bf16[64,512]{1,0:T(8,128)(2,1)S(1)} %get-tuple-element.24), channel_id=1, source_target_pairs={{0,8},{1,7},{2,10},{3,5},{4,12},{5,15},{6,14},{7,13},{8,0},{9,3},{... | collective-permute-start | bytes 196616 | tf_op jit(solution)/shard_map/ppermute | solution.py:55
  17.8 6.7 %collective-permute-start.8 = (bf16[64,512]{1,0:T(8,128)(2,1)S(1)}, bf16[64,512]{1,0:T(8,128)(2,1)S(1)}, u32[]{:S(2)}, u32[]{:S(2)}) collective-permute-start(bf16[64,512]{1,0:T(8,128)(2,1)S(1)} %get-tuple-element.25), channel_id=1, source_target_pairs={{0,12},{1,15},{2,14},{3,13},{4,8},{5,11},{6,10},{7,9},{8,4},{9,7},... | collective-permute-start | bytes 196616 | tf_op jit(solution)/shard_map/ppermute | solution.py:55
  18.3 6.2 %collective-permute-start.9 = (bf16[64,512]{1,0:T(8,128)(2,1)S(1)}, bf16[64,512]{1,0:T(8,128)(2,1)S(1)}, u32[]{:S(2)}, u32[]{:S(2)}) collective-permute-start(bf16[64,512]{1,0:T(8,128)(2,1)S(1)} %get-tuple-element.26), channel_id=1, source_target_pairs={{0,4},{1,11},{2,6},{3,9},{4,0},{5,3},{6,2},{7,1},{8,12},{9,15},{10... | collective-permute-start | bytes 196616 | tf_op jit(solution)/shard_map/ppermute | solution.py:55
  18.7 5.8 %collective-permute-start.10 = (bf16[64,512]{1,0:T(8,128)(2,1)S(1)}, bf16[64,512]{1,0:T(8,128)(2,1)S(1)}, u32[]{:S(2)}, u32[]{:S(2)}) collective-permute-start(bf16[64,512]{1,0:T(8,128)(2,1)S(1)} %get-tuple-element.27), channel_id=1, source_target_pairs={{0,2},{1,3},{2,0},{3,1},{4,6},{5,7},{6,4},{7,5},{8,10},{9,11},{10,... | collective-permute-start | bytes 196616 | tf_op jit(solution)/shard_map/ppermute | solution.py:55
  24.6 1.3 %collective-permute-start.11 = (bf16[64,256]{1,0:T(8,128)(2,1)S(1)}, bf16[64,256]{1,0:T(8,128)(2,1)S(1)}, u32[]{:S(2)}, u32[]{:S(2)}) collective-permute-start(bf16[64,256]{1,0:T(8,128)(2,1)S(1)} %get-tuple-element.30), channel_id=1, source_target_pairs={{0,1},{1,0},{2,3},{3,2},{4,5},{5,4},{6,7},{7,6},{8,9},{9,8},{10,11... | collective-permute-start | bytes 98312 | tf_op jit(solution)/shard_map/ppermute | solution.py:55
